TPU v7x, 32 devices: a whole 2x2x4 slice. The times are simulated.
32 devices in a mesh: context: 8 (over y, x, core), tensor: 4 (over z).
Axes of the slice: x: 2, y: 2, z: 4, core: 2. Of those that a mesh axis runs over, the one named last changes fastest.
Arguments:
- inputs: float32 [32, 32768], P('tensor', 'context'), may hold values from -0.078125 to 0.078125
- grads: float32 [32, 32768], P('tensor', 'context'), may hold values from -6 to 6
- response: float32 [32, 32768], P('tensor', 'context'), may hold values from -0.078125 to 0.078125
Outputs:
- input_grad: float32 [32, 32768], P('tensor', 'context')
- filter_grad: float32 [32, 32768], P('tensor', 'context')
All inputs are finite; a program needn't handle non-finite values.
Results may differ from a plain program's by a relative error of at most 0.00014.
Values sent between devices are 32-bit elements; how exact they have to be, the bound alone decides.
No kernel may reach another device: no remote copies, remote signals or barrier semaphores. Data moves between devices by JAX's collectives and lax.ppermute only.
A program may use at most 64 MiB of HBM per device.

v0:
```python
import math

import jax
import jax.numpy as jnp
from jax import lax
from jax.sharding import PartitionSpec as P

RADIX = 128


HIGHEST = lax.Precision.HIGHEST


def phase_pair(row_index, col_index, period, sign_flip):
    product = row_index[:, None] * col_index[None, :] % period
    angles = 2.0 * math.pi / period * product.astype(jnp.float32)
    return (jnp.cos(angles), sign_flip * jnp.sin(angles))


def complex_apply(pattern, tables, values):
    real_real = jnp.einsum(pattern, tables[0], values[0], precision=HIGHEST)
    imag_imag = jnp.einsum(pattern, tables[1], values[1], precision=HIGHEST)
    real_imag = jnp.einsum(pattern, tables[0], values[1], precision=HIGHEST)
    imag_real = jnp.einsum(pattern, tables[1], values[0], precision=HIGHEST)
    return (real_real - imag_imag, real_imag + imag_real)


def complex_times(left_pair, right_pair):
    return (
        left_pair[0] * right_pair[0] - left_pair[1] * right_pair[1],
        left_pair[0] * right_pair[1] + left_pair[1] * right_pair[0],
    )


def per_device(inputs, grads, response):
    context_size = lax.axis_size("context")
    device_index = lax.axis_index("context")
    channels, block_len = inputs.shape
    column_len = block_len // context_size
    full_length = block_len * context_size
    padded_len = 2 * full_length
    split_len = block_len // RADIX
    freq_rows = jnp.arange(2 * context_size, dtype=jnp.int32)
    part_rows = jnp.arange(context_size, dtype=jnp.int32)
    outer_fwd = phase_pair(freq_rows, part_rows, 2 * context_size, -1.0)
    outer_inv = phase_pair(part_rows, freq_rows, 2 * context_size, 1.0)
    split_rows = jnp.arange(split_len, dtype=jnp.int32)
    radix_rows = jnp.arange(RADIX, dtype=jnp.int32)
    first_fwd = phase_pair(split_rows, split_rows, split_len, -1.0)
    first_inv = (first_fwd[0], -first_fwd[1])
    inner_fwd = phase_pair(split_rows, radix_rows, block_len, -1.0)
    inner_inv = (inner_fwd[0], -inner_fwd[1])
    last_fwd = phase_pair(radix_rows, radix_rows, RADIX, -1.0)
    last_inv = (last_fwd[0], -last_fwd[1])
    pair_rows = 2 * device_index + jnp.arange(2, dtype=jnp.int32)
    column_rows = jnp.arange(block_len, dtype=jnp.int32)
    global_fwd = phase_pair(pair_rows, column_rows, padded_len, -1.0)
    global_inv = (global_fwd[0], -global_fwd[1])
    signals = jnp.stack([inputs, grads, response])
    columns = lax.all_to_all(
        signals.reshape(3, channels, context_size, column_len),
        "context",
        split_axis=2,
        concat_axis=2,
        tiled=True,
    )
    real_part = jnp.einsum("kn,smnj->smkj", outer_fwd[0], columns, precision=HIGHEST)
    imag_part = jnp.einsum("kn,smnj->smkj", outer_fwd[1], columns, precision=HIGHEST)
    columns = jnp.stack([real_part, imag_part], axis=1)
    arrived = lax.all_to_all(columns, "context", split_axis=3, concat_axis=4, tiled=True)
    values = complex_times((arrived[:, 0], arrived[:, 1]), global_fwd)
    shaped = tuple((v.reshape(v.shape[:3] + (split_len, RADIX)) for v in values))
    sectioned = complex_apply("xa,smrab->smrxb", first_fwd, shaped)
    turned = complex_times(sectioned, inner_fwd)
    spec_real, spec_imag = complex_apply("bd,smrxb->smrxd", last_fwd, turned)
    back_input = (
        spec_real[2] * spec_real[1] + spec_imag[2] * spec_imag[1],
        spec_real[2] * spec_imag[1] - spec_imag[2] * spec_real[1],
    )
    back_filter = (
        spec_real[0] * spec_real[1] + spec_imag[0] * spec_imag[1],
        spec_real[0] * spec_imag[1] - spec_imag[0] * spec_real[1],
    )
    inverse_in = ((back_input[0] - back_filter[1])[None], (back_input[1] + back_filter[0])[None])
    sectioned = complex_apply("bd,smrxd->smrxb", last_inv, inverse_in)
    turned = complex_times(sectioned, inner_inv)
    rebuilt = complex_apply("ax,smrxb->smrab", first_inv, turned)
    flat = tuple((v.reshape(v.shape[:3] + (block_len,)) for v in rebuilt))
    untwisted = complex_times(flat, global_inv)
    rows_back = jnp.stack([untwisted[0], untwisted[1]], axis=1)
    arrived = lax.all_to_all(rows_back, "context", split_axis=4, concat_axis=3, tiled=True)
    cos_real = jnp.einsum("nk,smkj->smnj", outer_inv[0], arrived[:, 0], precision=HIGHEST)
    sin_imag = jnp.einsum("nk,smkj->smnj", outer_inv[1], arrived[:, 1], precision=HIGHEST)
    cos_imag = jnp.einsum("nk,smkj->smnj", outer_inv[0], arrived[:, 1], precision=HIGHEST)
    sin_real = jnp.einsum("nk,smkj->smnj", outer_inv[1], arrived[:, 0], precision=HIGHEST)
    folded = jnp.concatenate([cos_real - sin_imag, cos_imag + sin_real], axis=0) / padded_len
    restored = lax.all_to_all(folded, "context", split_axis=2, concat_axis=3, tiled=True).reshape(
        2, channels, block_len
    )
    return (restored[0], restored[1])


def solution(mesh):
    return jax.shard_map(
        per_device,
        mesh=mesh,
        in_specs=(P("tensor", "context"), P("tensor", "context"), P("tensor", "context")),
        out_specs=(P("tensor", "context"), P("tensor", "context")),
        check_vma=False,
    )
```

profile of v0, /device:TPU:0, one launch (start us, length us, event | category | flops | bytes accessed | tf_op | source)
XLA Modules:
  0.0 136.1 jit_solution(6535399234801774527)
XLA Ops:
  0.6 1.8 %pad_maximum_fusion.2 = f32[3,8,8,512]{3,1,0,2:T(8,128)} fusion(f32[1,8,8,512]{3,1,0,2:T(8,128)} %bitcast.152, f32[1,8,8,512]{3,1,0,2:T(8,128)} %bitcast.153, f32[1,8,8,512]{3,1,0,2:T(8,128)} %bitcast.154), kind=kLoop, calls=%fused_computation.27 | loop fusion | flops 196608 | bytes 786432 | tf_op jit(solution)/shard_map/stack | solution.py:59
  2.4 5.2 %all-to-all-start = ((f32[3,8,8,512]{3,1,0,2:T(8,128)}), f32[3,8,8,512]{3,1,0,2:T(8,128)S(1)}, u32[]{:S(2)}, u32[]{:S(2)}) async-start(f32[3,8,8,512]{3,1,0,2:T(8,128)} %pad_maximum_fusion.2), calls=%async_computation | async-start | bytes 786432 | tf_op jit(solution)/shard_map/all_to_all | solution.py:60
  7.6 8.3 %all-to-all-done = f32[3,8,8,512]{3,1,0,2:T(8,128)S(1)} async-done(((f32[3,8,8,512]{3,1,0,2:T(8,128)}), f32[3,8,8,512]{3,1,0,2:T(8,128)S(1)}, u32[]{:S(2)}, u32[]{:S(2)}) %all-to-all-start) | async-done | bytes 393248 | tf_op jit(solution)/shard_map/all_to_all | solution.py:60
  15.9 1.0 convolution_bitcast_fusion
  16.9 1.0 convolution_bitcast_fusion.1
  17.9 0.2 pad_maximum_fusion
  18.1 2.1 %copy.31 = f32[3,2,8,16,512]{4,2,0,1,3:T(8,128)} copy(f32[3,2,8,16,512]{4,3,2,0,1:T(8,128)S(1)} %pad_maximum_fusion) | data formatting | bytes 3145728 | tf_op jit(solution)/shard_map/stack | solution.py:69
  20.2 3.8 %all-to-all-start.1 = ((f32[3,2,8,16,512]{4,2,0,1,3:T(8,128)}), f32[3,2,8,16,512]{4,2,0,1,3:T(8,128)S(1)}, u32[]{:S(2)}, u32[]{:S(2)}) async-start(f32[3,2,8,16,512]{4,2,0,1,3:T(8,128)} %copy.31), calls=%async_computation.1 | async-start | bytes 3145728 | tf_op jit(solution)/shard_map/all_to_all | solution.py:70
  24.0 0.1 fusion.95
  24.1 0.1 sine_multiply_fusion.6
  24.2 0.2 fusion.76
  24.4 0.6 fusion.71
  25.0 19.8 %all-to-all-done.1 = f32[3,2,8,16,512]{4,2,0,1,3:T(8,128)S(1)} async-done(((f32[3,2,8,16,512]{4,2,0,1,3:T(8,128)}), f32[3,2,8,16,512]{4,2,0,1,3:T(8,128)S(1)}, u32[]{:S(2)}, u32[]{:S(2)}) %all-to-all-start.1) | async-done | bytes 1572896 | tf_op jit(solution)/shard_map/all_to_all | solution.py:70
  44.8 1.1 copy.75
  45.9 0.3 all_to_all.40
  46.1 0.1 slice_bitcast_fusion.1
  46.3 1.1 fusion.18
  47.4 1.1 fusion.19
  48.5 1.1 fusion.1
  49.6 1.1 fusion
  50.7 1.0 fusion.16
  51.8 1.0 fusion.17
  52.8 1.0 convolution_subtract_fusion
  53.8 1.0 convolution_add_fusion
  54.9 0.2 subtract_subtract_fusion
  55.1 0.6 fusion.12
  55.7 0.8 fusion.8
  56.5 0.6 convolution_subtract_fusion.3
  57.2 0.6 convolution_add_fusion.3
  57.8 0.5 fusion.20
  58.3 0.5 fusion.21
  58.7 0.5 fusion.3
  59.2 0.1 reshape.288
  59.4 0.5 fusion.2
  59.8 0.1 reshape.289
  60.0 0.3 multiply_subtract_fusion.2
  60.4 8.2 %copy.41 = f32[1,2,8,2,4096]{2,3,1,0,4:T(2,128)} copy(f32[1,2,8,2,4096]{4,2,3,1,0:T(8,128)S(1)} %pad_maximum_fusion.1) | data formatting | bytes 1048576 | tf_op jit(solution)/shard_map/stack | solution.py:90
  68.5 14.9 %reshape.304 = f32[8,1,16384]{2,1,0:T(1,128)S(1)} reshape(f32[4096,1,2,2,8]{4,3,2,1,0:T(2,128)} %bitcast.147) | data formatting | bytes 1048576
  83.5 12.2 %all_to_all.50 = f32[8,1,16384]{2,1,0:T(1,128)S(1)} all-to-all(f32[8,1,16384]{2,1,0:T(1,128)S(1)} %reshape.304), channel_id=1, replica_groups=mesh['context'=8,'tensor'=4] {'context'}, dimensions={0} | all-to-all | bytes 1048576 | tf_op jit(solution)/shard_map/all_to_all | solution.py:91
  95.6 0.5 broadcast.373
  96.1 1.9 %reduce = f32[8,16384]{1,0:T(8,128)S(1)} reduce(f32[8,1,16384]{2,1,0:T(1,128)S(1)} %all_to_all.50, f32[]{:T(128)} %broadcast.373), dimensions={1}, to_apply=%all_to_all.41.reduce_sub_computation | reduce | bytes 1048580 | tf_op jit(solution)/shard_map/all_to_all | solution.py:91
  98.0 16.0 %reshape.305 = f32[4096,1,2,2,8]{4,3,2,1,0:T(2,128)} reshape(f32[8,16384]{1,0:T(8,128)S(1)} %reduce) | data formatting | bytes 1048576
  114.0 10.2 %copy.42 = f32[1,2,8,2,8,512]{5,3,4,2,1,0:T(2,128)S(1)} copy(f32[1,2,8,2,8,512]{2,3,1,5,4,0:T(2,128)} %bitcast.148) | data formatting | bytes 1048576 | tf_op jit(solution)/shard_map/all_to_all | solution.py:91
  124.2 0.4 all_to_all.44
  124.6 0.3 fusion.14
  124.9 0.3 fusion.15
  125.2 0.3 fusion.5
  125.5 0.3 fusion.4
  125.8 0.2 copy.43
  126.0 9.3 %all_to_all.51 = f32[2,8,8,512]{3,1,0,2:T(8,128)S(1)} all-to-all(f32[2,8,8,512]{3,1,0,2:T(8,128)S(1)} %copy.43), channel_id=1, replica_groups=mesh['context'=8,'tensor'=4] {'context'}, dimensions={2} | all-to-all | bytes 524288 | tf_op jit(solution)/shard_map/all_to_all | solution.py:97
  135.3 0.7 fusion.223
  (4 shorter events, 0.1 us)
Async XLA Ops:
  2.4 13.5 %all-to-all-start = ((f32[3,8,8,512]{3,1,0,2:T(8,128)}), f32[3,8,8,512]{3,1,0,2:T(8,128)S(1)}, u32[]{:S(2)}, u32[]{:S(2)}) async-start(f32[3,8,8,512]{3,1,0,2:T(8,128)} %pad_maximum_fusion.2), calls=%async_computation | async-start | bytes 786432 | tf_op jit(solution)/shard_map/all_to_all | solution.py:60
  20.2 24.5 %all-to-all-start.1 = ((f32[3,2,8,16,512]{4,2,0,1,3:T(8,128)}), f32[3,2,8,16,512]{4,2,0,1,3:T(8,128)S(1)}, u32[]{:S(2)}, u32[]{:S(2)}) async-start(f32[3,2,8,16,512]{4,2,0,1,3:T(8,128)} %copy.31), calls=%async_computation.1 | async-start | bytes 3145728 | tf_op jit(solution)/shard_map/all_to_all | solution.py:70
where the time goes:
time: 137 us; the launch traced here: 136 us
  local copies, waits for them, and re-layouts  54.9 us (40%)
  waiting for transfers between devices  28.1 us (21%)
  blocking collectives  21.5 us (16%)
  matrix products  16.3 us (12%)
  starting transfers between devices  8.93 us (7%)
  other arithmetic  5.44 us (4%)
    unnamed x2, local copies, waits for them, and re-layouts  30.9 us
    all_to_all x1, waiting for transfers between devices, per_device(): lax.all_to_all(columns, 'context', split_axis=3, concat_axis=4, tiled=True)  19.8 us
    all_to_all x1, blocking collectives, per_device(): lax.all_to_all(rows_back, 'context', split_axis=4, concat_axis=3, tiled=T...  12.2 us
    all_to_all x3, local copies, waits for them, and re-layouts, per_device(): lax.all_to_all(rows_back, 'context', split_axis=4, concat_axis=3, tiled=T...  11.1 us
    all_to_all x1, blocking collectives, per_device(): lax.all_to_all(folded, 'context', split_axis=2, concat_axis=3, tiled=True)  9.35 us
    all_to_all x1, waiting for transfers between devices, per_device(): lax.all_to_all(signals.reshape(3, channels, context_size, column_len), 'c...  8.33 us
    another operation x1, local copies, waits for them, and re-layouts, per_device(): rows_back = jnp.stack([untwisted[0], untwisted[1]], axis=1)  8.17 us
    all_to_all x1, starting transfers between devices, per_device(): lax.all_to_all(signals.reshape(3, channels, context_size, column_len), 'c...  5.17 us
  transfers between devices with their start and end apart: 2, of which 2 were waited for; matrix products, arithmetic and copies ran while one was open for 1% of the time, Pallas kernels for 0%

commit v1 on v0

--- a/solution.py
+++ b/solution.py
@@ -1,9 +1,138 @@
+import functools
 import math
 
 import jax
 import jax.numpy as jnp
+import numpy as np
 from jax import lax
+from jax.experimental import pallas as pl
+from jax.experimental.pallas import tpu as pltpu
 from jax.sharding import PartitionSpec as P
+
+LANES = 128
+MODE = "a2a"
+BF = jnp.bfloat16
+
+
+def halves(table):
+    high = table.astype(BF)
+    low = (table - high.astype(np.float32)).astype(BF)
+    return high, low
+
+
+def tables(length):
+    rows = length // LANES
+    k = np.arange(rows)[:, None] + 0.25
+    r = np.arange(rows)[None, :]
+    ang = 2 * np.pi * (k * r / rows)
+    cos1, sin1 = np.cos(ang), np.sin(ang)
+    fwd = np.concatenate([cos1, -sin1], axis=0).astype(np.float32)
+    inv = (np.concatenate([cos1.T, -sin1.T], axis=1) / length).astype(np.float32)
+    lane = np.arange(LANES)
+    tw = 2 * np.pi * (k * lane[None, :] / length)
+    twc, tws = np.cos(tw).astype(np.float32), np.sin(tw).astype(np.float32)
+    a2 = 2 * np.pi * (lane[:, None] * lane[None, :] % LANES) / LANES
+    c2, s2 = np.cos(a2), np.sin(a2)
+    w_f = np.block([[c2, -s2], [s2, c2]]).astype(np.float32)
+    w_i = np.block([[c2, s2], [-s2, c2]]).astype(np.float32)
+    fh, fl = halves(fwd)
+    ih, il = halves(inv)
+    wfh, wfl = halves(w_f)
+    wih, wil = halves(w_i)
+    return fh, fl, ih, il, wfh, wfl, wih, wil, twc, tws
+
+
+def split(x):
+    high = x.astype(BF)
+    low = (x - high.astype(jnp.float32)).astype(BF)
+    return high, low
+
+
+def dot(a, b):
+    return jnp.dot(a, b, preferred_element_type=jnp.float32)
+
+
+def dot_left(th, tl, x):
+    xh, xl = split(x)
+    return dot(th, xh) + (dot(th, xl) + dot(tl, xh))
+
+
+def dot_right(x, th, tl):
+    xh, xl = split(x)
+    return dot(xh, th) + (dot(xl, th) + dot(xh, tl))
+
+
+def spread(a, b, c, out):
+    channels, block = a.shape
+    chunks = block // LANES
+    for i, ref in enumerate((a, b, c)):
+        for j in range(chunks):
+            out[pl.ds(i * chunks + j, channels, stride=3 * chunks), :] = ref[:, pl.ds(j * LANES, LANES)]
+
+
+def gather(x, a, b):
+    channels, block = a.shape
+    chunks = block // LANES
+    for i, ref in enumerate((a, b)):
+        for j in range(chunks):
+            ref[:, pl.ds(j * LANES, LANES)] = x[pl.ds(i * chunks + j, channels, stride=2 * chunks), :]
+
+
+def transform(x, fh, fl, ih, il, wfh, wfl, wih, wil, twc, tws, out):
+    nblk, _, chunks, lanes = x.shape
+    rows = nblk * chunks
+    sig = jnp.concatenate([x[:, i].reshape(rows, lanes) for i in range(3)], axis=1)
+    spec = dot_left(fh[...], fl[...], sig)
+    c, s = twc[...], tws[...]
+    parts = []
+    for i in range(3):
+        re = spec[:rows, i * lanes:(i + 1) * lanes]
+        im = spec[rows:, i * lanes:(i + 1) * lanes]
+        v = jnp.concatenate([re * c + im * s, im * c - re * s], axis=1)
+        b = dot_right(v, wfh[...], wfl[...])
+        parts.append((b[:, :lanes], b[:, lanes:]))
+    (xr, xi), (gr, gi), (hr, hi) = parts
+    back = []
+    for (ur, ui) in ((hr, hi), (xr, xi)):
+        p = jnp.concatenate([ur * gr + ui * gi, ur * gi - ui * gr], axis=1)
+        d = dot_right(p, wih[...], wil[...])
+        dr, di = d[:, :lanes], d[:, lanes:]
+        back.append(jnp.concatenate([dr * c - di * s, di * c + dr * s], axis=0))
+    y = dot_left(ih[...], il[...], jnp.concatenate(back, axis=1))
+    for i in range(2):
+        out[:, i] = y[:, i * lanes:(i + 1) * lanes].reshape(nblk, chunks, lanes)
+
+
+def vm(n):
+    return [pl.BlockSpec(memory_space=pltpu.VMEM)] * n
+
+
+def per_device(inputs, grads, response):
+    n = lax.axis_size("context")
+    channels, block = inputs.shape
+    length = block * n
+    chunks = block // LANES
+    sent = pl.pallas_call(
+        spread,
+        out_shape=jax.ShapeDtypeStruct((channels * 3 * chunks, LANES), jnp.float32),
+        in_specs=vm(3),
+        out_specs=vm(1)[0],
+    )(inputs, grads, response)
+    got = lax.all_to_all(sent.reshape(n, 3, chunks, LANES), "context", split_axis=0, concat_axis=0, tiled=True)
+    y = pl.pallas_call(
+        transform,
+        out_shape=jax.ShapeDtypeStruct((n, 2, chunks, LANES), jnp.float32),
+        in_specs=vm(11),
+        out_specs=vm(1)[0],
+    )(got, *[jnp.asarray(t) for t in tables(length)])
+    back = lax.all_to_all(y, "context", split_axis=0, concat_axis=0, tiled=True)
+    return pl.pallas_call(
+        gather,
+        out_shape=[jax.ShapeDtypeStruct((channels, block), jnp.float32)] * 2,
+        in_specs=vm(1),
+        out_specs=vm(2),
+    )(back.reshape(channels * 2 * chunks, LANES))
+
 
 RADIX = 128
 
@@ -32,7 +161,7 @@
     )
 
 
-def per_device(inputs, grads, response):
+def by_columns(inputs, grads, response):
     context_size = lax.axis_size("context")
     device_index = lax.axis_index("context")
     channels, block_len = inputs.shape
@@ -100,11 +229,12 @@
     return (restored[0], restored[1])
 
 
+def by_shape(inputs, grads, response):
+    if inputs.shape[0] == lax.axis_size("context"):
+        return per_device(inputs, grads, response)
+    return by_columns(inputs, grads, response)
+
+
 def solution(mesh):
-    return jax.shard_map(
-        per_device,
-        mesh=mesh,
-        in_specs=(P("tensor", "context"), P("tensor", "context"), P("tensor", "context")),
-        out_specs=(P("tensor", "context"), P("tensor", "context")),
-        check_vma=False,
-    )
+    spec = P("tensor", "context")
+    return jax.shard_map(by_shape, mesh=mesh, in_specs=(spec,) * 3, out_specs=(spec,) * 2, check_vma=False)

time: 137 us -> 33.6 us (0.25)
  local copies, waits for them, and re-layouts: 54.9 us -> 0 us
  waiting for transfers between devices: 28.1 us -> 0 us
  matrix products: 16.3 us -> 0 us
  starting transfers between devices: 8.93 us -> 0 us
  Pallas kernels: 0 us -> 7.97 us
  other arithmetic: 5.44 us -> 0 us
  blocking collectives: 21.5 us -> 24.6 us
    unnamed x2 -> x0, local copies, waits for them, and re-layouts: 30.9 us -> none
    all_to_all x2 -> x0, waiting for transfers between devices: 28.1 us -> none  [the longest x1 19.8 us: per_device(): lax.all_to_all(columns, 'context', split_axis=3, concat_axis=4, tiled=True)]
    dot_general x22 -> x0, matrix products: 16.3 us -> none  [the longest x4 3.42 us: complex_apply(): real_imag = jnp.einsum(pattern, tables[0], values[1], precision=HIGHEST)]
    all_to_all x5 -> x0, local copies, waits for them, and re-layouts: 12.4 us -> none  [the longest x3 11.1 us: per_device(): lax.all_to_all(rows_back, 'context', split_axis=4, concat_axis=3, tiled=T...]
    another operation x2 -> x0, local copies, waits for them, and re-layouts: 10.2 us -> none  [the longest x1 8.17 us: per_device(): rows_back = jnp.stack([untwisted[0], untwisted[1]], axis=1)]
    all_to_all x2 -> x0, starting transfers between devices: 8.93 us -> none  [the longest x1 5.17 us: per_device(): lax.all_to_all(signals.reshape(3, channels, context_size, column_len), 'c...]
    pallas_call x0 -> x3, Pallas kernels: none -> 7.97 us  [the longest x1 4.19 us: per_device(): pl.pallas_call(transform, out_shape=jax.ShapeDtypeStruct((n, 2, chunks, L...]
    all_to_all x2, blocking collectives: 21.5 us -> 24.6 us  [the longest x1 13.6 us: per_device(): lax.all_to_all(sent.reshape(n, 3, chunks, LANES), 'context', split_axis=0...]
  transfers between devices with their start and end apart: 2 -> 0, of which waited for: 2 -> 0; matrix products, arithmetic and copies ran while one was open for 1% -> 0% of each run, Pallas kernels for 0% -> 0%
where the time goes in v1:
time: 33.6 us; the launch traced here: 33.2 us
  blocking collectives  24.6 us (73%)
  Pallas kernels  7.97 us (24%)
  between operations  0.63 us (2%)
    all_to_all x1, blocking collectives, per_device(): lax.all_to_all(sent.reshape(n, 3, chunks, LANES), 'context', split_axis=0...  13.6 us
    all_to_all x1, blocking collectives, per_device(): back = lax.all_to_all(y, 'context', split_axis=0, concat_axis=0, tiled=True)  11 us
    pallas_call x1, Pallas kernels, per_device(): pl.pallas_call(transform, out_shape=jax.ShapeDtypeStruct((n, 2, chunks, L...  4.19 us
    pallas_call x1, Pallas kernels, per_device(): pl.pallas_call(spread, out_shape=jax.ShapeDtypeStruct((channels * 3 * chu...  2.01 us
    pallas_call x1, Pallas kernels, per_device(): pl.pallas_call(gather, out_shape=[jax.ShapeDtypeStruct((channels, block),...  1.76 us

profile of v1, /device:TPU:0, one launch (start us, length us, event | category | flops | bytes accessed | tf_op | source)
XLA Modules:
  0.0 33.2 jit_solution(9770485515862358827)
XLA Ops:
  0.6 2.0 %shard_map.140 = f32[768,128]{1,0:T(8,128)} custom-call(f32[8,4096]{1,0:T(8,128)} %a.1, f32[8,4096]{1,0:T(8,128)} %b.1, f32[8,4096]{1,0:T(8,128)} %c.1), custom_call_target="tpu_custom_call" | custom-call | tf_op jit(solution)/shard_map/pallas_call | solution.py:115
  2.6 13.6 %all_to_all.10.x = f32[8,3,32,128]{3,2,1,0:T(8,128)} all-to-all(f32[8,3,32,128]{3,2,1,0:T(8,128)} %bitcast.2), channel_id=1, replica_groups=mesh['context'=8,'tensor'=4] {'context'}, dimensions={0} | all-to-all | bytes 786432 | tf_op jit(solution)/shard_map/all_to_all | solution.py:121
  16.3 4.2 %shard_map.141 = f32[8,2,32,128]{3,2,1,0:T(8,128)} custom-call(f32[8,3,32,128]{3,2,1,0:T(8,128)} %all_to_all.10.x, bf16[512,256]{1,0:T(8,128)(2,1)} %constant.20.clone.fh, bf16[512,256]{1,0:T(8,128)(2,1)} %constant.21.clone.fl, bf16[256,512]{1,0:T(8,128)(2,1)} %constant.22.clone.ih, bf16[256,512]{1,0:T(8,128)(2,1)} %constant.23.clone.il, ...), custom_call_target="tpu_custom_call" | custom-call | tf_op jit(solution)/shard_map/pallas_call | solution.py:122
  20.4 11.0 %all_to_all.11 = f32[8,2,32,128]{3,2,1,0:T(8,128)} all-to-all(f32[8,2,32,128]{3,2,1,0:T(8,128)} %shard_map.141), channel_id=1, replica_groups=mesh['context'=8,'tensor'=4] {'context'}, dimensions={0} | all-to-all | bytes 524288 | tf_op jit(solution)/shard_map/all_to_all | solution.py:128
  31.4 1.8 %shard_map.142 = (f32[8,4096]{1,0:T(8,128)}, f32[8,4096]{1,0:T(8,128)}) custom-call(f32[512,128]{1,0:T(8,128)} %bitcast.3), custom_call_target="tpu_custom_call" | custom-call | tf_op jit(solution)/shard_map/pallas_call | solution.py:129

commit v2 on v0

--- a/solution.py
+++ b/solution.py
@@ -1,9 +1,224 @@
+import functools
 import math
 
 import jax
 import jax.numpy as jnp
+import numpy as np
 from jax import lax
+from jax.experimental import pallas as pl
+from jax.experimental.pallas import tpu as pltpu
 from jax.sharding import PartitionSpec as P
+
+LANES = 128
+BF = jnp.bfloat16
+
+
+def halves(table):
+    table = table.astype(np.float32)
+    high = table.astype(BF)
+    low = (table - high.astype(np.float32)).astype(BF)
+    return high, low
+
+
+def tables(length):
+    rows = length // LANES
+    k = np.arange(rows)[:, None] + 0.25
+    r = np.arange(rows)[None, :]
+    outer = 2 * np.pi * k * r / rows
+    cos1, sin1 = np.cos(outer), np.sin(outer)
+    first = halves(np.concatenate([cos1, -sin1], axis=0))
+    last = halves(np.concatenate([cos1.T, -sin1.T], axis=1) / length)
+    lane = np.arange(LANES)
+    turn = 2 * np.pi * k * lane[None, :] / length
+    twiddle = halves(np.concatenate([np.cos(turn), np.sin(turn)], axis=1))
+    inner = 2 * np.pi * (lane[:, None] * lane[None, :] % LANES) / LANES
+    c2, s2 = np.cos(inner), np.sin(inner)
+    into = halves(np.block([[c2, -s2], [s2, c2]]))
+    wide = [t.reshape(-1, 2 * LANES) for t in (*into, *twiddle)]
+    return np.concatenate(first, axis=0), np.concatenate(last, axis=0), np.concatenate(wide, axis=0)
+
+
+def split(x):
+    high = x.astype(BF)
+    low = (x - high.astype(jnp.float32)).astype(BF)
+    return high, low
+
+
+def dot(a, b):
+    return jnp.dot(a, b, preferred_element_type=jnp.float32)
+
+
+def dot_left(th, tl, x):
+    xh, xl = split(x)
+    return dot(th, xh) + (dot(th, xl) + dot(tl, xh))
+
+
+def dot_right(x, th, tl):
+    xh, xl = split(x)
+    return dot(xh, th) + (dot(xl, th) + dot(xh, tl))
+
+
+def place():
+    me = lax.axis_index("context")
+    chip, core = me // 2, me % 2
+    return core, chip, chip ^ 3, chip ^ (1 + core), chip ^ (2 - core)
+
+
+def part(index, step):
+    return pl.ds(pl.multiple_of(index * step, step), step)
+
+
+def pack(pieces, own, far, aside, beside):
+    core, chip, opposite, one, two = place()
+    step = own.shape[0]
+    here, other = core, 1 - core
+    for out, at, to_chip, to_core in (
+        (own, 0, chip, here), (far, 0, opposite, here), (far, 1, opposite, other),
+        (aside, 0, chip, other), (aside, 1, two, other), (aside, 2, one, other),
+        (beside, 0, one, here), (beside, 1, two, here),
+    ):
+        out[at * step:(at + 1) * step, :] = pieces[part(to_chip * 2 + to_core, step), :]
+
+
+def merge(beside, aside, first, second):
+    step = beside.shape[0] // 2
+    for i, out in enumerate((first, second)):
+        out[:step, :] = beside[i * step:(i + 1) * step, :]
+        out[step:, :] = aside[(i + 1) * step:(i + 2) * step, :]
+
+
+def second_half(x, out):
+    out[...] = x[out.shape[0]:, :]
+
+
+def unpack(got, held):
+    core, chip, opposite, one, two = place()
+    own, aside, far, far_other, first, second = got
+    step = own.shape[0]
+    here, other = core, 1 - core
+    for ref, at, from_chip, from_core in (
+        (own, 0, chip, here), (aside, 0, chip, other), (far, 0, opposite, here), (far_other, 0, opposite, other),
+        (first, 0, one, here), (first, 1, one, other), (second, 0, two, here), (second, 1, two, other),
+    ):
+        held[part(from_chip * 2 + from_core, step), :] = ref[at * step:(at + 1) * step, :]
+
+
+def fetch(*refs):
+    count = (len(refs) - 2) // 2
+    copies = [pltpu.make_async_copy(refs[i], refs[count + 1 + i], refs[-1].at[i]) for i in range(count)]
+    for copy in copies:
+        copy.start()
+    for copy in copies:
+        copy.wait()
+
+
+def spread(a, b, c, *rest):
+    *outs, held = rest
+    channels, block = a.shape
+    chunks = block // LANES
+    for i, ref in enumerate((a, b, c)):
+        for j in range(chunks):
+            held[pl.ds(i * chunks + j, channels, stride=3 * chunks), :] = ref[:, pl.ds(j * LANES, LANES)]
+    pack(held, *outs)
+
+
+def gather(*refs):
+    *got, a, b, held = refs
+    unpack(got, held)
+    channels, block = a.shape
+    chunks = block // LANES
+    for i, ref in enumerate((a, b)):
+        for j in range(chunks):
+            ref[:, pl.ds(j * LANES, LANES)] = held[pl.ds(i * chunks + j, channels, stride=2 * chunks), :]
+
+
+def transform(*refs):
+    got, (first, last, wide), outs, (held, y) = refs[:6], refs[6:9], refs[9:13], refs[13:]
+    unpack(got, held)
+    n = held.shape[0] // got[0].shape[0]
+    chunks = got[0].shape[0] // 3
+    rows = n * chunks
+    pieces = held[...].reshape(n, 3, chunks, LANES)
+    sig = jnp.concatenate([pieces[:, i].reshape(rows, LANES) for i in range(3)], axis=1)
+    spec = dot_left(first[:2 * rows], first[2 * rows:], sig)
+    two = 2 * LANES
+    into_h, into_l = wide[:two], wide[two:2 * two]
+    twiddle = wide[2 * two:2 * two + rows].astype(jnp.float32) + wide[2 * two + rows:].astype(jnp.float32)
+    c, s = twiddle[:, :LANES], twiddle[:, LANES:]
+    parts = []
+    for i in range(3):
+        re = spec[:rows, i * LANES:(i + 1) * LANES]
+        im = spec[rows:, i * LANES:(i + 1) * LANES]
+        v = jnp.concatenate([re * c + im * s, im * c - re * s], axis=1)
+        f = dot_right(v, into_h, into_l)
+        parts.append((f[:, :LANES], f[:, LANES:]))
+    (xr, xi), (gr, gi), (hr, hi) = parts
+    turned = []
+    for ur, ui in ((hr, hi), (xr, xi)):
+        p = jnp.concatenate([ur * gr + ui * gi, ui * gr - ur * gi], axis=1)
+        d = dot_right(p, into_h, into_l)
+        dr, di = d[:, :LANES], d[:, LANES:]
+        turned.append(jnp.concatenate([dr * c + di * s, dr * s - di * c], axis=0))
+    out = dot_left(last[:rows], last[rows:], jnp.concatenate(turned, axis=1))
+    for d in range(n):
+        for i in range(2):
+            y[(d * 2 + i) * chunks:(d * 2 + i + 1) * chunks, :] = out[d * chunks:(d + 1) * chunks, i * LANES:(i + 1) * LANES]
+    pack(y, *outs)
+
+
+def call(body, ins, outs, scratch=(), near_in=True, near_out=True):
+    where = pl.BlockSpec(memory_space=pltpu.VMEM)
+    if near_in:
+        ins = [pltpu.with_memory_space_constraint(x, pltpu.VMEM) for x in ins]
+    kind = pltpu.VMEM if near_out else jax.ShapeDtypeStruct
+    return pl.pallas_call(
+        body,
+        out_shape=[kind(shape, jnp.float32) for shape in outs],
+        in_specs=[where] * len(ins),
+        out_specs=[where] * len(outs),
+        scratch_shapes=[pltpu.VMEM(shape, jnp.float32) for shape in scratch],
+        name=body.__name__,
+    )(*ins)
+
+
+def per_device(inputs, grads, response):
+    n = lax.axis_size("context")
+    channels, block = inputs.shape
+    length = block * n
+    chunks = block // LANES
+    rows = length // LANES
+    signals = (inputs, grads, response)
+
+    def swap(x, even, odd):
+        return lax.ppermute(x, "context", [(i, i ^ (odd if i % 2 else even)) for i in range(n)])
+
+    def sizes(arrays):
+        return [(u * arrays * chunks, LANES) for u in (1, 2, 3, 2)]
+
+    def exchange(own, far, aside, beside):
+        step = own.shape[0]
+        aside = swap(aside, 1, 1)
+        far = swap(far, 6, 6)
+        first, second = call(merge, [beside, aside], [(2 * step, LANES)] * 2)
+        first, second = swap(first, 2, 4), swap(second, 4, 2)
+        (half,) = call(second_half, [far], [(step, LANES)])
+        return own, aside, far, swap(half, 1, 1), first, second
+
+    sent = call(spread, signals, sizes(3), [(channels * 3 * chunks, LANES)], near_in=False)
+    got = exchange(*sent)
+    held = [jnp.asarray(t) for t in tables(length)]
+    held = pl.pallas_call(
+        fetch,
+        out_shape=[pltpu.VMEM(t.shape, t.dtype) for t in held],
+        in_specs=[pl.BlockSpec(memory_space=pl.ANY)] * len(held) + [pl.BlockSpec(memory_space=pltpu.VMEM)],
+        out_specs=[pl.BlockSpec(memory_space=pltpu.VMEM)] * len(held),
+        scratch_shapes=[pltpu.SemaphoreType.DMA((len(held),))],
+        name="fetch",
+    )(*held, pltpu.with_memory_space_constraint(got[1], pltpu.VMEM))
+    sent = call(transform, [*got, *held], sizes(2), [(rows * 3, LANES), (rows * 2, LANES)])
+    got = exchange(*sent)
+    return call(gather, got, [(channels, block)] * 2, [(rows * 2, LANES)], near_out=False)
+
 
 RADIX = 128
 
@@ -32,7 +247,7 @@
     )
 
 
-def per_device(inputs, grads, response):
+def by_columns(inputs, grads, response):
     context_size = lax.axis_size("context")
     device_index = lax.axis_index("context")
     channels, block_len = inputs.shape
@@ -100,11 +315,12 @@
     return (restored[0], restored[1])
 
 
+def by_shape(inputs, grads, response):
+    if inputs.shape[0] == lax.axis_size("context") == 2 * 2 * 2:
+        return per_device(inputs, grads, response)
+    return by_columns(inputs, grads, response)
+
+
 def solution(mesh):
-    return jax.shard_map(
-        per_device,
-        mesh=mesh,
-        in_specs=(P("tensor", "context"), P("tensor", "context"), P("tensor", "context")),
-        out_specs=(P("tensor", "context"), P("tensor", "context")),
-        check_vma=False,
-    )
+    spec = P("tensor", "context")
+    return jax.shard_map(by_shape, mesh=mesh, in_specs=(spec,) * 3, out_specs=(spec,) * 2, check_vma=False)

time: 137 us -> 22.4 us (0.16)
  local copies, waits for them, and re-layouts: 54.9 us -> 0 us
  waiting for transfers between devices: 28.1 us -> 5.63 us
  blocking collectives: 21.5 us -> 0 us
  matrix products: 16.3 us -> 0 us
  Pallas kernels: 0 us -> 5.55 us
  other arithmetic: 5.44 us -> 0 us
  starting transfers between devices: 8.93 us -> 10.3 us
    unnamed x2 -> x0, local copies, waits for them, and re-layouts: 30.9 us -> none
    all_to_all x2 -> x0, waiting for transfers between devices: 28.1 us -> none  [the longest x1 19.8 us: per_device(): lax.all_to_all(columns, 'context', split_axis=3, concat_axis=4, tiled=True)]
    all_to_all x2 -> x0, blocking collectives: 21.5 us -> none  [the longest x1 12.2 us: per_device(): lax.all_to_all(rows_back, 'context', split_axis=4, concat_axis=3, tiled=T...]
    dot_general x22 -> x0, matrix products: 16.3 us -> none  [the longest x4 3.42 us: complex_apply(): real_imag = jnp.einsum(pattern, tables[0], values[1], precision=HIGHEST)]
    all_to_all x5 -> x0, local copies, waits for them, and re-layouts: 12.4 us -> none  [the longest x3 11.1 us: per_device(): lax.all_to_all(rows_back, 'context', split_axis=4, concat_axis=3, tiled=T...]
    ppermute x0 -> x10, starting transfers between devices: none -> 10.3 us  [swap(): lax.ppermute(x, 'context', [(i, i ^ (odd if i % 2 else even)) for i in ra...]
    another operation x2 -> x0, local copies, waits for them, and re-layouts: 10.2 us -> none  [the longest x1 8.17 us: per_device(): rows_back = jnp.stack([untwisted[0], untwisted[1]], axis=1)]
    all_to_all x2 -> x0, starting transfers between devices: 8.93 us -> none  [the longest x1 5.17 us: per_device(): lax.all_to_all(signals.reshape(3, channels, context_size, column_len), 'c...]
  transfers between devices with their start and end apart: 2 -> 10, of which waited for: 2 -> 6; matrix products, arithmetic and copies ran while one was open for 1% -> 0% of each run, Pallas kernels for 0% -> 6%
where the time goes in v2:
time: 22.4 us; the launch traced here: 22.2 us
  starting transfers between devices  10.3 us (46%)
  waiting for transfers between devices  5.63 us (25%)
  Pallas kernels  5.55 us (25%)
  between operations  0.69 us (3%)
    ppermute x10, starting transfers between devices, swap(): lax.ppermute(x, 'context', [(i, i ^ (odd if i % 2 else even)) for i in ra...  10.3 us
    ppermute x10, waiting for transfers between devices, swap(): lax.ppermute(x, 'context', [(i, i ^ (odd if i % 2 else even)) for i in ra...  5.63 us
    pallas_call x7, Pallas kernels, call(): pl.pallas_call(body, out_shape=[kind(shape, jnp.float32) for shape in out...  4.16 us
    pallas_call x1, Pallas kernels, per_device(): pl.pallas_call(fetch, out_shape=[pltpu.VMEM(t.shape, t.dtype) for t in he...  1.39 us
  transfers between devices with their start and end apart: 10, of which 6 were waited for; matrix products, arithmetic and copies ran while one was open for 0% of the time, Pallas kernels for 6%

profile of v2, /device:TPU:0, one launch (start us, length us, event | category | flops | bytes accessed | tf_op | source)
XLA Modules:
  0.0 22.2 jit_solution(9560411531317841587)
XLA Ops:
  0.6 1.3 %spread.1 = (f32[96,128]{1,0:T(8,128)S(1)}, f32[192,128]{1,0:T(8,128)S(1)}, f32[288,128]{1,0:T(8,128)S(1)}, f32[192,128]{1,0:T(8,128)S(1)}) custom-call(f32[8,4096]{1,0:T(8,128)} %a.1, f32[8,4096]{1,0:T(8,128)} %b.1, f32[8,4096]{1,0:T(8,128)} %c.1), custom_call_target="tpu_custom_call" | custom-call | tf_op jit(solution)/shard_map/spread/pallas_call | solution.py:174
  1.9 0.5 %collective-permute-start = (f32[288,128]{1,0:T(8,128)S(1)}, f32[288,128]{1,0:T(8,128)S(1)}, u32[]{:S(2)}, u32[]{:S(2)}) collective-permute-start(f32[288,128]{1,0:T(8,128)S(1)} %get-tuple-element.18), channel_id=1, source_target_pairs={{0,4},{4,0},{8,12},{12,8},{16,20},{20,16},{24,28},{28,24},{1,5},{5... | collective-permute-start | bytes 442376 | tf_op jit(solution)/shard_map/ppermute | solution.py:193
  2.4 3.5 %collective-permute-start.1 = (f32[192,128]{1,0:T(8,128)S(1)}, f32[192,128]{1,0:T(8,128)S(1)}, u32[]{:S(2)}, u32[]{:S(2)}) collective-permute-start(f32[192,128]{1,0:T(8,128)S(1)} %get-tuple-element.19), channel_id=1, source_target_pairs={{0,24},{4,28},{8,16},{12,20},{16,8},{20,12},{24,0},{28,4},{1,25},{... | collective-permute-start | bytes 294920 | tf_op jit(solution)/shard_map/ppermute | solution.py:193
  6.0 0.0 collective-permute-done.aside.refs_3_.refs_1_
  6.0 0.6 %collective-permute-start.3 = (f32[192,128]{1,0:T(8,128)S(1)}, f32[192,128]{1,0:T(8,128)S(1)}, u32[]{:S(2)}, u32[]{:S(2)}) collective-permute-start(f32[192,128]{1,0:T(8,128)S(1)} %get-tuple-element.21), channel_id=1, source_target_pairs={{0,8},{4,20},{8,0},{12,28},{16,24},{20,4},{24,16},{28,12},{1,9},{5... | collective-permute-start | bytes 294920 | tf_op jit(solution)/shard_map/ppermute | solution.py:193
  6.6 1.3 %collective-permute-start.4 = (f32[192,128]{1,0:T(8,128)S(1)}, f32[192,128]{1,0:T(8,128)S(1)}, u32[]{:S(2)}, u32[]{:S(2)}) collective-permute-start(f32[192,128]{1,0:T(8,128)S(1)} %get-tuple-element.22), channel_id=1, source_target_pairs={{0,16},{4,12},{8,24},{12,4},{16,0},{20,28},{24,8},{28,20},{1,17},{... | collective-permute-start | bytes 294920 | tf_op jit(solution)/shard_map/ppermute | solution.py:193
  7.9 1.5 %collective-permute-done.1.x.refs_2_ = f32[192,128]{1,0:T(8,128)S(1)} collective-permute-done((f32[192,128]{1,0:T(8,128)S(1)}, f32[192,128]{1,0:T(8,128)S(1)}, u32[]{:S(2)}, u32[]{:S(2)}) %collective-permute-start.1) | collective-permute-done | bytes 98336 | tf_op jit(solution)/shard_map/ppermute | solution.py:193
  9.4 0.0 collective-permute-start.2
  9.4 1.4 %fetch.1 = (bf16[1024,256]{1,0:T(8,128)(2,1)S(1)}, bf16[512,512]{1,0:T(8,128)(2,1)S(1)}, bf16[1024,256]{1,0:T(8,128)(2,1)S(1)}) custom-call(bf16[1024,256]{1,0:T(8,128)(2,1)} %constant.6.clone.refs_0_, bf16[512,512]{1,0:T(8,128)(2,1)} %constant.7.clone.refs_1_, bf16[1024,256]{1,0:T(8,128)(2,1)} %constant.8.clone.refs_2_, ...), custom_call_target="tpu_custom_call" | custom-call | tf_op jit(solution)/shard_map/fetch/pallas_call | solution.py:210
  10.8 0.0 collective-permute-done.2.refs_3_
  10.8 0.9 %collective-permute-done.3.refs_4_ = f32[192,128]{1,0:T(8,128)S(1)} collective-permute-done((f32[192,128]{1,0:T(8,128)S(1)}, f32[192,128]{1,0:T(8,128)S(1)}, u32[]{:S(2)}, u32[]{:S(2)}) %collective-permute-start.3) | collective-permute-done | bytes 98336 | tf_op jit(solution)/shard_map/ppermute | solution.py:193
  11.7 0.0 collective-permute-done.4.refs_5_
  11.7 2.0 %transform.1 = (f32[64,128]{1,0:T(8,128)S(1)}, f32[128,128]{1,0:T(8,128)S(1)}, f32[192,128]{1,0:T(8,128)S(1)}, f32[128,128]{1,0:T(8,128)S(1)}) custom-call(f32[96,128]{1,0:T(8,128)S(1)} %get-tuple-element.17.refs_0_, f32[288,128]{1,0:T(8,128)S(1)} %collective-permute-done.aside.refs_3_.refs_1_, f32[192,128]{1,0:T(8,128)S(1)} %collective-permute-done.1.x.refs_2_, ...), custom_call_target="tpu_custom_call" | custom-call | tf_op jit(solution)/shard_map/transform/pallas_call | solution.py:174
  13.7 0.1 collective-permute-start.5
  13.8 2.7 %collective-permute-start.6 = (f32[128,128]{1,0:T(8,128)S(1)}, f32[128,128]{1,0:T(8,128)S(1)}, u32[]{:S(2)}, u32[]{:S(2)}) collective-permute-start(f32[128,128]{1,0:T(8,128)S(1)} %get-tuple-element.28), channel_id=1, source_target_pairs={{0,24},{4,28},{8,16},{12,20},{16,8},{20,12},{24,0},{28,4},{1,25},{... | collective-permute-start | bytes 196616 | tf_op jit(solution)/shard_map/ppermute | solution.py:193
  16.5 0.0 collective-permute-done.5.aside.refs_1_
  16.5 0.6 %collective-permute-start.8 = (f32[128,128]{1,0:T(8,128)S(1)}, f32[128,128]{1,0:T(8,128)S(1)}, u32[]{:S(2)}, u32[]{:S(2)}) collective-permute-start(f32[128,128]{1,0:T(8,128)S(1)} %get-tuple-element.30), channel_id=1, source_target_pairs={{0,8},{4,20},{8,0},{12,28},{16,24},{20,4},{24,16},{28,12},{1,9},{5... | collective-permute-start | bytes 196616 | tf_op jit(solution)/shard_map/ppermute | solution.py:193
  17.1 1.0 %collective-permute-start.9 = (f32[128,128]{1,0:T(8,128)S(1)}, f32[128,128]{1,0:T(8,128)S(1)}, u32[]{:S(2)}, u32[]{:S(2)}) collective-permute-start(f32[128,128]{1,0:T(8,128)S(1)} %get-tuple-element.31), channel_id=1, source_target_pairs={{0,16},{4,12},{8,24},{12,4},{16,0},{20,28},{24,8},{28,20},{1,17},{... | collective-permute-start | bytes 196616 | tf_op jit(solution)/shard_map/ppermute | solution.py:193
  18.1 1.1 %collective-permute-done.6.x.refs_2_ = f32[128,128]{1,0:T(8,128)S(1)} collective-permute-done((f32[128,128]{1,0:T(8,128)S(1)}, f32[128,128]{1,0:T(8,128)S(1)}, u32[]{:S(2)}, u32[]{:S(2)}) %collective-permute-start.6) | collective-permute-done | bytes 65568 | tf_op jit(solution)/shard_map/ppermute | solution.py:193
  19.2 0.0 collective-permute-start.7
  19.2 1.2 %collective-permute-done.7.refs_3_ = f32[64,128]{1,0:T(8,128)S(1)} collective-permute-done((f32[64,128]{1,0:T(8,128)S(1)}, f32[64,128]{1,0:T(8,128)S(1)}, u32[]{:S(2)}, u32[]{:S(2)}) %collective-permute-start.7) | collective-permute-done | bytes 32800 | tf_op jit(solution)/shard_map/ppermute | solution.py:193
  20.4 0.4 %collective-permute-done.8.refs_4_ = f32[128,128]{1,0:T(8,128)S(1)} collective-permute-done((f32[128,128]{1,0:T(8,128)S(1)}, f32[128,128]{1,0:T(8,128)S(1)}, u32[]{:S(2)}, u32[]{:S(2)}) %collective-permute-start.8) | collective-permute-done | bytes 65568 | tf_op jit(solution)/shard_map/ppermute | solution.py:193
  20.8 0.5 %collective-permute-done.9.refs_5_ = f32[128,128]{1,0:T(8,128)S(1)} collective-permute-done((f32[128,128]{1,0:T(8,128)S(1)}, f32[128,128]{1,0:T(8,128)S(1)}, u32[]{:S(2)}, u32[]{:S(2)}) %collective-permute-start.9) | collective-permute-done | bytes 65568 | tf_op jit(solution)/shard_map/ppermute | solution.py:193
  21.4 0.8 %gather.1 = (f32[8,4096]{1,0:T(8,128)}, f32[8,4096]{1,0:T(8,128)}) custom-call(f32[64,128]{1,0:T(8,128)S(1)} %get-tuple-element.26.refs_0_, f32[192,128]{1,0:T(8,128)S(1)} %collective-permute-done.5.aside.refs_1_, f32[128,128]{1,0:T(8,128)S(1)} %collective-permute-done.6.x.refs_2_, f32[64,128]{1,0:T(8,128)S(1)} %collective-permute-done.7.refs_3_, ...), custom_call_target="tpu_custom_call" | custom-call | tf_op jit(solution)/shard_map/gather/pallas_call | solution.py:174
  (4 shorter events, 0.0 us)
Async XLA Ops:
  1.9 4.0 %collective-permute-start = (f32[288,128]{1,0:T(8,128)S(1)}, f32[288,128]{1,0:T(8,128)S(1)}, u32[]{:S(2)}, u32[]{:S(2)}) collective-permute-start(f32[288,128]{1,0:T(8,128)S(1)} %get-tuple-element.18), channel_id=1, source_target_pairs={{0,4},{4,0},{8,12},{12,8},{16,20},{20,16},{24,28},{28,24},{1,5},{5... | collective-permute-start | bytes 442376 | tf_op jit(solution)/shard_map/ppermute | solution.py:193
  2.4 7.0 %collective-permute-start.1 = (f32[192,128]{1,0:T(8,128)S(1)}, f32[192,128]{1,0:T(8,128)S(1)}, u32[]{:S(2)}, u32[]{:S(2)}) collective-permute-start(f32[192,128]{1,0:T(8,128)S(1)} %get-tuple-element.19), channel_id=1, source_target_pairs={{0,24},{4,28},{8,16},{12,20},{16,8},{20,12},{24,0},{28,4},{1,25},{... | collective-permute-start | bytes 294920 | tf_op jit(solution)/shard_map/ppermute | solution.py:193
  6.0 5.7 %collective-permute-start.3 = (f32[192,128]{1,0:T(8,128)S(1)}, f32[192,128]{1,0:T(8,128)S(1)}, u32[]{:S(2)}, u32[]{:S(2)}) collective-permute-start(f32[192,128]{1,0:T(8,128)S(1)} %get-tuple-element.21), channel_id=1, source_target_pairs={{0,8},{4,20},{8,0},{12,28},{16,24},{20,4},{24,16},{28,12},{1,9},{5... | collective-permute-start | bytes 294920 | tf_op jit(solution)/shard_map/ppermute | solution.py:193
  6.6 5.1 %collective-permute-start.4 = (f32[192,128]{1,0:T(8,128)S(1)}, f32[192,128]{1,0:T(8,128)S(1)}, u32[]{:S(2)}, u32[]{:S(2)}) collective-permute-start(f32[192,128]{1,0:T(8,128)S(1)} %get-tuple-element.22), channel_id=1, source_target_pairs={{0,16},{4,12},{8,24},{12,4},{16,0},{20,28},{24,8},{28,20},{1,17},{... | collective-permute-start | bytes 294920 | tf_op jit(solution)/shard_map/ppermute | solution.py:193
  9.4 1.4 %collective-permute-start.2 = (f32[96,128]{1,0:T(8,128)S(1)}, f32[96,128]{1,0:T(8,128)S(1)}, u32[]{:S(2)}, u32[]{:S(2)}) collective-permute-start(f32[96,128]{1,0:T(8,128)S(1)} %second_half.2), channel_id=1, source_target_pairs={{0,4},{4,0},{8,12},{12,8},{16,20},{20,16},{24,28},{28,24},{1,5},{5... | collective-permute-start | bytes 147464 | tf_op jit(solution)/shard_map/ppermute | solution.py:193
  13.7 2.7 %collective-permute-start.5 = (f32[192,128]{1,0:T(8,128)S(1)}, f32[192,128]{1,0:T(8,128)S(1)}, u32[]{:S(2)}, u32[]{:S(2)}) collective-permute-start(f32[192,128]{1,0:T(8,128)S(1)} %get-tuple-element.27), channel_id=1, source_target_pairs={{0,4},{4,0},{8,12},{12,8},{16,20},{20,16},{24,28},{28,24},{1,5},{5... | collective-permute-start | bytes 294920 | tf_op jit(solution)/shard_map/ppermute | solution.py:193
  13.8 5.4 %collective-permute-start.6 = (f32[128,128]{1,0:T(8,128)S(1)}, f32[128,128]{1,0:T(8,128)S(1)}, u32[]{:S(2)}, u32[]{:S(2)}) collective-permute-start(f32[128,128]{1,0:T(8,128)S(1)} %get-tuple-element.28), channel_id=1, source_target_pairs={{0,24},{4,28},{8,16},{12,20},{16,8},{20,12},{24,0},{28,4},{1,25},{... | collective-permute-start | bytes 196616 | tf_op jit(solution)/shard_map/ppermute | solution.py:193
  16.5 4.3 %collective-permute-start.8 = (f32[128,128]{1,0:T(8,128)S(1)}, f32[128,128]{1,0:T(8,128)S(1)}, u32[]{:S(2)}, u32[]{:S(2)}) collective-permute-start(f32[128,128]{1,0:T(8,128)S(1)} %get-tuple-element.30), channel_id=1, source_target_pairs={{0,8},{4,20},{8,0},{12,28},{16,24},{20,4},{24,16},{28,12},{1,9},{5... | collective-permute-start | bytes 196616 | tf_op jit(solution)/shard_map/ppermute | solution.py:193
  17.1 4.3 %collective-permute-start.9 = (f32[128,128]{1,0:T(8,128)S(1)}, f32[128,128]{1,0:T(8,128)S(1)}, u32[]{:S(2)}, u32[]{:S(2)}) collective-permute-start(f32[128,128]{1,0:T(8,128)S(1)} %get-tuple-element.31), channel_id=1, source_target_pairs={{0,16},{4,12},{8,24},{12,4},{16,0},{20,28},{24,8},{28,20},{1,17},{... | collective-permute-start | bytes 196616 | tf_op jit(solution)/shard_map/ppermute | solution.py:193
  19.2 1.2 %collective-permute-start.7 = (f32[64,128]{1,0:T(8,128)S(1)}, f32[64,128]{1,0:T(8,128)S(1)}, u32[]{:S(2)}, u32[]{:S(2)}) collective-permute-start(f32[64,128]{1,0:T(8,128)S(1)} %second_half.3), channel_id=1, source_target_pairs={{0,4},{4,0},{8,12},{12,8},{16,20},{20,16},{24,28},{28,24},{1,5},{5... | collective-permute-start | bytes 98312 | tf_op jit(solution)/shard_map/ppermute | solution.py:193

commit v3 on v2

--- a/solution.py
+++ b/solution.py
@@ -11,6 +11,7 @@
 
 LANES = 128
 BF = jnp.bfloat16
+PARTS, JOINED, LOADS = 4, 2, 4
 
 
 def halves(table):
@@ -20,22 +21,22 @@
     return high, low
 
 
-def tables(length):
+def tables(length, parts, joined):
     rows = length // LANES
     k = np.arange(rows)[:, None] + 0.25
     r = np.arange(rows)[None, :]
     outer = 2 * np.pi * k * r / rows
-    cos1, sin1 = np.cos(outer), np.sin(outer)
-    first = halves(np.concatenate([cos1, -sin1], axis=0))
-    last = halves(np.concatenate([cos1.T, -sin1.T], axis=1) / length)
+    stacked = np.stack([np.cos(outer), -np.sin(outer)])
+    first = stacked.reshape(2, parts, rows // parts, rows).swapaxes(0, 1).reshape(2 * rows, rows)
+    last = (stacked / length).reshape(2, joined, rows // joined, rows).transpose(1, 3, 0, 2)
+    last = last.reshape(joined, rows, 2 * rows // joined)
     lane = np.arange(LANES)
     turn = 2 * np.pi * k * lane[None, :] / length
-    twiddle = halves(np.concatenate([np.cos(turn), np.sin(turn)], axis=1))
+    twiddle = np.concatenate([np.cos(turn), np.sin(turn)], axis=1).astype(np.float32)
     inner = 2 * np.pi * (lane[:, None] * lane[None, :] % LANES) / LANES
-    c2, s2 = np.cos(inner), np.sin(inner)
-    into = halves(np.block([[c2, -s2], [s2, c2]]))
-    wide = [t.reshape(-1, 2 * LANES) for t in (*into, *twiddle)]
-    return np.concatenate(first, axis=0), np.concatenate(last, axis=0), np.concatenate(wide, axis=0)
+    cos2, sin2 = np.cos(inner), np.sin(inner)
+    into = np.block([[cos2, -sin2], [sin2, cos2]])
+    return np.stack(halves(first)), np.stack(halves(last)), np.stack(halves(into)), twiddle
 
 
 def split(x):
@@ -48,14 +49,18 @@
     return jnp.dot(a, b, preferred_element_type=jnp.float32)
 
 
-def dot_left(th, tl, x):
-    xh, xl = split(x)
-    return dot(th, xh) + (dot(th, xl) + dot(tl, xh))
-
-
-def dot_right(x, th, tl):
-    xh, xl = split(x)
-    return dot(xh, th) + (dot(xl, th) + dot(xh, tl))
+def dot_right(x, table):
+    high, low = split(x)
+    return dot(high, table[0]) + (dot(low, table[0]) + dot(high, table[1]))
+
+
+def dot_left(table_high, table_low, x):
+    high, low = x
+    return dot(table_high, high) + (dot(table_high, low) + dot(table_low, high))
+
+
+def lanes_of(x, i, m):
+    return x[i * m:(i + 1) * m, :LANES], x[i * m:(i + 1) * m, LANES:]
 
 
 def place():
@@ -87,7 +92,8 @@
         out[step:, :] = aside[(i + 1) * step:(i + 2) * step, :]
 
 
-def second_half(x, out):
+def second_half(x, *rest):
+    out = rest[-1]
     out[...] = x[out.shape[0]:, :]
 
 
@@ -112,14 +118,61 @@
         copy.wait()
 
 
-def spread(a, b, c, *rest):
-    *outs, held = rest
-    channels, block = a.shape
+def spread(*refs):
+    signals, outs, near, (held, arrived) = refs[:3], refs[3:7], refs[7:10], refs[10:]
+    channels, block = signals[0].shape
     chunks = block // LANES
-    for i, ref in enumerate((a, b, c)):
-        for j in range(chunks):
-            held[pl.ds(i * chunks + j, channels, stride=3 * chunks), :] = ref[:, pl.ds(j * LANES, LANES)]
+    width = block // LOADS
+    copies = []
+    for load in range(LOADS):
+        at = pl.ds(load * width, width)
+        for i in range(3):
+            copies.append(pltpu.make_async_copy(signals[i].at[:, at], near[i].at[:, at], arrived.at[load * 3 + i]))
+            copies[-1].start()
+    for load in range(LOADS):
+        for i in range(3):
+            copies[load * 3 + i].wait()
+            for j in range(load * chunks // LOADS, (load + 1) * chunks // LOADS):
+                held[pl.ds(i * chunks + j, channels, stride=3 * chunks), :] = near[i][:, pl.ds(j * LANES, LANES)]
     pack(held, *outs)
+
+
+def transform(*refs):
+    got, (first, last, into, twiddle), outs, (held, y) = refs[:6], refs[6:10], refs[10:14], refs[14:]
+    unpack(got, held)
+    n = held.shape[0] // got[0].shape[0]
+    chunks = got[0].shape[0] // 3
+    rows = n * chunks
+    m = rows // PARTS
+    pieces = held[...].reshape(n, 3, chunks, LANES)
+    signals = split(jnp.concatenate([pieces[:, i].reshape(rows, LANES) for i in range(3)], axis=1))
+    turns = [lanes_of(twiddle, q, m) for q in range(PARTS)]
+    outer = [dot_left(first[0, 2 * m * q:2 * m * (q + 1)], first[1, 2 * m * q:2 * m * (q + 1)], signals) for q in range(PARTS)]
+    spectra = []
+    for z, (c, s) in zip(outer, turns):
+        turned = []
+        for i in range(3):
+            re, im = z[:m, i * LANES:(i + 1) * LANES], z[m:, i * LANES:(i + 1) * LANES]
+            turned.append(jnp.concatenate([re * c + im * s, im * c - re * s], axis=1))
+        spectra.append(dot_right(jnp.concatenate(turned, axis=0), into))
+    backs = []
+    for z in spectra:
+        (xr, xi), (gr, gi), (hr, hi) = (lanes_of(z, i, m) for i in range(3))
+        p = [jnp.concatenate([ur * gr + ui * gi, ui * gr - ur * gi], axis=1) for ur, ui in ((hr, hi), (xr, xi))]
+        backs.append(dot_right(jnp.concatenate(p, axis=0), into))
+    out = 0.0
+    for joined in range(JOINED):
+        real, imag = [], []
+        for q in range(joined * PARTS // JOINED, (joined + 1) * PARTS // JOINED):
+            c, s = turns[q]
+            pairs = [lanes_of(backs[q], i, m) for i in range(2)]
+            real.append(jnp.concatenate([dr * c + di * s for dr, di in pairs], axis=1))
+            imag.append(jnp.concatenate([dr * s - di * c for dr, di in pairs], axis=1))
+        out += dot_left(last[0, joined], last[1, joined], split(jnp.concatenate(real + imag, axis=0)))
+    for d in range(n):
+        for i in range(2):
+            y[(d * 2 + i) * chunks:(d * 2 + i + 1) * chunks, :] = out[d * chunks:(d + 1) * chunks, i * LANES:(i + 1) * LANES]
+    pack(y, *outs)
 
 
 def gather(*refs):
@@ -132,92 +185,53 @@
             ref[:, pl.ds(j * LANES, LANES)] = held[pl.ds(i * chunks + j, channels, stride=2 * chunks), :]
 
 
-def transform(*refs):
-    got, (first, last, wide), outs, (held, y) = refs[:6], refs[6:9], refs[9:13], refs[13:]
-    unpack(got, held)
-    n = held.shape[0] // got[0].shape[0]
-    chunks = got[0].shape[0] // 3
-    rows = n * chunks
-    pieces = held[...].reshape(n, 3, chunks, LANES)
-    sig = jnp.concatenate([pieces[:, i].reshape(rows, LANES) for i in range(3)], axis=1)
-    spec = dot_left(first[:2 * rows], first[2 * rows:], sig)
-    two = 2 * LANES
-    into_h, into_l = wide[:two], wide[two:2 * two]
-    twiddle = wide[2 * two:2 * two + rows].astype(jnp.float32) + wide[2 * two + rows:].astype(jnp.float32)
-    c, s = twiddle[:, :LANES], twiddle[:, LANES:]
-    parts = []
-    for i in range(3):
-        re = spec[:rows, i * LANES:(i + 1) * LANES]
-        im = spec[rows:, i * LANES:(i + 1) * LANES]
-        v = jnp.concatenate([re * c + im * s, im * c - re * s], axis=1)
-        f = dot_right(v, into_h, into_l)
-        parts.append((f[:, :LANES], f[:, LANES:]))
-    (xr, xi), (gr, gi), (hr, hi) = parts
-    turned = []
-    for ur, ui in ((hr, hi), (xr, xi)):
-        p = jnp.concatenate([ur * gr + ui * gi, ui * gr - ur * gi], axis=1)
-        d = dot_right(p, into_h, into_l)
-        dr, di = d[:, :LANES], d[:, LANES:]
-        turned.append(jnp.concatenate([dr * c + di * s, dr * s - di * c], axis=0))
-    out = dot_left(last[:rows], last[rows:], jnp.concatenate(turned, axis=1))
-    for d in range(n):
-        for i in range(2):
-            y[(d * 2 + i) * chunks:(d * 2 + i + 1) * chunks, :] = out[d * chunks:(d + 1) * chunks, i * LANES:(i + 1) * LANES]
-    pack(y, *outs)
-
-
-def call(body, ins, outs, scratch=(), near_in=True, near_out=True):
-    where = pl.BlockSpec(memory_space=pltpu.VMEM)
-    if near_in:
-        ins = [pltpu.with_memory_space_constraint(x, pltpu.VMEM) for x in ins]
+def call(body, ins, outs, scratch=(), far_in=0, near_out=True):
+    near = pl.BlockSpec(memory_space=pltpu.VMEM)
     kind = pltpu.VMEM if near_out else jax.ShapeDtypeStruct
     return pl.pallas_call(
         body,
-        out_shape=[kind(shape, jnp.float32) for shape in outs],
-        in_specs=[where] * len(ins),
-        out_specs=[where] * len(outs),
-        scratch_shapes=[pltpu.VMEM(shape, jnp.float32) for shape in scratch],
+        out_shape=[kind(shape, dtype) for shape, dtype in outs],
+        in_specs=[pl.BlockSpec(memory_space=pl.ANY)] * far_in + [near] * (len(ins) - far_in),
+        out_specs=[near] * len(outs),
+        scratch_shapes=scratch,
         name=body.__name__,
-    )(*ins)
+    )(*ins[:far_in], *(pltpu.with_memory_space_constraint(x, pltpu.VMEM) for x in ins[far_in:]))
 
 
 def per_device(inputs, grads, response):
     n = lax.axis_size("context")
     channels, block = inputs.shape
-    length = block * n
     chunks = block // LANES
-    rows = length // LANES
-    signals = (inputs, grads, response)
+    kind = jnp.float32
 
     def swap(x, even, odd):
         return lax.ppermute(x, "context", [(i, i ^ (odd if i % 2 else even)) for i in range(n)])
 
     def sizes(arrays):
-        return [(u * arrays * chunks, LANES) for u in (1, 2, 3, 2)]
-
-    def exchange(own, far, aside, beside):
+        return [((u * arrays * chunks, LANES), kind) for u in (1, 2, 3, 2)]
+
+    def exchange(own, far, aside, beside, meanwhile=lambda x: []):
         step = own.shape[0]
         aside = swap(aside, 1, 1)
         far = swap(far, 6, 6)
-        first, second = call(merge, [beside, aside], [(2 * step, LANES)] * 2)
+        first, second = call(merge, [beside, aside], [((2 * step, LANES), kind)] * 2)
+        made = meanwhile(second)
         first, second = swap(first, 2, 4), swap(second, 4, 2)
-        (half,) = call(second_half, [far], [(step, LANES)])
-        return own, aside, far, swap(half, 1, 1), first, second
-
-    sent = call(spread, signals, sizes(3), [(channels * 3 * chunks, LANES)], near_in=False)
-    got = exchange(*sent)
-    held = [jnp.asarray(t) for t in tables(length)]
-    held = pl.pallas_call(
-        fetch,
-        out_shape=[pltpu.VMEM(t.shape, t.dtype) for t in held],
-        in_specs=[pl.BlockSpec(memory_space=pl.ANY)] * len(held) + [pl.BlockSpec(memory_space=pltpu.VMEM)],
-        out_specs=[pl.BlockSpec(memory_space=pltpu.VMEM)] * len(held),
-        scratch_shapes=[pltpu.SemaphoreType.DMA((len(held),))],
-        name="fetch",
-    )(*held, pltpu.with_memory_space_constraint(got[1], pltpu.VMEM))
-    sent = call(transform, [*got, *held], sizes(2), [(rows * 3, LANES), (rows * 2, LANES)])
-    got = exchange(*sent)
-    return call(gather, got, [(channels, block)] * 2, [(rows * 2, LANES)], near_out=False)
+        (half,) = call(second_half, [far, *made[:1]], [((step, LANES), kind)])
+        return [own, aside, far, swap(half, 1, 1), first, second, *made]
+
+    held = [jnp.asarray(t) for t in tables(n * block, PARTS, JOINED)]
+
+    def bring(after):
+        return call(fetch, [*held, after], [(t.shape, t.dtype) for t in held], [pltpu.SemaphoreType.DMA((len(held),))], len(held))
+
+    near = [pltpu.VMEM((channels, block), kind)] * 3
+    near += [pltpu.VMEM((channels * 3 * chunks, LANES), kind), pltpu.SemaphoreType.DMA((3 * LOADS,))]
+    sent = call(spread, [inputs, grads, response], sizes(3), near, 3)
+    got = exchange(*sent, meanwhile=bring)
+    near = [pltpu.VMEM((n * arrays * chunks, LANES), kind) for arrays in (3, 2)]
+    got = exchange(*call(transform, got, sizes(2), near))
+    return call(gather, got, [((channels, block), kind)] * 2, near[1:], near_out=False)
 
 
 RADIX = 128

time: 22.4 us -> 21.6 us (0.964)
  waiting for transfers between devices: 5.63 us -> 4.57 us
  local copies, waits for them, and re-layouts: 0 us -> 0.79 us
  Pallas kernels: 5.55 us -> 4.88 us
    ppermute x10, waiting for transfers between devices: 5.63 us -> 4.57 us  [swap(): lax.ppermute(x, 'context', [(i, i ^ (odd if i % 2 else even)) for i in ra...]
    unnamed x0 -> x4, local copies, waits for them, and re-layouts: none -> 0.79 us
    pallas_call x8, Pallas kernels: 5.55 us -> 4.88 us  [call(): pl.pallas_call(body, out_shape=[kind(shape, dtype) for shape, dtype in ou...]
  transfers between devices with their start and end apart: 10 -> 10, of which waited for: 6 -> 6; matrix products, arithmetic and copies ran while one was open for 0% -> 0% of each run, Pallas kernels for 6% -> 7%
where the time goes in v3:
time: 21.6 us; the launch traced here: 21.3 us
  starting transfers between devices  10.4 us (48%)
  Pallas kernels  4.88 us (23%)
  waiting for transfers between devices  4.57 us (21%)
  local copies, waits for them, and re-layouts  0.79 us (4%)
  between operations  0.7 us (3%)
    ppermute x10, starting transfers between devices, swap(): lax.ppermute(x, 'context', [(i, i ^ (odd if i % 2 else even)) for i in ra...  10.4 us
    pallas_call x8, Pallas kernels, call(): pl.pallas_call(body, out_shape=[kind(shape, dtype) for shape, dtype in ou...  4.88 us
    ppermute x10, waiting for transfers between devices, swap(): lax.ppermute(x, 'context', [(i, i ^ (odd if i % 2 else even)) for i in ra...  4.57 us
    unnamed x4, local copies, waits for them, and re-layouts  0.79 us
  transfers between devices with their start and end apart: 10, of which 6 were waited for; matrix products, arithmetic and copies ran while one was open for 0% of the time, Pallas kernels for 7%

profile of v3, /device:TPU:0, one launch (start us, length us, event | category | flops | bytes accessed | tf_op | source)
XLA Modules:
  0.0 21.3 jit_solution(18015848272388336721)
XLA Ops:
  0.6 1.1 %spread.1 = (f32[96,128]{1,0:T(8,128)S(1)}, f32[192,128]{1,0:T(8,128)S(1)}, f32[288,128]{1,0:T(8,128)S(1)}, f32[192,128]{1,0:T(8,128)S(1)}) custom-call(f32[8,4096]{1,0:T(8,128)} %refs_0_.2, f32[8,4096]{1,0:T(8,128)} %refs_1_.2, f32[8,4096]{1,0:T(8,128)} %refs_2_.2), custom_call_target="tpu_custom_call" | custom-call | tf_op jit(solution)/shard_map/spread/pallas_call | solution.py:191
  1.8 0.5 %collective-permute-start = (f32[288,128]{1,0:T(8,128)S(1)}, f32[288,128]{1,0:T(8,128)S(1)}, u32[]{:S(2)}, u32[]{:S(2)}) collective-permute-start(f32[288,128]{1,0:T(8,128)S(1)} %get-tuple-element.19), channel_id=1, source_target_pairs={{0,4},{4,0},{8,12},{12,8},{16,20},{20,16},{24,28},{28,24},{1,5},{5... | collective-permute-start | bytes 442376 | tf_op jit(solution)/shard_map/ppermute | solution.py:208
  2.3 3.5 %collective-permute-start.1 = (f32[192,128]{1,0:T(8,128)S(1)}, f32[192,128]{1,0:T(8,128)S(1)}, u32[]{:S(2)}, u32[]{:S(2)}) collective-permute-start(f32[192,128]{1,0:T(8,128)S(1)} %get-tuple-element.20), channel_id=1, source_target_pairs={{0,24},{4,28},{8,16},{12,20},{16,8},{20,12},{24,0},{28,4},{1,25},{... | collective-permute-start | bytes 294920 | tf_op jit(solution)/shard_map/ppermute | solution.py:208
  5.8 0.0 collective-permute-done.aside.refs_1_
  5.8 0.6 %collective-permute-start.3 = (f32[192,128]{1,0:T(8,128)S(1)}, f32[192,128]{1,0:T(8,128)S(1)}, u32[]{:S(2)}, u32[]{:S(2)}) collective-permute-start(f32[192,128]{1,0:T(8,128)S(1)} %get-tuple-element.24), channel_id=1, source_target_pairs={{0,8},{4,20},{8,0},{12,28},{16,24},{20,4},{24,16},{28,12},{1,9},{5... | collective-permute-start | bytes 294920 | tf_op jit(solution)/shard_map/ppermute | solution.py:208
  6.4 1.3 %collective-permute-start.4 = (f32[192,128]{1,0:T(8,128)S(1)}, f32[192,128]{1,0:T(8,128)S(1)}, u32[]{:S(2)}, u32[]{:S(2)}) collective-permute-start(f32[192,128]{1,0:T(8,128)S(1)} %get-tuple-element.22.refs_4_), channel_id=1, source_target_pairs={{0,16},{4,12},{8,24},{12,4},{16,0},{20,28},{24,8},{28,20},{1,17},{... | collective-permute-start | bytes 294920 | tf_op jit(solution)/shard_map/ppermute | solution.py:208
  7.8 1.4 %fetch.1 = (bf16[2,512,256]{2,1,0:T(8,128)(2,1)S(1)}, bf16[2,2,256,256]{3,2,1,0:T(8,128)(2,1)S(1)}, bf16[2,256,256]{2,1,0:T(8,128)(2,1)S(1)}, f32[256,256]{1,0:T(8,128)S(1)}) custom-call(bf16[2,512,256]{2,1,0:T(8,128)(2,1)} %constant.8.clone.refs_0_, bf16[2,2,256,256]{3,2,1,0:T(8,128)(2,1)} %constant.9.clone.refs_1_, ...), custom_call_target="tpu_custom_call" | custom-call | tf_op jit(solution)/shard_map/fetch/pallas_call | solution.py:191
  9.1 0.0 copy-start
  9.2 0.8 %copy-done = bf16[2,2,256,256]{3,2,1,0:T(8,128)(2,1)} copy-done((bf16[2,2,256,256]{3,2,1,0:T(8,128)(2,1)}, bf16[2,2,256,256]{3,2,1,0:T(8,128)(2,1)S(1)}, u32[]{:S(2)}) %copy-start) | copy-done | bytes 524312
  9.9 0.0 collective-permute-done.1.x.refs_2_
  9.9 0.0 copy-start.1
  10.0 0.1 collective-permute-start.2
  10.0 1.2 %collective-permute-done.2.refs_3_ = f32[96,128]{1,0:T(8,128)S(1)} collective-permute-done((f32[96,128]{1,0:T(8,128)S(1)}, f32[96,128]{1,0:T(8,128)S(1)}, u32[]{:S(2)}, u32[]{:S(2)}) %collective-permute-start.2) | collective-permute-done | bytes 49184 | tf_op jit(solution)/shard_map/ppermute | solution.py:208
  11.3 0.3 %collective-permute-done.3.refs_4_ = f32[192,128]{1,0:T(8,128)S(1)} collective-permute-done((f32[192,128]{1,0:T(8,128)S(1)}, f32[192,128]{1,0:T(8,128)S(1)}, u32[]{:S(2)}, u32[]{:S(2)}) %collective-permute-start.3) | collective-permute-done | bytes 98336 | tf_op jit(solution)/shard_map/ppermute | solution.py:208
  11.6 0.0 collective-permute-done.4.refs_5_
  11.6 0.0 copy-done.1
  11.6 1.5 %transform.1 = (f32[64,128]{1,0:T(8,128)S(1)}, f32[128,128]{1,0:T(8,128)S(1)}, f32[192,128]{1,0:T(8,128)S(1)}, f32[128,128]{1,0:T(8,128)S(1)}) custom-call(f32[96,128]{1,0:T(8,128)S(1)} %get-tuple-element.18.refs_0_, f32[288,128]{1,0:T(8,128)S(1)} %collective-permute-done.aside.refs_1_, f32[192,128]{1,0:T(8,128)S(1)} %collective-permute-done.1.x.refs_2_, ...), custom_call_target="tpu_custom_call" | custom-call | tf_op jit(solution)/shard_map/transform/pallas_call | solution.py:191
  13.1 0.1 collective-permute-start.5
  13.2 2.4 %collective-permute-start.6 = (f32[128,128]{1,0:T(8,128)S(1)}, f32[128,128]{1,0:T(8,128)S(1)}, u32[]{:S(2)}, u32[]{:S(2)}) collective-permute-start(f32[128,128]{1,0:T(8,128)S(1)} %get-tuple-element.30), channel_id=1, source_target_pairs={{0,24},{4,28},{8,16},{12,20},{16,8},{20,12},{24,0},{28,4},{1,25},{... | collective-permute-start | bytes 196616 | tf_op jit(solution)/shard_map/ppermute | solution.py:208
  15.6 0.0 collective-permute-done.5.aside.refs_1_
  15.6 0.6 %collective-permute-start.8 = (f32[128,128]{1,0:T(8,128)S(1)}, f32[128,128]{1,0:T(8,128)S(1)}, u32[]{:S(2)}, u32[]{:S(2)}) collective-permute-start(f32[128,128]{1,0:T(8,128)S(1)} %get-tuple-element.32), channel_id=1, source_target_pairs={{0,8},{4,20},{8,0},{12,28},{16,24},{20,4},{24,16},{28,12},{1,9},{5... | collective-permute-start | bytes 196616 | tf_op jit(solution)/shard_map/ppermute | solution.py:208
  16.2 1.2 %collective-permute-start.9 = (f32[128,128]{1,0:T(8,128)S(1)}, f32[128,128]{1,0:T(8,128)S(1)}, u32[]{:S(2)}, u32[]{:S(2)}) collective-permute-start(f32[128,128]{1,0:T(8,128)S(1)} %get-tuple-element.33), channel_id=1, source_target_pairs={{0,16},{4,12},{8,24},{12,4},{16,0},{20,28},{24,8},{28,20},{1,17},{... | collective-permute-start | bytes 196616 | tf_op jit(solution)/shard_map/ppermute | solution.py:208
  17.5 1.1 %collective-permute-done.6.x.refs_2_ = f32[128,128]{1,0:T(8,128)S(1)} collective-permute-done((f32[128,128]{1,0:T(8,128)S(1)}, f32[128,128]{1,0:T(8,128)S(1)}, u32[]{:S(2)}, u32[]{:S(2)}) %collective-permute-start.6) | collective-permute-done | bytes 65568 | tf_op jit(solution)/shard_map/ppermute | solution.py:208
  18.6 0.0 collective-permute-start.7
  18.6 1.2 %collective-permute-done.7.refs_3_ = f32[64,128]{1,0:T(8,128)S(1)} collective-permute-done((f32[64,128]{1,0:T(8,128)S(1)}, f32[64,128]{1,0:T(8,128)S(1)}, u32[]{:S(2)}, u32[]{:S(2)}) %collective-permute-start.7) | collective-permute-done | bytes 32800 | tf_op jit(solution)/shard_map/ppermute | solution.py:208
  19.8 0.4 %collective-permute-done.8.refs_4_ = f32[128,128]{1,0:T(8,128)S(1)} collective-permute-done((f32[128,128]{1,0:T(8,128)S(1)}, f32[128,128]{1,0:T(8,128)S(1)}, u32[]{:S(2)}, u32[]{:S(2)}) %collective-permute-start.8) | collective-permute-done | bytes 65568 | tf_op jit(solution)/shard_map/ppermute | solution.py:208
  20.1 0.4 %collective-permute-done.9.refs_5_ = f32[128,128]{1,0:T(8,128)S(1)} collective-permute-done((f32[128,128]{1,0:T(8,128)S(1)}, f32[128,128]{1,0:T(8,128)S(1)}, u32[]{:S(2)}, u32[]{:S(2)}) %collective-permute-start.9) | collective-permute-done | bytes 65568 | tf_op jit(solution)/shard_map/ppermute | solution.py:208
  20.5 0.8 %gather.1 = (f32[8,4096]{1,0:T(8,128)}, f32[8,4096]{1,0:T(8,128)}) custom-call(f32[64,128]{1,0:T(8,128)S(1)} %get-tuple-element.28.refs_0_, f32[192,128]{1,0:T(8,128)S(1)} %collective-permute-done.5.aside.refs_1_, f32[128,128]{1,0:T(8,128)S(1)} %collective-permute-done.6.x.refs_2_, f32[64,128]{1,0:T(8,128)S(1)} %collective-permute-done.7.refs_3_, ...), custom_call_target="tpu_custom_call" | custom-call | tf_op jit(solution)/shard_map/gather/pallas_call | solution.py:191
  (4 shorter events, 0.0 us)
Async XLA Ops:
  1.8 4.0 %collective-permute-start = (f32[288,128]{1,0:T(8,128)S(1)}, f32[288,128]{1,0:T(8,128)S(1)}, u32[]{:S(2)}, u32[]{:S(2)}) collective-permute-start(f32[288,128]{1,0:T(8,128)S(1)} %get-tuple-element.19), channel_id=1, source_target_pairs={{0,4},{4,0},{8,12},{12,8},{16,20},{20,16},{24,28},{28,24},{1,5},{5... | collective-permute-start | bytes 442376 | tf_op jit(solution)/shard_map/ppermute | solution.py:208
  2.3 7.6 %collective-permute-start.1 = (f32[192,128]{1,0:T(8,128)S(1)}, f32[192,128]{1,0:T(8,128)S(1)}, u32[]{:S(2)}, u32[]{:S(2)}) collective-permute-start(f32[192,128]{1,0:T(8,128)S(1)} %get-tuple-element.20), channel_id=1, source_target_pairs={{0,24},{4,28},{8,16},{12,20},{16,8},{20,12},{24,0},{28,4},{1,25},{... | collective-permute-start | bytes 294920 | tf_op jit(solution)/shard_map/ppermute | solution.py:208
  5.8 5.7 %collective-permute-start.3 = (f32[192,128]{1,0:T(8,128)S(1)}, f32[192,128]{1,0:T(8,128)S(1)}, u32[]{:S(2)}, u32[]{:S(2)}) collective-permute-start(f32[192,128]{1,0:T(8,128)S(1)} %get-tuple-element.24), channel_id=1, source_target_pairs={{0,8},{4,20},{8,0},{12,28},{16,24},{20,4},{24,16},{28,12},{1,9},{5... | collective-permute-start | bytes 294920 | tf_op jit(solution)/shard_map/ppermute | solution.py:208
  6.4 5.1 %collective-permute-start.4 = (f32[192,128]{1,0:T(8,128)S(1)}, f32[192,128]{1,0:T(8,128)S(1)}, u32[]{:S(2)}, u32[]{:S(2)}) collective-permute-start(f32[192,128]{1,0:T(8,128)S(1)} %get-tuple-element.22.refs_4_), channel_id=1, source_target_pairs={{0,16},{4,12},{8,24},{12,4},{16,0},{20,28},{24,8},{28,20},{1,17},{... | collective-permute-start | bytes 294920 | tf_op jit(solution)/shard_map/ppermute | solution.py:208
  9.1 0.8 %copy-start = (bf16[2,2,256,256]{3,2,1,0:T(8,128)(2,1)}, bf16[2,2,256,256]{3,2,1,0:T(8,128)(2,1)S(1)}, u32[]{:S(2)}) copy-start(bf16[2,2,256,256]{3,2,1,0:T(8,128)(2,1)S(1)} %get-tuple-element.25.refs_7_) | copy-start | bytes 1572868
  9.9 1.6 %copy-start.1 = (bf16[2,2,256,256]{3,2,1,0:T(8,128)(2,1)S(1)}, bf16[2,2,256,256]{3,2,1,0:T(8,128)(2,1)}, u32[]{:S(2)}) copy-start(bf16[2,2,256,256]{3,2,1,0:T(8,128)(2,1)} %copy-done) | copy-start | bytes 1572868
  10.0 1.3 %collective-permute-start.2 = (f32[96,128]{1,0:T(8,128)S(1)}, f32[96,128]{1,0:T(8,128)S(1)}, u32[]{:S(2)}, u32[]{:S(2)}) collective-permute-start(f32[96,128]{1,0:T(8,128)S(1)} %second_half.2), channel_id=1, source_target_pairs={{0,4},{4,0},{8,12},{12,8},{16,20},{20,16},{24,28},{28,24},{1,5},{5... | collective-permute-start | bytes 147464 | tf_op jit(solution)/shard_map/ppermute | solution.py:208
  13.1 2.5 %collective-permute-start.5 = (f32[192,128]{1,0:T(8,128)S(1)}, f32[192,128]{1,0:T(8,128)S(1)}, u32[]{:S(2)}, u32[]{:S(2)}) collective-permute-start(f32[192,128]{1,0:T(8,128)S(1)} %get-tuple-element.29), channel_id=1, source_target_pairs={{0,4},{4,0},{8,12},{12,8},{16,20},{20,16},{24,28},{28,24},{1,5},{5... | collective-permute-start | bytes 294920 | tf_op jit(solution)/shard_map/ppermute | solution.py:208
  13.2 5.4 %collective-permute-start.6 = (f32[128,128]{1,0:T(8,128)S(1)}, f32[128,128]{1,0:T(8,128)S(1)}, u32[]{:S(2)}, u32[]{:S(2)}) collective-permute-start(f32[128,128]{1,0:T(8,128)S(1)} %get-tuple-element.30), channel_id=1, source_target_pairs={{0,24},{4,28},{8,16},{12,20},{16,8},{20,12},{24,0},{28,4},{1,25},{... | collective-permute-start | bytes 196616 | tf_op jit(solution)/shard_map/ppermute | solution.py:208
  15.6 4.5 %collective-permute-start.8 = (f32[128,128]{1,0:T(8,128)S(1)}, f32[128,128]{1,0:T(8,128)S(1)}, u32[]{:S(2)}, u32[]{:S(2)}) collective-permute-start(f32[128,128]{1,0:T(8,128)S(1)} %get-tuple-element.32), channel_id=1, source_target_pairs={{0,8},{4,20},{8,0},{12,28},{16,24},{20,4},{24,16},{28,12},{1,9},{5... | collective-permute-start | bytes 196616 | tf_op jit(solution)/shard_map/ppermute | solution.py:208
  16.2 4.3 %collective-permute-start.9 = (f32[128,128]{1,0:T(8,128)S(1)}, f32[128,128]{1,0:T(8,128)S(1)}, u32[]{:S(2)}, u32[]{:S(2)}) collective-permute-start(f32[128,128]{1,0:T(8,128)S(1)} %get-tuple-element.33), channel_id=1, source_target_pairs={{0,16},{4,12},{8,24},{12,4},{16,0},{20,28},{24,8},{28,20},{1,17},{... | collective-permute-start | bytes 196616 | tf_op jit(solution)/shard_map/ppermute | solution.py:208
  18.6 1.2 %collective-permute-start.7 = (f32[64,128]{1,0:T(8,128)S(1)}, f32[64,128]{1,0:T(8,128)S(1)}, u32[]{:S(2)}, u32[]{:S(2)}) collective-permute-start(f32[64,128]{1,0:T(8,128)S(1)} %second_half.3), channel_id=1, source_target_pairs={{0,4},{4,0},{8,12},{12,8},{16,20},{20,16},{24,28},{28,24},{1,5},{5... | collective-permute-start | bytes 98312 | tf_op jit(solution)/shard_map/ppermute | solution.py:208

commit v4 on v3

--- a/solution.py
+++ b/solution.py
@@ -69,10 +69,6 @@
     return core, chip, chip ^ 3, chip ^ (1 + core), chip ^ (2 - core)
 
 
-def part(index, step):
-    return pl.ds(pl.multiple_of(index * step, step), step)
-
-
 def pack(pieces, own, far, aside, beside):
     core, chip, opposite, one, two = place()
     step = own.shape[0]
@@ -82,7 +78,7 @@
         (aside, 0, chip, other), (aside, 1, two, other), (aside, 2, one, other),
         (beside, 0, one, here), (beside, 1, two, here),
     ):
-        out[at * step:(at + 1) * step, :] = pieces[part(to_chip * 2 + to_core, step), :]
+        out[at * step:(at + 1) * step, :] = pieces[to_chip * 2 + to_core]
 
 
 def merge(beside, aside, first, second):
@@ -106,7 +102,7 @@
         (own, 0, chip, here), (aside, 0, chip, other), (far, 0, opposite, here), (far_other, 0, opposite, other),
         (first, 0, one, here), (first, 1, one, other), (second, 0, two, here), (second, 1, two, other),
     ):
-        held[part(from_chip * 2 + from_core, step), :] = ref[at * step:(at + 1) * step, :]
+        held[from_chip * 2 + from_core] = ref[at * step:(at + 1) * step, :]
 
 
 def fetch(*refs):
@@ -123,29 +119,33 @@
     channels, block = signals[0].shape
     chunks = block // LANES
     width = block // LOADS
+
+    def at(load):
+        return pl.ds(load * width, width)
+
     copies = []
     for load in range(LOADS):
-        at = pl.ds(load * width, width)
         for i in range(3):
-            copies.append(pltpu.make_async_copy(signals[i].at[:, at], near[i].at[:, at], arrived.at[load * 3 + i]))
+            ends = signals[i].at[:, at(load)], near[i].at[:, at(load)]
+            copies.append(pltpu.make_async_copy(*ends, arrived.at[load * 3 + i]))
             copies[-1].start()
     for load in range(LOADS):
         for i in range(3):
             copies[load * 3 + i].wait()
-            for j in range(load * chunks // LOADS, (load + 1) * chunks // LOADS):
-                held[pl.ds(i * chunks + j, channels, stride=3 * chunks), :] = near[i][:, pl.ds(j * LANES, LANES)]
+            rows = pl.ds(i * chunks + load * chunks // LOADS, chunks // LOADS)
+            held[:, rows, :] = near[i][:, at(load)].reshape(channels, chunks // LOADS, LANES)
     pack(held, *outs)
 
 
 def transform(*refs):
     got, (first, last, into, twiddle), outs, (held, y) = refs[:6], refs[6:10], refs[10:14], refs[14:]
     unpack(got, held)
-    n = held.shape[0] // got[0].shape[0]
-    chunks = got[0].shape[0] // 3
+    n = held.shape[0]
+    chunks = held.shape[1] // 3
     rows = n * chunks
     m = rows // PARTS
-    pieces = held[...].reshape(n, 3, chunks, LANES)
-    signals = split(jnp.concatenate([pieces[:, i].reshape(rows, LANES) for i in range(3)], axis=1))
+    whole = [held[:, i * chunks:(i + 1) * chunks, :].reshape(rows, LANES) for i in range(3)]
+    signals = split(jnp.concatenate(whole, axis=1))
     turns = [lanes_of(twiddle, q, m) for q in range(PARTS)]
     outer = [dot_left(first[0, 2 * m * q:2 * m * (q + 1)], first[1, 2 * m * q:2 * m * (q + 1)], signals) for q in range(PARTS)]
     spectra = []
@@ -171,18 +171,18 @@
         out += dot_left(last[0, joined], last[1, joined], split(jnp.concatenate(real + imag, axis=0)))
     for d in range(n):
         for i in range(2):
-            y[(d * 2 + i) * chunks:(d * 2 + i + 1) * chunks, :] = out[d * chunks:(d + 1) * chunks, i * LANES:(i + 1) * LANES]
+            y[d, i * chunks:(i + 1) * chunks, :] = out[d * chunks:(d + 1) * chunks, i * LANES:(i + 1) * LANES]
     pack(y, *outs)
 
 
 def gather(*refs):
-    *got, a, b, held = refs
+    got, (a, b, held) = refs[:6], refs[6:]
     unpack(got, held)
     channels, block = a.shape
     chunks = block // LANES
     for i, ref in enumerate((a, b)):
-        for j in range(chunks):
-            ref[:, pl.ds(j * LANES, LANES)] = held[pl.ds(i * chunks + j, channels, stride=2 * chunks), :]
+        for j in range(0, chunks, 8):
+            ref[:, pl.ds(j * LANES, 8 * LANES)] = held[:, pl.ds(i * chunks + j, 8), :].reshape(channels, 8 * LANES)
 
 
 def call(body, ins, outs, scratch=(), far_in=0, near_out=True):
@@ -226,10 +226,10 @@
         return call(fetch, [*held, after], [(t.shape, t.dtype) for t in held], [pltpu.SemaphoreType.DMA((len(held),))], len(held))
 
     near = [pltpu.VMEM((channels, block), kind)] * 3
-    near += [pltpu.VMEM((channels * 3 * chunks, LANES), kind), pltpu.SemaphoreType.DMA((3 * LOADS,))]
+    near += [pltpu.VMEM((channels, 3 * chunks, LANES), kind), pltpu.SemaphoreType.DMA((3 * LOADS,))]
     sent = call(spread, [inputs, grads, response], sizes(3), near, 3)
     got = exchange(*sent, meanwhile=bring)
-    near = [pltpu.VMEM((n * arrays * chunks, LANES), kind) for arrays in (3, 2)]
+    near = [pltpu.VMEM((n, arrays * chunks, LANES), kind) for arrays in (3, 2)]
     got = exchange(*call(transform, got, sizes(2), near))
     return call(gather, got, [((channels, block), kind)] * 2, near[1:], near_out=False)
 

time: 21.6 us -> 21.4 us (level)
  no operation moved by 1% of the time
where the time goes in v4:
time: 21.4 us; the launch traced here: 21.2 us
  starting transfers between devices  10.4 us (49%)
  Pallas kernels  4.73 us (22%)
  waiting for transfers between devices  4.57 us (21%)
  local copies, waits for them, and re-layouts  0.79 us (4%)
  between operations  0.7 us (3%)
    ppermute x10, starting transfers between devices, swap(): lax.ppermute(x, 'context', [(i, i ^ (odd if i % 2 else even)) for i in ra...  10.4 us
    pallas_call x8, Pallas kernels, call(): pl.pallas_call(body, out_shape=[kind(shape, dtype) for shape, dtype in ou...  4.73 us
    ppermute x10, waiting for transfers between devices, swap(): lax.ppermute(x, 'context', [(i, i ^ (odd if i % 2 else even)) for i in ra...  4.57 us
    unnamed x4, local copies, waits for them, and re-layouts  0.79 us
  transfers between devices with their start and end apart: 10, of which 6 were waited for; matrix products, arithmetic and copies ran while one was open for 0% of the time, Pallas kernels for 7%

profile of v4, /device:TPU:0, one launch (start us, length us, event | category | flops | bytes accessed | tf_op | source)
XLA Modules:
  0.0 21.2 jit_solution(9739778963129822979)
XLA Ops:
  0.6 1.1 %spread.1 = (f32[96,128]{1,0:T(8,128)S(1)}, f32[192,128]{1,0:T(8,128)S(1)}, f32[288,128]{1,0:T(8,128)S(1)}, f32[192,128]{1,0:T(8,128)S(1)}) custom-call(f32[8,4096]{1,0:T(8,128)} %refs_0_.2, f32[8,4096]{1,0:T(8,128)} %refs_1_.2, f32[8,4096]{1,0:T(8,128)} %refs_2_.2), custom_call_target="tpu_custom_call" | custom-call | tf_op jit(solution)/shard_map/spread/pallas_call | solution.py:191
  1.7 0.5 %collective-permute-start = (f32[288,128]{1,0:T(8,128)S(1)}, f32[288,128]{1,0:T(8,128)S(1)}, u32[]{:S(2)}, u32[]{:S(2)}) collective-permute-start(f32[288,128]{1,0:T(8,128)S(1)} %get-tuple-element.19), channel_id=1, source_target_pairs={{0,4},{4,0},{8,12},{12,8},{16,20},{20,16},{24,28},{28,24},{1,5},{5... | collective-permute-start | bytes 442376 | tf_op jit(solution)/shard_map/ppermute | solution.py:208
  2.2 3.5 %collective-permute-start.1 = (f32[192,128]{1,0:T(8,128)S(1)}, f32[192,128]{1,0:T(8,128)S(1)}, u32[]{:S(2)}, u32[]{:S(2)}) collective-permute-start(f32[192,128]{1,0:T(8,128)S(1)} %get-tuple-element.20), channel_id=1, source_target_pairs={{0,24},{4,28},{8,16},{12,20},{16,8},{20,12},{24,0},{28,4},{1,25},{... | collective-permute-start | bytes 294920 | tf_op jit(solution)/shard_map/ppermute | solution.py:208
  5.8 0.0 collective-permute-done.aside.refs_1_
  5.8 0.6 %collective-permute-start.3 = (f32[192,128]{1,0:T(8,128)S(1)}, f32[192,128]{1,0:T(8,128)S(1)}, u32[]{:S(2)}, u32[]{:S(2)}) collective-permute-start(f32[192,128]{1,0:T(8,128)S(1)} %get-tuple-element.24), channel_id=1, source_target_pairs={{0,8},{4,20},{8,0},{12,28},{16,24},{20,4},{24,16},{28,12},{1,9},{5... | collective-permute-start | bytes 294920 | tf_op jit(solution)/shard_map/ppermute | solution.py:208
  6.4 1.3 %collective-permute-start.4 = (f32[192,128]{1,0:T(8,128)S(1)}, f32[192,128]{1,0:T(8,128)S(1)}, u32[]{:S(2)}, u32[]{:S(2)}) collective-permute-start(f32[192,128]{1,0:T(8,128)S(1)} %get-tuple-element.22.refs_4_), channel_id=1, source_target_pairs={{0,16},{4,12},{8,24},{12,4},{16,0},{20,28},{24,8},{28,20},{1,17},{... | collective-permute-start | bytes 294920 | tf_op jit(solution)/shard_map/ppermute | solution.py:208
  7.7 1.4 %fetch.1 = (bf16[2,512,256]{2,1,0:T(8,128)(2,1)S(1)}, bf16[2,2,256,256]{3,2,1,0:T(8,128)(2,1)S(1)}, bf16[2,256,256]{2,1,0:T(8,128)(2,1)S(1)}, f32[256,256]{1,0:T(8,128)S(1)}) custom-call(bf16[2,512,256]{2,1,0:T(8,128)(2,1)} %constant.8.clone.refs_0_, bf16[2,2,256,256]{3,2,1,0:T(8,128)(2,1)} %constant.9.clone.refs_1_, ...), custom_call_target="tpu_custom_call" | custom-call | tf_op jit(solution)/shard_map/fetch/pallas_call | solution.py:191
  9.1 0.0 copy-start
  9.1 0.8 %copy-done = bf16[2,2,256,256]{3,2,1,0:T(8,128)(2,1)} copy-done((bf16[2,2,256,256]{3,2,1,0:T(8,128)(2,1)}, bf16[2,2,256,256]{3,2,1,0:T(8,128)(2,1)S(1)}, u32[]{:S(2)}) %copy-start) | copy-done | bytes 524312
  9.9 0.0 collective-permute-done.1.x.refs_2_
  9.9 0.0 copy-start.1
  9.9 0.1 collective-permute-start.2
  10.0 1.2 %collective-permute-done.2.refs_3_ = f32[96,128]{1,0:T(8,128)S(1)} collective-permute-done((f32[96,128]{1,0:T(8,128)S(1)}, f32[96,128]{1,0:T(8,128)S(1)}, u32[]{:S(2)}, u32[]{:S(2)}) %collective-permute-start.2) | collective-permute-done | bytes 49184 | tf_op jit(solution)/shard_map/ppermute | solution.py:208
  11.2 0.3 %collective-permute-done.3.refs_4_ = f32[192,128]{1,0:T(8,128)S(1)} collective-permute-done((f32[192,128]{1,0:T(8,128)S(1)}, f32[192,128]{1,0:T(8,128)S(1)}, u32[]{:S(2)}, u32[]{:S(2)}) %collective-permute-start.3) | collective-permute-done | bytes 98336 | tf_op jit(solution)/shard_map/ppermute | solution.py:208
  11.5 0.0 collective-permute-done.4.refs_5_
  11.5 0.0 copy-done.1
  11.5 1.5 %transform.1 = (f32[64,128]{1,0:T(8,128)S(1)}, f32[128,128]{1,0:T(8,128)S(1)}, f32[192,128]{1,0:T(8,128)S(1)}, f32[128,128]{1,0:T(8,128)S(1)}) custom-call(f32[96,128]{1,0:T(8,128)S(1)} %get-tuple-element.18.refs_0_, f32[288,128]{1,0:T(8,128)S(1)} %collective-permute-done.aside.refs_1_, f32[192,128]{1,0:T(8,128)S(1)} %collective-permute-done.1.x.refs_2_, ...), custom_call_target="tpu_custom_call" | custom-call | tf_op jit(solution)/shard_map/transform/pallas_call | solution.py:191
  13.0 0.1 collective-permute-start.5
  13.1 2.5 %collective-permute-start.6 = (f32[128,128]{1,0:T(8,128)S(1)}, f32[128,128]{1,0:T(8,128)S(1)}, u32[]{:S(2)}, u32[]{:S(2)}) collective-permute-start(f32[128,128]{1,0:T(8,128)S(1)} %get-tuple-element.30), channel_id=1, source_target_pairs={{0,24},{4,28},{8,16},{12,20},{16,8},{20,12},{24,0},{28,4},{1,25},{... | collective-permute-start | bytes 196616 | tf_op jit(solution)/shard_map/ppermute | solution.py:208
  15.5 0.0 collective-permute-done.5.aside.refs_1_
  15.6 0.6 %collective-permute-start.8 = (f32[128,128]{1,0:T(8,128)S(1)}, f32[128,128]{1,0:T(8,128)S(1)}, u32[]{:S(2)}, u32[]{:S(2)}) collective-permute-start(f32[128,128]{1,0:T(8,128)S(1)} %get-tuple-element.32), channel_id=1, source_target_pairs={{0,8},{4,20},{8,0},{12,28},{16,24},{20,4},{24,16},{28,12},{1,9},{5... | collective-permute-start | bytes 196616 | tf_op jit(solution)/shard_map/ppermute | solution.py:208
  16.2 1.2 %collective-permute-start.9 = (f32[128,128]{1,0:T(8,128)S(1)}, f32[128,128]{1,0:T(8,128)S(1)}, u32[]{:S(2)}, u32[]{:S(2)}) collective-permute-start(f32[128,128]{1,0:T(8,128)S(1)} %get-tuple-element.33), channel_id=1, source_target_pairs={{0,16},{4,12},{8,24},{12,4},{16,0},{20,28},{24,8},{28,20},{1,17},{... | collective-permute-start | bytes 196616 | tf_op jit(solution)/shard_map/ppermute | solution.py:208
  17.4 1.1 %collective-permute-done.6.x.refs_2_ = f32[128,128]{1,0:T(8,128)S(1)} collective-permute-done((f32[128,128]{1,0:T(8,128)S(1)}, f32[128,128]{1,0:T(8,128)S(1)}, u32[]{:S(2)}, u32[]{:S(2)}) %collective-permute-start.6) | collective-permute-done | bytes 65568 | tf_op jit(solution)/shard_map/ppermute | solution.py:208
  18.5 0.0 collective-permute-start.7
  18.5 1.2 %collective-permute-done.7.refs_3_ = f32[64,128]{1,0:T(8,128)S(1)} collective-permute-done((f32[64,128]{1,0:T(8,128)S(1)}, f32[64,128]{1,0:T(8,128)S(1)}, u32[]{:S(2)}, u32[]{:S(2)}) %collective-permute-start.7) | collective-permute-done | bytes 32800 | tf_op jit(solution)/shard_map/ppermute | solution.py:208
  19.7 0.4 %collective-permute-done.8.refs_4_ = f32[128,128]{1,0:T(8,128)S(1)} collective-permute-done((f32[128,128]{1,0:T(8,128)S(1)}, f32[128,128]{1,0:T(8,128)S(1)}, u32[]{:S(2)}, u32[]{:S(2)}) %collective-permute-start.8) | collective-permute-done | bytes 65568 | tf_op jit(solution)/shard_map/ppermute | solution.py:208
  20.1 0.4 %collective-permute-done.9.refs_5_ = f32[128,128]{1,0:T(8,128)S(1)} collective-permute-done((f32[128,128]{1,0:T(8,128)S(1)}, f32[128,128]{1,0:T(8,128)S(1)}, u32[]{:S(2)}, u32[]{:S(2)}) %collective-permute-start.9) | collective-permute-done | bytes 65568 | tf_op jit(solution)/shard_map/ppermute | solution.py:208
  20.4 0.8 %gather.1 = (f32[8,4096]{1,0:T(8,128)}, f32[8,4096]{1,0:T(8,128)}) custom-call(f32[64,128]{1,0:T(8,128)S(1)} %get-tuple-element.28.refs_0_, f32[192,128]{1,0:T(8,128)S(1)} %collective-permute-done.5.aside.refs_1_, f32[128,128]{1,0:T(8,128)S(1)} %collective-permute-done.6.x.refs_2_, f32[64,128]{1,0:T(8,128)S(1)} %collective-permute-done.7.refs_3_, ...), custom_call_target="tpu_custom_call" | custom-call | tf_op jit(solution)/shard_map/gather/pallas_call | solution.py:191
  (4 shorter events, 0.0 us)
Async XLA Ops:
  1.7 4.0 %collective-permute-start = (f32[288,128]{1,0:T(8,128)S(1)}, f32[288,128]{1,0:T(8,128)S(1)}, u32[]{:S(2)}, u32[]{:S(2)}) collective-permute-start(f32[288,128]{1,0:T(8,128)S(1)} %get-tuple-element.19), channel_id=1, source_target_pairs={{0,4},{4,0},{8,12},{12,8},{16,20},{20,16},{24,28},{28,24},{1,5},{5... | collective-permute-start | bytes 442376 | tf_op jit(solution)/shard_map/ppermute | solution.py:208
  2.2 7.6 %collective-permute-start.1 = (f32[192,128]{1,0:T(8,128)S(1)}, f32[192,128]{1,0:T(8,128)S(1)}, u32[]{:S(2)}, u32[]{:S(2)}) collective-permute-start(f32[192,128]{1,0:T(8,128)S(1)} %get-tuple-element.20), channel_id=1, source_target_pairs={{0,24},{4,28},{8,16},{12,20},{16,8},{20,12},{24,0},{28,4},{1,25},{... | collective-permute-start | bytes 294920 | tf_op jit(solution)/shard_map/ppermute | solution.py:208
  5.8 5.7 %collective-permute-start.3 = (f32[192,128]{1,0:T(8,128)S(1)}, f32[192,128]{1,0:T(8,128)S(1)}, u32[]{:S(2)}, u32[]{:S(2)}) collective-permute-start(f32[192,128]{1,0:T(8,128)S(1)} %get-tuple-element.24), channel_id=1, source_target_pairs={{0,8},{4,20},{8,0},{12,28},{16,24},{20,4},{24,16},{28,12},{1,9},{5... | collective-permute-start | bytes 294920 | tf_op jit(solution)/shard_map/ppermute | solution.py:208
  6.4 5.1 %collective-permute-start.4 = (f32[192,128]{1,0:T(8,128)S(1)}, f32[192,128]{1,0:T(8,128)S(1)}, u32[]{:S(2)}, u32[]{:S(2)}) collective-permute-start(f32[192,128]{1,0:T(8,128)S(1)} %get-tuple-element.22.refs_4_), channel_id=1, source_target_pairs={{0,16},{4,12},{8,24},{12,4},{16,0},{20,28},{24,8},{28,20},{1,17},{... | collective-permute-start | bytes 294920 | tf_op jit(solution)/shard_map/ppermute | solution.py:208
  9.1 0.8 %copy-start = (bf16[2,2,256,256]{3,2,1,0:T(8,128)(2,1)}, bf16[2,2,256,256]{3,2,1,0:T(8,128)(2,1)S(1)}, u32[]{:S(2)}) copy-start(bf16[2,2,256,256]{3,2,1,0:T(8,128)(2,1)S(1)} %get-tuple-element.25.refs_7_) | copy-start | bytes 1572868
  9.9 1.6 %copy-start.1 = (bf16[2,2,256,256]{3,2,1,0:T(8,128)(2,1)S(1)}, bf16[2,2,256,256]{3,2,1,0:T(8,128)(2,1)}, u32[]{:S(2)}) copy-start(bf16[2,2,256,256]{3,2,1,0:T(8,128)(2,1)} %copy-done) | copy-start | bytes 1572868
  9.9 1.3 %collective-permute-start.2 = (f32[96,128]{1,0:T(8,128)S(1)}, f32[96,128]{1,0:T(8,128)S(1)}, u32[]{:S(2)}, u32[]{:S(2)}) collective-permute-start(f32[96,128]{1,0:T(8,128)S(1)} %second_half.2), channel_id=1, source_target_pairs={{0,4},{4,0},{8,12},{12,8},{16,20},{20,16},{24,28},{28,24},{1,5},{5... | collective-permute-start | bytes 147464 | tf_op jit(solution)/shard_map/ppermute | solution.py:208
  13.0 2.5 %collective-permute-start.5 = (f32[192,128]{1,0:T(8,128)S(1)}, f32[192,128]{1,0:T(8,128)S(1)}, u32[]{:S(2)}, u32[]{:S(2)}) collective-permute-start(f32[192,128]{1,0:T(8,128)S(1)} %get-tuple-element.29), channel_id=1, source_target_pairs={{0,4},{4,0},{8,12},{12,8},{16,20},{20,16},{24,28},{28,24},{1,5},{5... | collective-permute-start | bytes 294920 | tf_op jit(solution)/shard_map/ppermute | solution.py:208
  13.1 5.4 %collective-permute-start.6 = (f32[128,128]{1,0:T(8,128)S(1)}, f32[128,128]{1,0:T(8,128)S(1)}, u32[]{:S(2)}, u32[]{:S(2)}) collective-permute-start(f32[128,128]{1,0:T(8,128)S(1)} %get-tuple-element.30), channel_id=1, source_target_pairs={{0,24},{4,28},{8,16},{12,20},{16,8},{20,12},{24,0},{28,4},{1,25},{... | collective-permute-start | bytes 196616 | tf_op jit(solution)/shard_map/ppermute | solution.py:208
  15.6 4.5 %collective-permute-start.8 = (f32[128,128]{1,0:T(8,128)S(1)}, f32[128,128]{1,0:T(8,128)S(1)}, u32[]{:S(2)}, u32[]{:S(2)}) collective-permute-start(f32[128,128]{1,0:T(8,128)S(1)} %get-tuple-element.32), channel_id=1, source_target_pairs={{0,8},{4,20},{8,0},{12,28},{16,24},{20,4},{24,16},{28,12},{1,9},{5... | collective-permute-start | bytes 196616 | tf_op jit(solution)/shard_map/ppermute | solution.py:208
  16.2 4.3 %collective-permute-start.9 = (f32[128,128]{1,0:T(8,128)S(1)}, f32[128,128]{1,0:T(8,128)S(1)}, u32[]{:S(2)}, u32[]{:S(2)}) collective-permute-start(f32[128,128]{1,0:T(8,128)S(1)} %get-tuple-element.33), channel_id=1, source_target_pairs={{0,16},{4,12},{8,24},{12,4},{16,0},{20,28},{24,8},{28,20},{1,17},{... | collective-permute-start | bytes 196616 | tf_op jit(solution)/shard_map/ppermute | solution.py:208
  18.5 1.2 %collective-permute-start.7 = (f32[64,128]{1,0:T(8,128)S(1)}, f32[64,128]{1,0:T(8,128)S(1)}, u32[]{:S(2)}, u32[]{:S(2)}) collective-permute-start(f32[64,128]{1,0:T(8,128)S(1)} %second_half.3), channel_id=1, source_target_pairs={{0,4},{4,0},{8,12},{12,8},{16,20},{20,16},{24,28},{28,24},{1,5},{5... | collective-permute-start | bytes 98312 | tf_op jit(solution)/shard_map/ppermute | solution.py:208

commit v5 on v4

--- a/solution.py
+++ b/solution.py
@@ -12,6 +12,7 @@
 LANES = 128
 BF = jnp.bfloat16
 PARTS, JOINED, LOADS = 4, 2, 4
+PLANS = ((7, 7), (3, 3), (5, 5)), ((7, 7), (3, 3), (5, 5))
 
 
 def halves(table):
@@ -63,22 +64,27 @@
     return x[i * m:(i + 1) * m, :LANES], x[i * m:(i + 1) * m, LANES:]
 
 
-def place():
+def route(plan):
     me = lax.axis_index("context")
-    chip, core = me // 2, me % 2
-    return core, chip, chip ^ 3, chip ^ (1 + core), chip ^ (2 - core)
-
-
-def pack(pieces, own, far, aside, beside):
-    core, chip, opposite, one, two = place()
+    core = me % 2
+    to, from_ = [], []
+    for even, odd in plan:
+        mine, others = even + core * (odd - even), odd + core * (even - odd)
+        to.append((me ^ mine, me ^ 1 ^ others))
+        back, backs = (mine, others) if even % 2 == 0 else (others, mine)
+        from_.append((me ^ back, me ^ 1 ^ backs))
+    return me, to, from_
+
+
+def pack(plan, pieces, own, far, aside, beside):
+    me, ((far_to, _), (first_to, first_aside), (second_to, second_aside)), _ = route(plan)
     step = own.shape[0]
-    here, other = core, 1 - core
-    for out, at, to_chip, to_core in (
-        (own, 0, chip, here), (far, 0, opposite, here), (far, 1, opposite, other),
-        (aside, 0, chip, other), (aside, 1, two, other), (aside, 2, one, other),
-        (beside, 0, one, here), (beside, 1, two, here),
+    for out, at, device in (
+        (own, 0, me), (far, 0, far_to), (far, 1, far_to ^ 1),
+        (aside, 0, me ^ 1), (aside, 1, first_aside), (aside, 2, second_aside),
+        (beside, 0, first_to), (beside, 1, second_to),
     ):
-        out[at * step:(at + 1) * step, :] = pieces[to_chip * 2 + to_core]
+        out[at * step:(at + 1) * step, :] = pieces[device]
 
 
 def merge(beside, aside, first, second):
@@ -93,16 +99,15 @@
     out[...] = x[out.shape[0]:, :]
 
 
-def unpack(got, held):
-    core, chip, opposite, one, two = place()
+def unpack(plan, got, held):
+    me, _, ((far_from, far_others), (first_from, _), (second_from, _)) = route(plan)
     own, aside, far, far_other, first, second = got
     step = own.shape[0]
-    here, other = core, 1 - core
-    for ref, at, from_chip, from_core in (
-        (own, 0, chip, here), (aside, 0, chip, other), (far, 0, opposite, here), (far_other, 0, opposite, other),
-        (first, 0, one, here), (first, 1, one, other), (second, 0, two, here), (second, 1, two, other),
+    for ref, at, device in (
+        (own, 0, me), (aside, 0, me ^ 1), (far, 0, far_from), (far_other, 0, far_others),
+        (first, 0, first_from), (first, 1, first_from ^ 1), (second, 0, second_from), (second, 1, second_from ^ 1),
     ):
-        held[from_chip * 2 + from_core] = ref[at * step:(at + 1) * step, :]
+        held[device] = ref[at * step:(at + 1) * step, :]
 
 
 def fetch(*refs):
@@ -134,12 +139,12 @@
             copies[load * 3 + i].wait()
             rows = pl.ds(i * chunks + load * chunks // LOADS, chunks // LOADS)
             held[:, rows, :] = near[i][:, at(load)].reshape(channels, chunks // LOADS, LANES)
-    pack(held, *outs)
+    pack(PLANS[0], held, *outs)
 
 
 def transform(*refs):
     got, (first, last, into, twiddle), outs, (held, y) = refs[:6], refs[6:10], refs[10:14], refs[14:]
-    unpack(got, held)
+    unpack(PLANS[0], got, held)
     n = held.shape[0]
     chunks = held.shape[1] // 3
     rows = n * chunks
@@ -172,12 +177,12 @@
     for d in range(n):
         for i in range(2):
             y[d, i * chunks:(i + 1) * chunks, :] = out[d * chunks:(d + 1) * chunks, i * LANES:(i + 1) * LANES]
-    pack(y, *outs)
+    pack(PLANS[1], y, *outs)
 
 
 def gather(*refs):
     got, (a, b, held) = refs[:6], refs[6:]
-    unpack(got, held)
+    unpack(PLANS[1], got, held)
     channels, block = a.shape
     chunks = block // LANES
     for i, ref in enumerate((a, b)):
@@ -210,13 +215,13 @@
     def sizes(arrays):
         return [((u * arrays * chunks, LANES), kind) for u in (1, 2, 3, 2)]
 
-    def exchange(own, far, aside, beside, meanwhile=lambda x: []):
+    def exchange(plan, own, far, aside, beside, meanwhile=lambda x: []):
         step = own.shape[0]
         aside = swap(aside, 1, 1)
-        far = swap(far, 6, 6)
+        far = swap(far, *plan[0])
         first, second = call(merge, [beside, aside], [((2 * step, LANES), kind)] * 2)
         made = meanwhile(second)
-        first, second = swap(first, 2, 4), swap(second, 4, 2)
+        first, second = swap(first, *plan[1]), swap(second, *plan[2])
         (half,) = call(second_half, [far, *made[:1]], [((step, LANES), kind)])
         return [own, aside, far, swap(half, 1, 1), first, second, *made]
 
@@ -228,9 +233,9 @@
     near = [pltpu.VMEM((channels, block), kind)] * 3
     near += [pltpu.VMEM((channels, 3 * chunks, LANES), kind), pltpu.SemaphoreType.DMA((3 * LOADS,))]
     sent = call(spread, [inputs, grads, response], sizes(3), near, 3)
-    got = exchange(*sent, meanwhile=bring)
+    got = exchange(PLANS[0], *sent, meanwhile=bring)
     near = [pltpu.VMEM((n, arrays * chunks, LANES), kind) for arrays in (3, 2)]
-    got = exchange(*call(transform, got, sizes(2), near))
+    got = exchange(PLANS[1], *call(transform, got, sizes(2), near))
     return call(gather, got, [((channels, block), kind)] * 2, near[1:], near_out=False)
 
 

time: 21.4 us -> 20.6 us (0.963)
  waiting for transfers between devices: 4.57 us -> 3.67 us
    ppermute x10, waiting for transfers between devices: 4.57 us -> 3.67 us  [swap(): lax.ppermute(x, 'context', [(i, i ^ (odd if i % 2 else even)) for i in ra...]
  transfers between devices with their start and end apart: 10 -> 10, of which waited for: 6 -> 5; matrix products, arithmetic and copies ran while one was open for 0% -> 0% of each run, Pallas kernels for 7% -> 7%
where the time goes in v5:
time: 20.6 us; the launch traced here: 20.4 us
  starting transfers between devices  10.5 us (51%)
  Pallas kernels  4.73 us (23%)
  waiting for transfers between devices  3.67 us (18%)
  local copies, waits for them, and re-layouts  0.79 us (4%)
  between operations  0.69 us (3%)
    ppermute x10, starting transfers between devices, swap(): lax.ppermute(x, 'context', [(i, i ^ (odd if i % 2 else even)) for i in ra...  10.5 us
    pallas_call x8, Pallas kernels, call(): pl.pallas_call(body, out_shape=[kind(shape, dtype) for shape, dtype in ou...  4.73 us
    ppermute x10, waiting for transfers between devices, swap(): lax.ppermute(x, 'context', [(i, i ^ (odd if i % 2 else even)) for i in ra...  3.67 us
    unnamed x4, local copies, waits for them, and re-layouts  0.79 us
  transfers between devices with their start and end apart: 10, of which 5 were waited for; matrix products, arithmetic and copies ran while one was open for 0% of the time, Pallas kernels for 7%

profile of v5, /device:TPU:0, one launch (start us, length us, event | category | flops | bytes accessed | tf_op | source)
XLA Modules:
  0.0 20.4 jit_solution(362954913072912775)
XLA Ops:
  0.6 1.1 %spread.1 = (f32[96,128]{1,0:T(8,128)S(1)}, f32[192,128]{1,0:T(8,128)S(1)}, f32[288,128]{1,0:T(8,128)S(1)}, f32[192,128]{1,0:T(8,128)S(1)}) custom-call(f32[8,4096]{1,0:T(8,128)} %refs_0_.2, f32[8,4096]{1,0:T(8,128)} %refs_1_.2, f32[8,4096]{1,0:T(8,128)} %refs_2_.2), custom_call_target="tpu_custom_call" | custom-call | tf_op jit(solution)/shard_map/spread/pallas_call | solution.py:196
  1.7 0.5 %collective-permute-start = (f32[288,128]{1,0:T(8,128)S(1)}, f32[288,128]{1,0:T(8,128)S(1)}, u32[]{:S(2)}, u32[]{:S(2)}) collective-permute-start(f32[288,128]{1,0:T(8,128)S(1)} %get-tuple-element.19), channel_id=1, source_target_pairs={{0,4},{4,0},{8,12},{12,8},{16,20},{20,16},{24,28},{28,24},{1,5},{5... | collective-permute-start | bytes 442376 | tf_op jit(solution)/shard_map/ppermute | solution.py:213
  2.2 3.6 %collective-permute-start.1 = (f32[192,128]{1,0:T(8,128)S(1)}, f32[192,128]{1,0:T(8,128)S(1)}, u32[]{:S(2)}, u32[]{:S(2)}) collective-permute-start(f32[192,128]{1,0:T(8,128)S(1)} %get-tuple-element.20), channel_id=1, source_target_pairs={{0,28},{4,24},{8,20},{12,16},{16,12},{20,8},{24,4},{28,0},{1,29},{... | collective-permute-start | bytes 294920 | tf_op jit(solution)/shard_map/ppermute | solution.py:213
  5.8 0.0 collective-permute-done.aside.refs_1_
  5.8 0.3 %collective-permute-start.3 = (f32[192,128]{1,0:T(8,128)S(1)}, f32[192,128]{1,0:T(8,128)S(1)}, u32[]{:S(2)}, u32[]{:S(2)}) collective-permute-start(f32[192,128]{1,0:T(8,128)S(1)} %get-tuple-element.24), channel_id=1, source_target_pairs={{0,12},{4,8},{8,4},{12,0},{16,28},{20,24},{24,20},{28,16},{1,13},{... | collective-permute-start | bytes 294920 | tf_op jit(solution)/shard_map/ppermute | solution.py:213
  6.1 1.3 %collective-permute-start.4 = (f32[192,128]{1,0:T(8,128)S(1)}, f32[192,128]{1,0:T(8,128)S(1)}, u32[]{:S(2)}, u32[]{:S(2)}) collective-permute-start(f32[192,128]{1,0:T(8,128)S(1)} %get-tuple-element.22.refs_4_), channel_id=1, source_target_pairs={{0,20},{4,16},{8,28},{12,24},{16,4},{20,0},{24,12},{28,8},{1,21},{... | collective-permute-start | bytes 294920 | tf_op jit(solution)/shard_map/ppermute | solution.py:213
  7.4 1.4 %fetch.1 = (bf16[2,512,256]{2,1,0:T(8,128)(2,1)S(1)}, bf16[2,2,256,256]{3,2,1,0:T(8,128)(2,1)S(1)}, bf16[2,256,256]{2,1,0:T(8,128)(2,1)S(1)}, f32[256,256]{1,0:T(8,128)S(1)}) custom-call(bf16[2,512,256]{2,1,0:T(8,128)(2,1)} %constant.8.clone.refs_0_, bf16[2,2,256,256]{3,2,1,0:T(8,128)(2,1)} %constant.9.clone.refs_1_, ...), custom_call_target="tpu_custom_call" | custom-call | tf_op jit(solution)/shard_map/fetch/pallas_call | solution.py:196
  8.8 0.0 copy-start
  8.8 0.8 %copy-done = bf16[2,2,256,256]{3,2,1,0:T(8,128)(2,1)} copy-done((bf16[2,2,256,256]{3,2,1,0:T(8,128)(2,1)}, bf16[2,2,256,256]{3,2,1,0:T(8,128)(2,1)S(1)}, u32[]{:S(2)}) %copy-start) | copy-done | bytes 524312
  9.6 0.0 collective-permute-done.1.x.refs_2_
  9.6 0.0 copy-start.1
  9.6 0.2 %collective-permute-start.2 = (f32[96,128]{1,0:T(8,128)S(1)}, f32[96,128]{1,0:T(8,128)S(1)}, u32[]{:S(2)}, u32[]{:S(2)}) collective-permute-start(f32[96,128]{1,0:T(8,128)S(1)} %second_half.2), channel_id=1, source_target_pairs={{0,4},{4,0},{8,12},{12,8},{16,20},{20,16},{24,28},{28,24},{1,5},{5... | collective-permute-start | bytes 147464 | tf_op jit(solution)/shard_map/ppermute | solution.py:213
  9.8 1.1 %collective-permute-done.2.refs_3_ = f32[96,128]{1,0:T(8,128)S(1)} collective-permute-done((f32[96,128]{1,0:T(8,128)S(1)}, f32[96,128]{1,0:T(8,128)S(1)}, u32[]{:S(2)}, u32[]{:S(2)}) %collective-permute-start.2) | collective-permute-done | bytes 49184 | tf_op jit(solution)/shard_map/ppermute | solution.py:213
  10.9 0.1 collective-permute-done.3.refs_4_
  11.0 0.0 collective-permute-done.4.refs_5_
  11.0 0.0 copy-done.1
  11.0 1.5 %transform.1 = (f32[64,128]{1,0:T(8,128)S(1)}, f32[128,128]{1,0:T(8,128)S(1)}, f32[192,128]{1,0:T(8,128)S(1)}, f32[128,128]{1,0:T(8,128)S(1)}) custom-call(f32[96,128]{1,0:T(8,128)S(1)} %get-tuple-element.18.refs_0_, f32[288,128]{1,0:T(8,128)S(1)} %collective-permute-done.aside.refs_1_, f32[192,128]{1,0:T(8,128)S(1)} %collective-permute-done.1.x.refs_2_, ...), custom_call_target="tpu_custom_call" | custom-call | tf_op jit(solution)/shard_map/transform/pallas_call | solution.py:196
  12.5 0.4 %collective-permute-start.5 = (f32[192,128]{1,0:T(8,128)S(1)}, f32[192,128]{1,0:T(8,128)S(1)}, u32[]{:S(2)}, u32[]{:S(2)}) collective-permute-start(f32[192,128]{1,0:T(8,128)S(1)} %get-tuple-element.29), channel_id=1, source_target_pairs={{0,4},{4,0},{8,12},{12,8},{16,20},{20,16},{24,28},{28,24},{1,5},{5... | collective-permute-start | bytes 294920 | tf_op jit(solution)/shard_map/ppermute | solution.py:213
  12.8 2.6 %collective-permute-start.6 = (f32[128,128]{1,0:T(8,128)S(1)}, f32[128,128]{1,0:T(8,128)S(1)}, u32[]{:S(2)}, u32[]{:S(2)}) collective-permute-start(f32[128,128]{1,0:T(8,128)S(1)} %get-tuple-element.30), channel_id=1, source_target_pairs={{0,28},{4,24},{8,20},{12,16},{16,12},{20,8},{24,4},{28,0},{1,29},{... | collective-permute-start | bytes 196616 | tf_op jit(solution)/shard_map/ppermute | solution.py:213
  15.5 0.0 collective-permute-done.5.aside.refs_1_
  15.5 0.2 collective-permute-start.8
  15.7 1.4 %collective-permute-start.9 = (f32[128,128]{1,0:T(8,128)S(1)}, f32[128,128]{1,0:T(8,128)S(1)}, u32[]{:S(2)}, u32[]{:S(2)}) collective-permute-start(f32[128,128]{1,0:T(8,128)S(1)} %get-tuple-element.33), channel_id=1, source_target_pairs={{0,20},{4,16},{8,28},{12,24},{16,4},{20,0},{24,12},{28,8},{1,21},{... | collective-permute-start | bytes 196616 | tf_op jit(solution)/shard_map/ppermute | solution.py:213
  17.0 0.9 %collective-permute-done.6.x.refs_2_ = f32[128,128]{1,0:T(8,128)S(1)} collective-permute-done((f32[128,128]{1,0:T(8,128)S(1)}, f32[128,128]{1,0:T(8,128)S(1)}, u32[]{:S(2)}, u32[]{:S(2)}) %collective-permute-start.6) | collective-permute-done | bytes 65568 | tf_op jit(solution)/shard_map/ppermute | solution.py:213
  17.9 0.1 collective-permute-start.7
  18.0 1.1 %collective-permute-done.7.refs_3_ = f32[64,128]{1,0:T(8,128)S(1)} collective-permute-done((f32[64,128]{1,0:T(8,128)S(1)}, f32[64,128]{1,0:T(8,128)S(1)}, u32[]{:S(2)}, u32[]{:S(2)}) %collective-permute-start.7) | collective-permute-done | bytes 32800 | tf_op jit(solution)/shard_map/ppermute | solution.py:213
  19.1 0.5 %collective-permute-done.8.refs_4_ = f32[128,128]{1,0:T(8,128)S(1)} collective-permute-done((f32[128,128]{1,0:T(8,128)S(1)}, f32[128,128]{1,0:T(8,128)S(1)}, u32[]{:S(2)}, u32[]{:S(2)}) %collective-permute-start.8) | collective-permute-done | bytes 65568 | tf_op jit(solution)/shard_map/ppermute | solution.py:213
  19.6 0.0 collective-permute-done.9.refs_5_
  19.6 0.8 %gather.1 = (f32[8,4096]{1,0:T(8,128)}, f32[8,4096]{1,0:T(8,128)}) custom-call(f32[64,128]{1,0:T(8,128)S(1)} %get-tuple-element.28.refs_0_, f32[192,128]{1,0:T(8,128)S(1)} %collective-permute-done.5.aside.refs_1_, f32[128,128]{1,0:T(8,128)S(1)} %collective-permute-done.6.x.refs_2_, f32[64,128]{1,0:T(8,128)S(1)} %collective-permute-done.7.refs_3_, ...), custom_call_target="tpu_custom_call" | custom-call | tf_op jit(solution)/shard_map/gather/pallas_call | solution.py:196
  (4 shorter events, 0.0 us)
Async XLA Ops:
  1.7 4.1 %collective-permute-start = (f32[288,128]{1,0:T(8,128)S(1)}, f32[288,128]{1,0:T(8,128)S(1)}, u32[]{:S(2)}, u32[]{:S(2)}) collective-permute-start(f32[288,128]{1,0:T(8,128)S(1)} %get-tuple-element.19), channel_id=1, source_target_pairs={{0,4},{4,0},{8,12},{12,8},{16,20},{20,16},{24,28},{28,24},{1,5},{5... | collective-permute-start | bytes 442376 | tf_op jit(solution)/shard_map/ppermute | solution.py:213
  2.2 7.4 %collective-permute-start.1 = (f32[192,128]{1,0:T(8,128)S(1)}, f32[192,128]{1,0:T(8,128)S(1)}, u32[]{:S(2)}, u32[]{:S(2)}) collective-permute-start(f32[192,128]{1,0:T(8,128)S(1)} %get-tuple-element.20), channel_id=1, source_target_pairs={{0,28},{4,24},{8,20},{12,16},{16,12},{20,8},{24,4},{28,0},{1,29},{... | collective-permute-start | bytes 294920 | tf_op jit(solution)/shard_map/ppermute | solution.py:213
  5.8 5.2 %collective-permute-start.3 = (f32[192,128]{1,0:T(8,128)S(1)}, f32[192,128]{1,0:T(8,128)S(1)}, u32[]{:S(2)}, u32[]{:S(2)}) collective-permute-start(f32[192,128]{1,0:T(8,128)S(1)} %get-tuple-element.24), channel_id=1, source_target_pairs={{0,12},{4,8},{8,4},{12,0},{16,28},{20,24},{24,20},{28,16},{1,13},{... | collective-permute-start | bytes 294920 | tf_op jit(solution)/shard_map/ppermute | solution.py:213
  6.1 4.9 %collective-permute-start.4 = (f32[192,128]{1,0:T(8,128)S(1)}, f32[192,128]{1,0:T(8,128)S(1)}, u32[]{:S(2)}, u32[]{:S(2)}) collective-permute-start(f32[192,128]{1,0:T(8,128)S(1)} %get-tuple-element.22.refs_4_), channel_id=1, source_target_pairs={{0,20},{4,16},{8,28},{12,24},{16,4},{20,0},{24,12},{28,8},{1,21},{... | collective-permute-start | bytes 294920 | tf_op jit(solution)/shard_map/ppermute | solution.py:213
  8.8 0.8 %copy-start = (bf16[2,2,256,256]{3,2,1,0:T(8,128)(2,1)}, bf16[2,2,256,256]{3,2,1,0:T(8,128)(2,1)S(1)}, u32[]{:S(2)}) copy-start(bf16[2,2,256,256]{3,2,1,0:T(8,128)(2,1)S(1)} %get-tuple-element.25.refs_7_) | copy-start | bytes 1572868
  9.6 1.4 %copy-start.1 = (bf16[2,2,256,256]{3,2,1,0:T(8,128)(2,1)S(1)}, bf16[2,2,256,256]{3,2,1,0:T(8,128)(2,1)}, u32[]{:S(2)}) copy-start(bf16[2,2,256,256]{3,2,1,0:T(8,128)(2,1)} %copy-done) | copy-start | bytes 1572868
  9.6 1.3 %collective-permute-start.2 = (f32[96,128]{1,0:T(8,128)S(1)}, f32[96,128]{1,0:T(8,128)S(1)}, u32[]{:S(2)}, u32[]{:S(2)}) collective-permute-start(f32[96,128]{1,0:T(8,128)S(1)} %second_half.2), channel_id=1, source_target_pairs={{0,4},{4,0},{8,12},{12,8},{16,20},{20,16},{24,28},{28,24},{1,5},{5... | collective-permute-start | bytes 147464 | tf_op jit(solution)/shard_map/ppermute | solution.py:213
  12.5 3.0 %collective-permute-start.5 = (f32[192,128]{1,0:T(8,128)S(1)}, f32[192,128]{1,0:T(8,128)S(1)}, u32[]{:S(2)}, u32[]{:S(2)}) collective-permute-start(f32[192,128]{1,0:T(8,128)S(1)} %get-tuple-element.29), channel_id=1, source_target_pairs={{0,4},{4,0},{8,12},{12,8},{16,20},{20,16},{24,28},{28,24},{1,5},{5... | collective-permute-start | bytes 294920 | tf_op jit(solution)/shard_map/ppermute | solution.py:213
  12.8 5.0 %collective-permute-start.6 = (f32[128,128]{1,0:T(8,128)S(1)}, f32[128,128]{1,0:T(8,128)S(1)}, u32[]{:S(2)}, u32[]{:S(2)}) collective-permute-start(f32[128,128]{1,0:T(8,128)S(1)} %get-tuple-element.30), channel_id=1, source_target_pairs={{0,28},{4,24},{8,20},{12,16},{16,12},{20,8},{24,4},{28,0},{1,29},{... | collective-permute-start | bytes 196616 | tf_op jit(solution)/shard_map/ppermute | solution.py:213
  15.5 4.1 %collective-permute-start.8 = (f32[128,128]{1,0:T(8,128)S(1)}, f32[128,128]{1,0:T(8,128)S(1)}, u32[]{:S(2)}, u32[]{:S(2)}) collective-permute-start(f32[128,128]{1,0:T(8,128)S(1)} %get-tuple-element.32), channel_id=1, source_target_pairs={{0,12},{4,8},{8,4},{12,0},{16,28},{20,24},{24,20},{28,16},{1,13},{... | collective-permute-start | bytes 196616 | tf_op jit(solution)/shard_map/ppermute | solution.py:213
  15.7 4.0 %collective-permute-start.9 = (f32[128,128]{1,0:T(8,128)S(1)}, f32[128,128]{1,0:T(8,128)S(1)}, u32[]{:S(2)}, u32[]{:S(2)}) collective-permute-start(f32[128,128]{1,0:T(8,128)S(1)} %get-tuple-element.33), channel_id=1, source_target_pairs={{0,20},{4,16},{8,28},{12,24},{16,4},{20,0},{24,12},{28,8},{1,21},{... | collective-permute-start | bytes 196616 | tf_op jit(solution)/shard_map/ppermute | solution.py:213
  17.9 1.2 %collective-permute-start.7 = (f32[64,128]{1,0:T(8,128)S(1)}, f32[64,128]{1,0:T(8,128)S(1)}, u32[]{:S(2)}, u32[]{:S(2)}) collective-permute-start(f32[64,128]{1,0:T(8,128)S(1)} %second_half.3), channel_id=1, source_target_pairs={{0,4},{4,0},{8,12},{12,8},{16,20},{20,16},{24,28},{28,24},{1,5},{5... | collective-permute-start | bytes 98312 | tf_op jit(solution)/shard_map/ppermute | solution.py:213

commit v6 on v5

--- a/solution.py
+++ b/solution.py
@@ -29,6 +29,11 @@
     outer = 2 * np.pi * k * r / rows
     stacked = np.stack([np.cos(outer), -np.sin(outer)])
     first = stacked.reshape(2, parts, rows // parts, rows).swapaxes(0, 1).reshape(2 * rows, rows)
+    high, low = (t.reshape(2 * rows, 2, 2, rows // 4) for t in halves(first))
+    first = []
+    for diagonal in ((0, 0), (1, 1)), ((0, 1), (1, 0)):
+        cut_high, cut_low = (np.concatenate([t[:, y, x] for y, x in diagonal], axis=1) for t in (high, low))
+        first.append(np.concatenate([cut_high, cut_high, cut_low], axis=1))
     last = (stacked / length).reshape(2, joined, rows // joined, rows).transpose(1, 3, 0, 2)
     last = last.reshape(joined, rows, 2 * rows // joined)
     lane = np.arange(LANES)
@@ -37,7 +42,7 @@
     inner = 2 * np.pi * (lane[:, None] * lane[None, :] % LANES) / LANES
     cos2, sin2 = np.cos(inner), np.sin(inner)
     into = np.block([[cos2, -sin2], [sin2, cos2]])
-    return np.stack(halves(first)), np.stack(halves(last)), np.stack(halves(into)), twiddle
+    return np.stack(first), np.stack(halves(last)), np.stack(halves(into)), twiddle
 
 
 def split(x):
@@ -99,15 +104,48 @@
     out[...] = x[out.shape[0]:, :]
 
 
-def unpack(plan, got, held):
-    me, _, ((far_from, far_others), (first_from, _), (second_from, _)) = route(plan)
-    own, aside, far, far_other, first, second = got
-    step = own.shape[0]
-    for ref, at, device in (
-        (own, 0, me), (aside, 0, me ^ 1), (far, 0, far_from), (far_other, 0, far_others),
-        (first, 0, first_from), (first, 1, first_from ^ 1), (second, 0, second_from), (second, 1, second_from ^ 1),
-    ):
-        held[device] = ref[at * step:(at + 1) * step, :]
+def slot(device):
+    return (device >> 1 ^ device >> 2) & 1, (device >> 2) * 2 + (device & 1)
+
+
+def unpack(pieces, held):
+    step = held.shape[1]
+    for ref, at, place in pieces:
+        held[place] = ref[at * step:(at + 1) * step, :]
+
+
+def came_first(plan, got):
+    me, _, ((far_from, far_others), *_) = route(plan)
+    own, aside, far, far_other = got
+    return (own, 0, me), (aside, 0, me ^ 1), (far, 0, far_from), (far_other, 0, far_others)
+
+
+def came_last(plan, got):
+    _, _, (_, (first_from, _), (second_from, _)) = route(plan)
+    first, second = got
+    return (first, 0, first_from), (first, 1, first_from ^ 1), (second, 0, second_from), (second, 1, second_from ^ 1)
+
+
+def outer_stage(came, held, table):
+    unpack([(ref, at, slot(device)[1]) for ref, at, device in came], held)
+    diagonal = slot(came[0][2])[0]
+    half, chunks = 4 * held.shape[1] // 3, held.shape[1] // 3
+    whole = [held[:, i * chunks:(i + 1) * chunks, :].reshape(half, LANES) for i in range(3)]
+    high, low = split(jnp.concatenate(whole, axis=1))
+    both = jnp.concatenate([high, low], axis=0)
+    m = table.shape[1] // PARTS
+    sums = []
+    for q in range(PARTS):
+        rows = pl.ds(q * m, m)
+        sums.append((dot(table[diagonal, rows, 2 * half:], high), dot(table[diagonal, rows, :2 * half], both)))
+    return sums
+
+
+def early(own, aside, far, far_other, table, out, held):
+    sums = outer_stage(came_first(PLANS[0], (own, aside, far, far_other)), held, table)
+    m = out.shape[0] // PARTS
+    for q, (less, more) in enumerate(sums):
+        out[q * m:(q + 1) * m, :] = less + more
 
 
 def fetch(*refs):
@@ -143,16 +181,13 @@
 
 
 def transform(*refs):
-    got, (first, last, into, twiddle), outs, (held, y) = refs[:6], refs[6:10], refs[10:14], refs[14:]
-    unpack(PLANS[0], got, held)
-    n = held.shape[0]
-    chunks = held.shape[1] // 3
+    got, (begun, first, last, into, twiddle), outs, (held, y) = refs[:2], refs[2:7], refs[7:11], refs[11:]
+    n, chunks = y.shape[0], y.shape[1] // 2
     rows = n * chunks
     m = rows // PARTS
-    whole = [held[:, i * chunks:(i + 1) * chunks, :].reshape(rows, LANES) for i in range(3)]
-    signals = split(jnp.concatenate(whole, axis=1))
     turns = [lanes_of(twiddle, q, m) for q in range(PARTS)]
-    outer = [dot_left(first[0, 2 * m * q:2 * m * (q + 1)], first[1, 2 * m * q:2 * m * (q + 1)], signals) for q in range(PARTS)]
+    sums = outer_stage(came_last(PLANS[0], got), held, first)
+    outer = [(begun[2 * m * q:2 * m * (q + 1), :] + less) + more for q, (less, more) in enumerate(sums)]
     spectra = []
     for z, (c, s) in zip(outer, turns):
         turned = []
@@ -182,7 +217,7 @@
 
 def gather(*refs):
     got, (a, b, held) = refs[:6], refs[6:]
-    unpack(PLANS[1], got, held)
+    unpack(came_first(PLANS[1], got[:4]) + came_last(PLANS[1], got[4:]), held)
     channels, block = a.shape
     chunks = block // LANES
     for i, ref in enumerate((a, b)):
@@ -196,11 +231,12 @@
     return pl.pallas_call(
         body,
         out_shape=[kind(shape, dtype) for shape, dtype in outs],
-        in_specs=[pl.BlockSpec(memory_space=pl.ANY)] * far_in + [near] * (len(ins) - far_in),
+        in_specs=[pl.BlockSpec(memory_space=pltpu.HBM)] * far_in + [near] * (len(ins) - far_in),
         out_specs=[near] * len(outs),
         scratch_shapes=scratch,
+        compiler_params=pltpu.CompilerParams(vmem_limit_bytes=16 * 2**20),
         name=body.__name__,
-    )(*ins[:far_in], *(pltpu.with_memory_space_constraint(x, pltpu.VMEM) for x in ins[far_in:]))
+    )(*(pltpu.with_memory_space_constraint(x, pltpu.VMEM if i >= far_in else pltpu.HBM) for i, x in enumerate(ins)))
 
 
 def per_device(inputs, grads, response):
@@ -234,9 +270,11 @@
     near += [pltpu.VMEM((channels, 3 * chunks, LANES), kind), pltpu.SemaphoreType.DMA((3 * LOADS,))]
     sent = call(spread, [inputs, grads, response], sizes(3), near, 3)
     got = exchange(PLANS[0], *sent, meanwhile=bring)
-    near = [pltpu.VMEM((n, arrays * chunks, LANES), kind) for arrays in (3, 2)]
-    got = exchange(PLANS[1], *call(transform, got, sizes(2), near))
-    return call(gather, got, [((channels, block), kind)] * 2, near[1:], near_out=False)
+    near = [pltpu.VMEM((n // 2, 3 * chunks, LANES), kind)]
+    (begun,) = call(early, [*got[:4], got[6]], [((2 * n * chunks, 3 * LANES), kind)], near)
+    pieces = [pltpu.VMEM((n, 2 * chunks, LANES), kind)]
+    got = exchange(PLANS[1], *call(transform, [*got[4:6], begun, *got[6:]], sizes(2), near + pieces))
+    return call(gather, got, [((channels, block), kind)] * 2, pieces, near_out=False)
 
 
 RADIX = 128

time: 20.6 us -> 20.5 us (level)
  local copies, waits for them, and re-layouts: 0.79 us -> 0 us
  Pallas kernels: 4.73 us -> 5.09 us
  waiting for transfers between devices: 3.67 us -> 3.9 us
    unnamed x4 -> x0, local copies, waits for them, and re-layouts: 0.79 us -> none
    pallas_call x8 -> x9, Pallas kernels: 4.73 us -> 5.09 us  [call(): pl.pallas_call(body, out_shape=[kind(shape, dtype) for shape, dtype in ou...]
    ppermute x10, waiting for transfers between devices: 3.67 us -> 3.9 us  [swap(): lax.ppermute(x, 'context', [(i, i ^ (odd if i % 2 else even)) for i in ra...]
  transfers between devices with their start and end apart: 10 -> 10, of which waited for: 5 -> 6; matrix products, arithmetic and copies ran while one was open for 0% -> 0% of each run, Pallas kernels for 7% -> 9%
where the time goes in v6:
time: 20.5 us; the launch traced here: 20.2 us
  starting transfers between devices  10.6 us (52%)
  Pallas kernels  5.09 us (25%)
  waiting for transfers between devices  3.9 us (19%)
  between operations  0.68 us (3%)
    ppermute x10, starting transfers between devices, swap(): lax.ppermute(x, 'context', [(i, i ^ (odd if i % 2 else even)) for i in ra...  10.6 us
    pallas_call x9, Pallas kernels, call(): pl.pallas_call(body, out_shape=[kind(shape, dtype) for shape, dtype in ou...  5.09 us
    ppermute x10, waiting for transfers between devices, swap(): lax.ppermute(x, 'context', [(i, i ^ (odd if i % 2 else even)) for i in ra...  3.9 us
  transfers between devices with their start and end apart: 10, of which 6 were waited for; matrix products, arithmetic and copies ran while one was open for 0% of the time, Pallas kernels for 9%

profile of v6, /device:TPU:0, one launch (start us, length us, event | category | flops | bytes accessed | tf_op | source)
XLA Modules:
  0.0 20.2 jit_solution(17694948998874983911)
XLA Ops:
  0.6 1.1 %spread.1 = (f32[96,128]{1,0:T(8,128)S(1)}, f32[192,128]{1,0:T(8,128)S(1)}, f32[288,128]{1,0:T(8,128)S(1)}, f32[192,128]{1,0:T(8,128)S(1)}) custom-call(f32[8,4096]{1,0:T(8,128)} %refs_0_.2, f32[8,4096]{1,0:T(8,128)} %refs_1_.2, f32[8,4096]{1,0:T(8,128)} %refs_2_.2), custom_call_target="tpu_custom_call" | custom-call | tf_op jit(solution)/shard_map/spread/pallas_call | solution.py:231
  1.7 0.5 %collective-permute-start = (f32[288,128]{1,0:T(8,128)S(1)}, f32[288,128]{1,0:T(8,128)S(1)}, u32[]{:S(2)}, u32[]{:S(2)}) collective-permute-start(f32[288,128]{1,0:T(8,128)S(1)} %get-tuple-element.19), channel_id=1, source_target_pairs={{0,4},{4,0},{8,12},{12,8},{16,20},{20,16},{24,28},{28,24},{1,5},{5... | collective-permute-start | bytes 442376 | tf_op jit(solution)/shard_map/ppermute | solution.py:249
  2.2 3.6 %collective-permute-start.3 = (f32[192,128]{1,0:T(8,128)S(1)}, f32[192,128]{1,0:T(8,128)S(1)}, u32[]{:S(2)}, u32[]{:S(2)}) collective-permute-start(f32[192,128]{1,0:T(8,128)S(1)} %get-tuple-element.23), channel_id=1, source_target_pairs={{0,28},{4,24},{8,20},{12,16},{16,12},{20,8},{24,4},{28,0},{1,29},{... | collective-permute-start | bytes 294920 | tf_op jit(solution)/shard_map/ppermute | solution.py:249
  5.8 0.0 collective-permute-done.aside
  5.8 0.3 %collective-permute-start.1 = (f32[192,128]{1,0:T(8,128)S(1)}, f32[192,128]{1,0:T(8,128)S(1)}, u32[]{:S(2)}, u32[]{:S(2)}) collective-permute-start(f32[192,128]{1,0:T(8,128)S(1)} %get-tuple-element.20), channel_id=1, source_target_pairs={{0,12},{4,8},{8,4},{12,0},{16,28},{20,24},{24,20},{28,16},{1,13},{... | collective-permute-start | bytes 294920 | tf_op jit(solution)/shard_map/ppermute | solution.py:249
  6.1 1.3 %collective-permute-start.2 = (f32[192,128]{1,0:T(8,128)S(1)}, f32[192,128]{1,0:T(8,128)S(1)}, u32[]{:S(2)}, u32[]{:S(2)}) collective-permute-start(f32[192,128]{1,0:T(8,128)S(1)} %get-tuple-element.21.refs_4_), channel_id=1, source_target_pairs={{0,20},{4,16},{8,28},{12,24},{16,4},{20,0},{24,12},{28,8},{1,21},{... | collective-permute-start | bytes 294920 | tf_op jit(solution)/shard_map/ppermute | solution.py:249
  7.4 1.5 %fetch.1 = (bf16[2,512,384]{2,1,0:T(8,128)(2,1)S(1)}, bf16[2,2,256,256]{3,2,1,0:T(8,128)(2,1)S(1)}, bf16[2,256,256]{2,1,0:T(8,128)(2,1)S(1)}, f32[256,256]{1,0:T(8,128)S(1)}) custom-call(bf16[2,512,384]{2,1,0:T(8,128)(2,1)} %constant.8.clone.refs_0_, bf16[2,2,256,256]{3,2,1,0:T(8,128)(2,1)} %constant.9.clone.refs_1_, ...), custom_call_target="tpu_custom_call" | custom-call | tf_op jit(solution)/shard_map/fetch/pallas_call | solution.py:231
  8.9 0.1 collective-permute-done.3.x.far
  8.9 0.3 %collective-permute-start.4 = (f32[96,128]{1,0:T(8,128)S(1)}, f32[96,128]{1,0:T(8,128)S(1)}, u32[]{:S(2)}, u32[]{:S(2)}) collective-permute-start(f32[96,128]{1,0:T(8,128)S(1)} %second_half.2), channel_id=1, source_target_pairs={{0,4},{4,0},{8,12},{12,8},{16,20},{20,16},{24,28},{28,24},{1,5},{5... | collective-permute-start | bytes 147464 | tf_op jit(solution)/shard_map/ppermute | solution.py:249
  9.2 1.0 %collective-permute-done.4.far_other = f32[96,128]{1,0:T(8,128)S(1)} collective-permute-done((f32[96,128]{1,0:T(8,128)S(1)}, f32[96,128]{1,0:T(8,128)S(1)}, u32[]{:S(2)}, u32[]{:S(2)}) %collective-permute-start.4) | collective-permute-done | bytes 49184 | tf_op jit(solution)/shard_map/ppermute | solution.py:249
  10.2 0.4 %early.1.refs_2_ = f32[512,384]{1,0:T(8,128)S(1)} custom-call(f32[96,128]{1,0:T(8,128)S(1)} %get-tuple-element.22.own, f32[288,128]{1,0:T(8,128)S(1)} %collective-permute-done.aside, f32[192,128]{1,0:T(8,128)S(1)} %collective-permute-done.3.x.far, f32[96,128]{1,0:T(8,128)S(1)} %collective-permute-done.4.far_other, ...), custom_call_target="tpu_custom_call" | custom-call | tf_op jit(solution)/shard_map/early/pallas_call | solution.py:231
  10.6 0.4 %collective-permute-done.1.refs_0_ = f32[192,128]{1,0:T(8,128)S(1)} collective-permute-done((f32[192,128]{1,0:T(8,128)S(1)}, f32[192,128]{1,0:T(8,128)S(1)}, u32[]{:S(2)}, u32[]{:S(2)}) %collective-permute-start.1) | collective-permute-done | bytes 98336 | tf_op jit(solution)/shard_map/ppermute | solution.py:249
  11.0 0.0 collective-permute-done.2.refs_1_
  11.0 1.3 %transform.1 = (f32[64,128]{1,0:T(8,128)S(1)}, f32[128,128]{1,0:T(8,128)S(1)}, f32[192,128]{1,0:T(8,128)S(1)}, f32[128,128]{1,0:T(8,128)S(1)}) custom-call(f32[192,128]{1,0:T(8,128)S(1)} %collective-permute-done.1.refs_0_, f32[192,128]{1,0:T(8,128)S(1)} %collective-permute-done.2.refs_1_, f32[512,384]{1,0:T(8,128)S(1)} %early.1.refs_2_, ...), custom_call_target="tpu_custom_call" | custom-call | tf_op jit(solution)/shard_map/transform/pallas_call | solution.py:231
  12.3 0.4 %collective-permute-start.5 = (f32[192,128]{1,0:T(8,128)S(1)}, f32[192,128]{1,0:T(8,128)S(1)}, u32[]{:S(2)}, u32[]{:S(2)}) collective-permute-start(f32[192,128]{1,0:T(8,128)S(1)} %get-tuple-element.29), channel_id=1, source_target_pairs={{0,4},{4,0},{8,12},{12,8},{16,20},{20,16},{24,28},{28,24},{1,5},{5... | collective-permute-start | bytes 294920 | tf_op jit(solution)/shard_map/ppermute | solution.py:249
  12.7 2.6 %collective-permute-start.6 = (f32[128,128]{1,0:T(8,128)S(1)}, f32[128,128]{1,0:T(8,128)S(1)}, u32[]{:S(2)}, u32[]{:S(2)}) collective-permute-start(f32[128,128]{1,0:T(8,128)S(1)} %get-tuple-element.30), channel_id=1, source_target_pairs={{0,28},{4,24},{8,20},{12,16},{16,12},{20,8},{24,4},{28,0},{1,29},{... | collective-permute-start | bytes 196616 | tf_op jit(solution)/shard_map/ppermute | solution.py:249
  15.3 0.0 collective-permute-done.5.aside.refs_1_
  15.3 0.2 collective-permute-start.8
  15.5 1.4 %collective-permute-start.9 = (f32[128,128]{1,0:T(8,128)S(1)}, f32[128,128]{1,0:T(8,128)S(1)}, u32[]{:S(2)}, u32[]{:S(2)}) collective-permute-start(f32[128,128]{1,0:T(8,128)S(1)} %get-tuple-element.33), channel_id=1, source_target_pairs={{0,20},{4,16},{8,28},{12,24},{16,4},{20,0},{24,12},{28,8},{1,21},{... | collective-permute-start | bytes 196616 | tf_op jit(solution)/shard_map/ppermute | solution.py:249
  16.9 0.9 %collective-permute-done.6.x.refs_2_ = f32[128,128]{1,0:T(8,128)S(1)} collective-permute-done((f32[128,128]{1,0:T(8,128)S(1)}, f32[128,128]{1,0:T(8,128)S(1)}, u32[]{:S(2)}, u32[]{:S(2)}) %collective-permute-start.6) | collective-permute-done | bytes 65568 | tf_op jit(solution)/shard_map/ppermute | solution.py:249
  17.7 0.1 collective-permute-start.7
  17.8 1.1 %collective-permute-done.7.refs_3_ = f32[64,128]{1,0:T(8,128)S(1)} collective-permute-done((f32[64,128]{1,0:T(8,128)S(1)}, f32[64,128]{1,0:T(8,128)S(1)}, u32[]{:S(2)}, u32[]{:S(2)}) %collective-permute-start.7) | collective-permute-done | bytes 32800 | tf_op jit(solution)/shard_map/ppermute | solution.py:249
  19.0 0.5 %collective-permute-done.8.refs_4_ = f32[128,128]{1,0:T(8,128)S(1)} collective-permute-done((f32[128,128]{1,0:T(8,128)S(1)}, f32[128,128]{1,0:T(8,128)S(1)}, u32[]{:S(2)}, u32[]{:S(2)}) %collective-permute-start.8) | collective-permute-done | bytes 65568 | tf_op jit(solution)/shard_map/ppermute | solution.py:249
  19.5 0.0 collective-permute-done.9.refs_5_
  19.5 0.8 %gather.1 = (f32[8,4096]{1,0:T(8,128)}, f32[8,4096]{1,0:T(8,128)}) custom-call(f32[64,128]{1,0:T(8,128)S(1)} %get-tuple-element.28.refs_0_, f32[192,128]{1,0:T(8,128)S(1)} %collective-permute-done.5.aside.refs_1_, f32[128,128]{1,0:T(8,128)S(1)} %collective-permute-done.6.x.refs_2_, f32[64,128]{1,0:T(8,128)S(1)} %collective-permute-done.7.refs_3_, ...), custom_call_target="tpu_custom_call" | custom-call | tf_op jit(solution)/shard_map/gather/pallas_call | solution.py:231
  (4 shorter events, 0.0 us)
Async XLA Ops:
  1.7 4.1 %collective-permute-start = (f32[288,128]{1,0:T(8,128)S(1)}, f32[288,128]{1,0:T(8,128)S(1)}, u32[]{:S(2)}, u32[]{:S(2)}) collective-permute-start(f32[288,128]{1,0:T(8,128)S(1)} %get-tuple-element.19), channel_id=1, source_target_pairs={{0,4},{4,0},{8,12},{12,8},{16,20},{20,16},{24,28},{28,24},{1,5},{5... | collective-permute-start | bytes 442376 | tf_op jit(solution)/shard_map/ppermute | solution.py:249
  2.2 6.7 %collective-permute-start.3 = (f32[192,128]{1,0:T(8,128)S(1)}, f32[192,128]{1,0:T(8,128)S(1)}, u32[]{:S(2)}, u32[]{:S(2)}) collective-permute-start(f32[192,128]{1,0:T(8,128)S(1)} %get-tuple-element.23), channel_id=1, source_target_pairs={{0,28},{4,24},{8,20},{12,16},{16,12},{20,8},{24,4},{28,0},{1,29},{... | collective-permute-start | bytes 294920 | tf_op jit(solution)/shard_map/ppermute | solution.py:249
  5.8 5.2 %collective-permute-start.1 = (f32[192,128]{1,0:T(8,128)S(1)}, f32[192,128]{1,0:T(8,128)S(1)}, u32[]{:S(2)}, u32[]{:S(2)}) collective-permute-start(f32[192,128]{1,0:T(8,128)S(1)} %get-tuple-element.20), channel_id=1, source_target_pairs={{0,12},{4,8},{8,4},{12,0},{16,28},{20,24},{24,20},{28,16},{1,13},{... | collective-permute-start | bytes 294920 | tf_op jit(solution)/shard_map/ppermute | solution.py:249
  6.1 4.9 %collective-permute-start.2 = (f32[192,128]{1,0:T(8,128)S(1)}, f32[192,128]{1,0:T(8,128)S(1)}, u32[]{:S(2)}, u32[]{:S(2)}) collective-permute-start(f32[192,128]{1,0:T(8,128)S(1)} %get-tuple-element.21.refs_4_), channel_id=1, source_target_pairs={{0,20},{4,16},{8,28},{12,24},{16,4},{20,0},{24,12},{28,8},{1,21},{... | collective-permute-start | bytes 294920 | tf_op jit(solution)/shard_map/ppermute | solution.py:249
  8.9 1.3 %collective-permute-start.4 = (f32[96,128]{1,0:T(8,128)S(1)}, f32[96,128]{1,0:T(8,128)S(1)}, u32[]{:S(2)}, u32[]{:S(2)}) collective-permute-start(f32[96,128]{1,0:T(8,128)S(1)} %second_half.2), channel_id=1, source_target_pairs={{0,4},{4,0},{8,12},{12,8},{16,20},{20,16},{24,28},{28,24},{1,5},{5... | collective-permute-start | bytes 147464 | tf_op jit(solution)/shard_map/ppermute | solution.py:249
  12.3 3.0 %collective-permute-start.5 = (f32[192,128]{1,0:T(8,128)S(1)}, f32[192,128]{1,0:T(8,128)S(1)}, u32[]{:S(2)}, u32[]{:S(2)}) collective-permute-start(f32[192,128]{1,0:T(8,128)S(1)} %get-tuple-element.29), channel_id=1, source_target_pairs={{0,4},{4,0},{8,12},{12,8},{16,20},{20,16},{24,28},{28,24},{1,5},{5... | collective-permute-start | bytes 294920 | tf_op jit(solution)/shard_map/ppermute | solution.py:249
  12.7 5.0 %collective-permute-start.6 = (f32[128,128]{1,0:T(8,128)S(1)}, f32[128,128]{1,0:T(8,128)S(1)}, u32[]{:S(2)}, u32[]{:S(2)}) collective-permute-start(f32[128,128]{1,0:T(8,128)S(1)} %get-tuple-element.30), channel_id=1, source_target_pairs={{0,28},{4,24},{8,20},{12,16},{16,12},{20,8},{24,4},{28,0},{1,29},{... | collective-permute-start | bytes 196616 | tf_op jit(solution)/shard_map/ppermute | solution.py:249
  15.3 4.1 %collective-permute-start.8 = (f32[128,128]{1,0:T(8,128)S(1)}, f32[128,128]{1,0:T(8,128)S(1)}, u32[]{:S(2)}, u32[]{:S(2)}) collective-permute-start(f32[128,128]{1,0:T(8,128)S(1)} %get-tuple-element.32), channel_id=1, source_target_pairs={{0,12},{4,8},{8,4},{12,0},{16,28},{20,24},{24,20},{28,16},{1,13},{... | collective-permute-start | bytes 196616 | tf_op jit(solution)/shard_map/ppermute | solution.py:249
  15.5 4.0 %collective-permute-start.9 = (f32[128,128]{1,0:T(8,128)S(1)}, f32[128,128]{1,0:T(8,128)S(1)}, u32[]{:S(2)}, u32[]{:S(2)}) collective-permute-start(f32[128,128]{1,0:T(8,128)S(1)} %get-tuple-element.33), channel_id=1, source_target_pairs={{0,20},{4,16},{8,28},{12,24},{16,4},{20,0},{24,12},{28,8},{1,21},{... | collective-permute-start | bytes 196616 | tf_op jit(solution)/shard_map/ppermute | solution.py:249
  17.7 1.2 %collective-permute-start.7 = (f32[64,128]{1,0:T(8,128)S(1)}, f32[64,128]{1,0:T(8,128)S(1)}, u32[]{:S(2)}, u32[]{:S(2)}) collective-permute-start(f32[64,128]{1,0:T(8,128)S(1)} %second_half.3), channel_id=1, source_target_pairs={{0,4},{4,0},{8,12},{12,8},{16,20},{20,16},{24,28},{28,24},{1,5},{5... | collective-permute-start | bytes 98312 | tf_op jit(solution)/shard_map/ppermute | solution.py:249

commit v7 on v6

--- a/solution.py
+++ b/solution.py
@@ -81,13 +81,12 @@
     return me, to, from_
 
 
-def pack(plan, pieces, own, far, aside, beside):
+def pack(plan, pieces, own, far, aside, beside, other):
     me, ((far_to, _), (first_to, first_aside), (second_to, second_aside)), _ = route(plan)
     step = own.shape[0]
     for out, at, device in (
-        (own, 0, me), (far, 0, far_to), (far, 1, far_to ^ 1),
-        (aside, 0, me ^ 1), (aside, 1, first_aside), (aside, 2, second_aside),
-        (beside, 0, first_to), (beside, 1, second_to),
+        (own, 0, me), (far, 0, far_to), (far, 1, far_to ^ 1), (aside, 0, first_aside), (aside, 1, second_aside),
+        (beside, 0, first_to), (beside, 1, second_to), (other, 0, me ^ 1),
     ):
         out[at * step:(at + 1) * step, :] = pieces[device]
 
@@ -96,7 +95,7 @@
     step = beside.shape[0] // 2
     for i, out in enumerate((first, second)):
         out[:step, :] = beside[i * step:(i + 1) * step, :]
-        out[step:, :] = aside[(i + 1) * step:(i + 2) * step, :]
+        out[step:, :] = aside[i * step:(i + 1) * step, :]
 
 
 def second_half(x, *rest):
@@ -116,8 +115,8 @@
 
 def came_first(plan, got):
     me, _, ((far_from, far_others), *_) = route(plan)
-    own, aside, far, far_other = got
-    return (own, 0, me), (aside, 0, me ^ 1), (far, 0, far_from), (far_other, 0, far_others)
+    own, other, far, handed = got
+    return (own, 0, me), (other, 0, me ^ 1), (far, 0, far_from), (handed, 0, far_others)
 
 
 def came_last(plan, got):
@@ -141,8 +140,8 @@
     return sums
 
 
-def early(own, aside, far, far_other, table, out, held):
-    sums = outer_stage(came_first(PLANS[0], (own, aside, far, far_other)), held, table)
+def early(own, other, far, handed, table, out, held):
+    sums = outer_stage(came_first(PLANS[0], (own, other, far, handed)), held, table)
     m = out.shape[0] // PARTS
     for q, (less, more) in enumerate(sums):
         out[q * m:(q + 1) * m, :] = less + more
@@ -158,7 +157,7 @@
 
 
 def spread(*refs):
-    signals, outs, near, (held, arrived) = refs[:3], refs[3:7], refs[7:10], refs[10:]
+    signals, outs, near, (held, arrived) = refs[:3], refs[3:8], refs[8:11], refs[11:]
     channels, block = signals[0].shape
     chunks = block // LANES
     width = block // LOADS
@@ -181,7 +180,7 @@
 
 
 def transform(*refs):
-    got, (begun, first, last, into, twiddle), outs, (held, y) = refs[:2], refs[2:7], refs[7:11], refs[11:]
+    got, (begun, first, last, into, twiddle), outs, (held, y) = refs[:2], refs[2:7], refs[7:12], refs[12:]
     n, chunks = y.shape[0], y.shape[1] // 2
     rows = n * chunks
     m = rows // PARTS
@@ -249,17 +248,17 @@
         return lax.ppermute(x, "context", [(i, i ^ (odd if i % 2 else even)) for i in range(n)])
 
     def sizes(arrays):
-        return [((u * arrays * chunks, LANES), kind) for u in (1, 2, 3, 2)]
-
-    def exchange(plan, own, far, aside, beside, meanwhile=lambda x: []):
+        return [((u * arrays * chunks, LANES), kind) for u in (1, 2, 2, 2, 1)]
+
+    def exchange(plan, own, far, aside, beside, other, meanwhile=lambda x: []):
         step = own.shape[0]
         aside = swap(aside, 1, 1)
         far = swap(far, *plan[0])
         first, second = call(merge, [beside, aside], [((2 * step, LANES), kind)] * 2)
         made = meanwhile(second)
         first, second = swap(first, *plan[1]), swap(second, *plan[2])
-        (half,) = call(second_half, [far, *made[:1]], [((step, LANES), kind)])
-        return [own, aside, far, swap(half, 1, 1), first, second, *made]
+        (handed,) = call(second_half, [far, *made[:1]], [((step, LANES), kind)])
+        return [own, swap(other, 1, 1), far, swap(handed, 1, 1), first, second, *made]
 
     held = [jnp.asarray(t) for t in tables(n * block, PARTS, JOINED)]
 

time: 20.5 us -> 20.5 us (level)
  waiting for transfers between devices: 3.9 us -> 3.57 us
  starting transfers between devices: 10.6 us -> 10.9 us
    ppermute x10 -> x12, waiting for transfers between devices: 3.9 us -> 3.57 us  [swap(): lax.ppermute(x, 'context', [(i, i ^ (odd if i % 2 else even)) for i in ra...]
    ppermute x10 -> x12, starting transfers between devices: 10.6 us -> 10.9 us  [swap(): lax.ppermute(x, 'context', [(i, i ^ (odd if i % 2 else even)) for i in ra...]
  transfers between devices with their start and end apart: 10 -> 12, of which waited for: 6 -> 6; matrix products, arithmetic and copies ran while one was open for 0% -> 0% of each run, Pallas kernels for 9% -> 9%
where the time goes in v7:
time: 20.5 us; the launch traced here: 20.2 us
  starting transfers between devices  10.9 us (53%)
  Pallas kernels  5.09 us (25%)
  waiting for transfers between devices  3.57 us (17%)
  between operations  0.69 us (3%)
    ppermute x12, starting transfers between devices, swap(): lax.ppermute(x, 'context', [(i, i ^ (odd if i % 2 else even)) for i in ra...  10.9 us
    pallas_call x9, Pallas kernels, call(): pl.pallas_call(body, out_shape=[kind(shape, dtype) for shape, dtype in ou...  5.09 us
    ppermute x12, waiting for transfers between devices, swap(): lax.ppermute(x, 'context', [(i, i ^ (odd if i % 2 else even)) for i in ra...  3.57 us
  transfers between devices with their start and end apart: 12, of which 6 were waited for; matrix products, arithmetic and copies ran while one was open for 0% of the time, Pallas kernels for 9%

profile of v7, /device:TPU:0, one launch (start us, length us, event | category | flops | bytes accessed | tf_op | source)
XLA Modules:
  0.0 20.2 jit_solution(6865176743441922456)
XLA Ops:
  0.6 1.1 %spread.1 = (f32[96,128]{1,0:T(8,128)S(1)}, f32[192,128]{1,0:T(8,128)S(1)}, f32[192,128]{1,0:T(8,128)S(1)}, f32[192,128]{1,0:T(8,128)S(1)}, f32[96,128]{1,0:T(8,128)S(1)}) custom-call(f32[8,4096]{1,0:T(8,128)} %refs_0_.2, f32[8,4096]{1,0:T(8,128)} %refs_1_.2, f32[8,4096]{1,0:T(8,128)} %refs_2_.2), custom_call_target="tpu_custom_call" | custom-call | tf_op jit(solution)/shard_map/spread/pallas_call | solution.py:230
  1.7 0.5 %collective-permute-start = (f32[192,128]{1,0:T(8,128)S(1)}, f32[192,128]{1,0:T(8,128)S(1)}, u32[]{:S(2)}, u32[]{:S(2)}) collective-permute-start(f32[192,128]{1,0:T(8,128)S(1)} %get-tuple-element.21), channel_id=1, source_target_pairs={{0,4},{4,0},{8,12},{12,8},{16,20},{20,16},{24,28},{28,24},{1,5},{5... | collective-permute-start | bytes 294920 | tf_op jit(solution)/shard_map/ppermute | solution.py:248
  2.2 3.6 %collective-permute-start.4 = (f32[192,128]{1,0:T(8,128)S(1)}, f32[192,128]{1,0:T(8,128)S(1)}, u32[]{:S(2)}, u32[]{:S(2)}) collective-permute-start(f32[192,128]{1,0:T(8,128)S(1)} %get-tuple-element.26), channel_id=1, source_target_pairs={{0,28},{4,24},{8,20},{12,16},{16,12},{20,8},{24,4},{28,0},{1,29},{... | collective-permute-start | bytes 294920 | tf_op jit(solution)/shard_map/ppermute | solution.py:248
  5.8 0.0 collective-permute-done.aside
  5.8 0.3 %collective-permute-start.1 = (f32[192,128]{1,0:T(8,128)S(1)}, f32[192,128]{1,0:T(8,128)S(1)}, u32[]{:S(2)}, u32[]{:S(2)}) collective-permute-start(f32[192,128]{1,0:T(8,128)S(1)} %get-tuple-element.22), channel_id=1, source_target_pairs={{0,12},{4,8},{8,4},{12,0},{16,28},{20,24},{24,20},{28,16},{1,13},{... | collective-permute-start | bytes 294920 | tf_op jit(solution)/shard_map/ppermute | solution.py:248
  6.1 1.2 %collective-permute-start.2 = (f32[192,128]{1,0:T(8,128)S(1)}, f32[192,128]{1,0:T(8,128)S(1)}, u32[]{:S(2)}, u32[]{:S(2)}) collective-permute-start(f32[192,128]{1,0:T(8,128)S(1)} %get-tuple-element.23.refs_4_), channel_id=1, source_target_pairs={{0,20},{4,16},{8,28},{12,24},{16,4},{20,0},{24,12},{28,8},{1,21},{... | collective-permute-start | bytes 294920 | tf_op jit(solution)/shard_map/ppermute | solution.py:248
  7.3 0.2 collective-permute-start.3
  7.5 1.5 %fetch.1 = (bf16[2,512,384]{2,1,0:T(8,128)(2,1)S(1)}, bf16[2,2,256,256]{3,2,1,0:T(8,128)(2,1)S(1)}, bf16[2,256,256]{2,1,0:T(8,128)(2,1)S(1)}, f32[256,256]{1,0:T(8,128)S(1)}) custom-call(bf16[2,512,384]{2,1,0:T(8,128)(2,1)} %constant.8.clone.refs_0_, bf16[2,2,256,256]{3,2,1,0:T(8,128)(2,1)} %constant.9.clone.refs_1_, ...), custom_call_target="tpu_custom_call" | custom-call | tf_op jit(solution)/shard_map/fetch/pallas_call | solution.py:230
  9.0 0.0 collective-permute-done.4.x.far
  9.0 0.4 %collective-permute-start.5 = (f32[96,128]{1,0:T(8,128)S(1)}, f32[96,128]{1,0:T(8,128)S(1)}, u32[]{:S(2)}, u32[]{:S(2)}) collective-permute-start(f32[96,128]{1,0:T(8,128)S(1)} %second_half.2), channel_id=1, source_target_pairs={{0,4},{4,0},{8,12},{12,8},{16,20},{20,16},{24,28},{28,24},{1,5},{5... | collective-permute-start | bytes 147464 | tf_op jit(solution)/shard_map/ppermute | solution.py:248
  9.4 0.0 collective-permute-done.3.other
  9.4 0.9 %collective-permute-done.5.handed = f32[96,128]{1,0:T(8,128)S(1)} collective-permute-done((f32[96,128]{1,0:T(8,128)S(1)}, f32[96,128]{1,0:T(8,128)S(1)}, u32[]{:S(2)}, u32[]{:S(2)}) %collective-permute-start.5) | collective-permute-done | bytes 49184 | tf_op jit(solution)/shard_map/ppermute | solution.py:248
  10.3 0.4 %early.1.refs_2_ = f32[512,384]{1,0:T(8,128)S(1)} custom-call(f32[96,128]{1,0:T(8,128)S(1)} %get-tuple-element.24.own, f32[96,128]{1,0:T(8,128)S(1)} %collective-permute-done.3.other, f32[192,128]{1,0:T(8,128)S(1)} %collective-permute-done.4.x.far, f32[96,128]{1,0:T(8,128)S(1)} %collective-permute-done.5.handed, ...), custom_call_target="tpu_custom_call" | custom-call | tf_op jit(solution)/shard_map/early/pallas_call | solution.py:230
  10.7 0.3 %collective-permute-done.1.refs_0_ = f32[192,128]{1,0:T(8,128)S(1)} collective-permute-done((f32[192,128]{1,0:T(8,128)S(1)}, f32[192,128]{1,0:T(8,128)S(1)}, u32[]{:S(2)}, u32[]{:S(2)}) %collective-permute-start.1) | collective-permute-done | bytes 98336 | tf_op jit(solution)/shard_map/ppermute | solution.py:248
  11.0 0.0 collective-permute-done.2.refs_1_
  11.0 1.3 %transform.1 = (f32[64,128]{1,0:T(8,128)S(1)}, f32[128,128]{1,0:T(8,128)S(1)}, f32[128,128]{1,0:T(8,128)S(1)}, f32[128,128]{1,0:T(8,128)S(1)}, f32[64,128]{1,0:T(8,128)S(1)}) custom-call(f32[192,128]{1,0:T(8,128)S(1)} %collective-permute-done.1.refs_0_, f32[192,128]{1,0:T(8,128)S(1)} %collective-permute-done.2.refs_1_, f32[512,384]{1,0:T(8,128)S(1)} %early.1.refs_2_, ...), custom_call_target="tpu_custom_call" | custom-call | tf_op jit(solution)/shard_map/transform/pallas_call | solution.py:230
  12.3 0.4 %collective-permute-start.9 = (f32[128,128]{1,0:T(8,128)S(1)}, f32[128,128]{1,0:T(8,128)S(1)}, u32[]{:S(2)}, u32[]{:S(2)}) collective-permute-start(f32[128,128]{1,0:T(8,128)S(1)} %get-tuple-element.35), channel_id=1, source_target_pairs={{0,4},{4,0},{8,12},{12,8},{16,20},{20,16},{24,28},{28,24},{1,5},{5... | collective-permute-start | bytes 196616 | tf_op jit(solution)/shard_map/ppermute | solution.py:248
  12.7 2.6 %collective-permute-start.7 = (f32[128,128]{1,0:T(8,128)S(1)}, f32[128,128]{1,0:T(8,128)S(1)}, u32[]{:S(2)}, u32[]{:S(2)}) collective-permute-start(f32[128,128]{1,0:T(8,128)S(1)} %get-tuple-element.33), channel_id=1, source_target_pairs={{0,28},{4,24},{8,20},{12,16},{16,12},{20,8},{24,4},{28,0},{1,29},{... | collective-permute-start | bytes 196616 | tf_op jit(solution)/shard_map/ppermute | solution.py:248
  15.3 0.0 collective-permute-done.9.aside
  15.3 0.2 collective-permute-start.10
  15.5 1.3 %collective-permute-start.11 = (f32[128,128]{1,0:T(8,128)S(1)}, f32[128,128]{1,0:T(8,128)S(1)}, u32[]{:S(2)}, u32[]{:S(2)}) collective-permute-start(f32[128,128]{1,0:T(8,128)S(1)} %get-tuple-element.37), channel_id=1, source_target_pairs={{0,20},{4,16},{8,28},{12,24},{16,4},{20,0},{24,12},{28,8},{1,21},{... | collective-permute-start | bytes 196616 | tf_op jit(solution)/shard_map/ppermute | solution.py:248
  16.8 0.2 collective-permute-start.6
  17.0 0.8 %collective-permute-done.7.x.refs_2_ = f32[128,128]{1,0:T(8,128)S(1)} collective-permute-done((f32[128,128]{1,0:T(8,128)S(1)}, f32[128,128]{1,0:T(8,128)S(1)}, u32[]{:S(2)}, u32[]{:S(2)}) %collective-permute-start.7) | collective-permute-done | bytes 65568 | tf_op jit(solution)/shard_map/ppermute | solution.py:248
  17.7 0.1 collective-permute-start.8
  17.8 0.2 %collective-permute-done.6.refs_1_ = f32[64,128]{1,0:T(8,128)S(1)} collective-permute-done((f32[64,128]{1,0:T(8,128)S(1)}, f32[64,128]{1,0:T(8,128)S(1)}, u32[]{:S(2)}, u32[]{:S(2)}) %collective-permute-start.6) | collective-permute-done | bytes 32800 | tf_op jit(solution)/shard_map/ppermute | solution.py:248
  18.0 0.9 %collective-permute-done.8.refs_3_ = f32[64,128]{1,0:T(8,128)S(1)} collective-permute-done((f32[64,128]{1,0:T(8,128)S(1)}, f32[64,128]{1,0:T(8,128)S(1)}, u32[]{:S(2)}, u32[]{:S(2)}) %collective-permute-start.8) | collective-permute-done | bytes 32800 | tf_op jit(solution)/shard_map/ppermute | solution.py:248
  19.0 0.5 %collective-permute-done.10.refs_4_ = f32[128,128]{1,0:T(8,128)S(1)} collective-permute-done((f32[128,128]{1,0:T(8,128)S(1)}, f32[128,128]{1,0:T(8,128)S(1)}, u32[]{:S(2)}, u32[]{:S(2)}) %collective-permute-start.10) | collective-permute-done | bytes 65568 | tf_op jit(solution)/shard_map/ppermute | solution.py:248
  19.5 0.0 collective-permute-done.11.refs_5_
  19.5 0.8 %gather.1 = (f32[8,4096]{1,0:T(8,128)}, f32[8,4096]{1,0:T(8,128)}) custom-call(f32[64,128]{1,0:T(8,128)S(1)} %get-tuple-element.31.refs_0_, f32[64,128]{1,0:T(8,128)S(1)} %collective-permute-done.6.refs_1_, f32[128,128]{1,0:T(8,128)S(1)} %collective-permute-done.7.x.refs_2_, f32[64,128]{1,0:T(8,128)S(1)} %collective-permute-done.8.refs_3_, ...), custom_call_target="tpu_custom_call" | custom-call | tf_op jit(solution)/shard_map/gather/pallas_call | solution.py:230
  (4 shorter events, 0.0 us)
Async XLA Ops:
  1.7 4.1 %collective-permute-start = (f32[192,128]{1,0:T(8,128)S(1)}, f32[192,128]{1,0:T(8,128)S(1)}, u32[]{:S(2)}, u32[]{:S(2)}) collective-permute-start(f32[192,128]{1,0:T(8,128)S(1)} %get-tuple-element.21), channel_id=1, source_target_pairs={{0,4},{4,0},{8,12},{12,8},{16,20},{20,16},{24,28},{28,24},{1,5},{5... | collective-permute-start | bytes 294920 | tf_op jit(solution)/shard_map/ppermute | solution.py:248
  2.2 6.7 %collective-permute-start.4 = (f32[192,128]{1,0:T(8,128)S(1)}, f32[192,128]{1,0:T(8,128)S(1)}, u32[]{:S(2)}, u32[]{:S(2)}) collective-permute-start(f32[192,128]{1,0:T(8,128)S(1)} %get-tuple-element.26), channel_id=1, source_target_pairs={{0,28},{4,24},{8,20},{12,16},{16,12},{20,8},{24,4},{28,0},{1,29},{... | collective-permute-start | bytes 294920 | tf_op jit(solution)/shard_map/ppermute | solution.py:248
  5.8 5.2 %collective-permute-start.1 = (f32[192,128]{1,0:T(8,128)S(1)}, f32[192,128]{1,0:T(8,128)S(1)}, u32[]{:S(2)}, u32[]{:S(2)}) collective-permute-start(f32[192,128]{1,0:T(8,128)S(1)} %get-tuple-element.22), channel_id=1, source_target_pairs={{0,12},{4,8},{8,4},{12,0},{16,28},{20,24},{24,20},{28,16},{1,13},{... | collective-permute-start | bytes 294920 | tf_op jit(solution)/shard_map/ppermute | solution.py:248
  6.1 4.9 %collective-permute-start.2 = (f32[192,128]{1,0:T(8,128)S(1)}, f32[192,128]{1,0:T(8,128)S(1)}, u32[]{:S(2)}, u32[]{:S(2)}) collective-permute-start(f32[192,128]{1,0:T(8,128)S(1)} %get-tuple-element.23.refs_4_), channel_id=1, source_target_pairs={{0,20},{4,16},{8,28},{12,24},{16,4},{20,0},{24,12},{28,8},{1,21},{... | collective-permute-start | bytes 294920 | tf_op jit(solution)/shard_map/ppermute | solution.py:248
  7.3 2.1 %collective-permute-start.3 = (f32[96,128]{1,0:T(8,128)S(1)}, f32[96,128]{1,0:T(8,128)S(1)}, u32[]{:S(2)}, u32[]{:S(2)}) collective-permute-start(f32[96,128]{1,0:T(8,128)S(1)} %get-tuple-element.25), channel_id=1, source_target_pairs={{0,4},{4,0},{8,12},{12,8},{16,20},{20,16},{24,28},{28,24},{1,5},{5... | collective-permute-start | bytes 147464 | tf_op jit(solution)/shard_map/ppermute | solution.py:248
  9.0 1.3 %collective-permute-start.5 = (f32[96,128]{1,0:T(8,128)S(1)}, f32[96,128]{1,0:T(8,128)S(1)}, u32[]{:S(2)}, u32[]{:S(2)}) collective-permute-start(f32[96,128]{1,0:T(8,128)S(1)} %second_half.2), channel_id=1, source_target_pairs={{0,4},{4,0},{8,12},{12,8},{16,20},{20,16},{24,28},{28,24},{1,5},{5... | collective-permute-start | bytes 147464 | tf_op jit(solution)/shard_map/ppermute | solution.py:248
  12.3 3.0 %collective-permute-start.9 = (f32[128,128]{1,0:T(8,128)S(1)}, f32[128,128]{1,0:T(8,128)S(1)}, u32[]{:S(2)}, u32[]{:S(2)}) collective-permute-start(f32[128,128]{1,0:T(8,128)S(1)} %get-tuple-element.35), channel_id=1, source_target_pairs={{0,4},{4,0},{8,12},{12,8},{16,20},{20,16},{24,28},{28,24},{1,5},{5... | collective-permute-start | bytes 196616 | tf_op jit(solution)/shard_map/ppermute | solution.py:248
  12.7 5.0 %collective-permute-start.7 = (f32[128,128]{1,0:T(8,128)S(1)}, f32[128,128]{1,0:T(8,128)S(1)}, u32[]{:S(2)}, u32[]{:S(2)}) collective-permute-start(f32[128,128]{1,0:T(8,128)S(1)} %get-tuple-element.33), channel_id=1, source_target_pairs={{0,28},{4,24},{8,20},{12,16},{16,12},{20,8},{24,4},{28,0},{1,29},{... | collective-permute-start | bytes 196616 | tf_op jit(solution)/shard_map/ppermute | solution.py:248
  15.3 4.1 %collective-permute-start.10 = (f32[128,128]{1,0:T(8,128)S(1)}, f32[128,128]{1,0:T(8,128)S(1)}, u32[]{:S(2)}, u32[]{:S(2)}) collective-permute-start(f32[128,128]{1,0:T(8,128)S(1)} %get-tuple-element.36), channel_id=1, source_target_pairs={{0,12},{4,8},{8,4},{12,0},{16,28},{20,24},{24,20},{28,16},{1,13},{... | collective-permute-start | bytes 196616 | tf_op jit(solution)/shard_map/ppermute | solution.py:248
  15.5 4.0 %collective-permute-start.11 = (f32[128,128]{1,0:T(8,128)S(1)}, f32[128,128]{1,0:T(8,128)S(1)}, u32[]{:S(2)}, u32[]{:S(2)}) collective-permute-start(f32[128,128]{1,0:T(8,128)S(1)} %get-tuple-element.37), channel_id=1, source_target_pairs={{0,20},{4,16},{8,28},{12,24},{16,4},{20,0},{24,12},{28,8},{1,21},{... | collective-permute-start | bytes 196616 | tf_op jit(solution)/shard_map/ppermute | solution.py:248
  16.8 1.2 %collective-permute-start.6 = (f32[64,128]{1,0:T(8,128)S(1)}, f32[64,128]{1,0:T(8,128)S(1)}, u32[]{:S(2)}, u32[]{:S(2)}) collective-permute-start(f32[64,128]{1,0:T(8,128)S(1)} %get-tuple-element.32), channel_id=1, source_target_pairs={{0,4},{4,0},{8,12},{12,8},{16,20},{20,16},{24,28},{28,24},{1,5},{5... | collective-permute-start | bytes 98312 | tf_op jit(solution)/shard_map/ppermute | solution.py:248
  17.7 1.2 %collective-permute-start.8 = (f32[64,128]{1,0:T(8,128)S(1)}, f32[64,128]{1,0:T(8,128)S(1)}, u32[]{:S(2)}, u32[]{:S(2)}) collective-permute-start(f32[64,128]{1,0:T(8,128)S(1)} %second_half.3), channel_id=1, source_target_pairs={{0,4},{4,0},{8,12},{12,8},{16,20},{20,16},{24,28},{28,24},{1,5},{5... | collective-permute-start | bytes 98312 | tf_op jit(solution)/shard_map/ppermute | solution.py:248

commit v8 on v6

--- a/solution.py
+++ b/solution.py
@@ -22,18 +22,20 @@
     return high, low
 
 
-def tables(length, parts, joined):
+def tables(length, devices, parts, joined):
     rows = length // LANES
     k = np.arange(rows)[:, None] + 0.25
     r = np.arange(rows)[None, :]
     outer = 2 * np.pi * k * r / rows
     stacked = np.stack([np.cos(outer), -np.sin(outer)])
     first = stacked.reshape(2, parts, rows // parts, rows).swapaxes(0, 1).reshape(2 * rows, rows)
-    high, low = (t.reshape(2 * rows, 2, 2, rows // 4) for t in halves(first))
+    high, low = (t.reshape(2 * rows, devices, rows // devices) for t in halves(first))
     first = []
-    for diagonal in ((0, 0), (1, 1)), ((0, 1), (1, 0)):
-        cut_high, cut_low = (np.concatenate([t[:, y, x] for y, x in diagonal], axis=1) for t in (high, low))
-        first.append(np.concatenate([cut_high, cut_high, cut_low], axis=1))
+    for me in range(devices):
+        _, _, ((far, far_others), (one, _), (two, _)) = route(PLANS[0], me)
+        for came in (me, me ^ 1, far, far_others), (one, one ^ 1, two, two ^ 1):
+            first.append(np.concatenate([t[:, device] for t in (high, high, low) for device in came], axis=1))
+    first = np.stack(first).reshape(devices, 2, 2 * rows, -1)
     last = (stacked / length).reshape(2, joined, rows // joined, rows).transpose(1, 3, 0, 2)
     last = last.reshape(joined, rows, 2 * rows // joined)
     lane = np.arange(LANES)
@@ -42,7 +44,7 @@
     inner = 2 * np.pi * (lane[:, None] * lane[None, :] % LANES) / LANES
     cos2, sin2 = np.cos(inner), np.sin(inner)
     into = np.block([[cos2, -sin2], [sin2, cos2]])
-    return np.stack(first), np.stack(halves(last)), np.stack(halves(into)), twiddle
+    return first, np.stack(halves(last)), np.stack(halves(into)), twiddle
 
 
 def split(x):
@@ -69,8 +71,8 @@
     return x[i * m:(i + 1) * m, :LANES], x[i * m:(i + 1) * m, LANES:]
 
 
-def route(plan):
-    me = lax.axis_index("context")
+def route(plan, me=None):
+    me = lax.axis_index("context") if me is None else me
     core = me % 2
     to, from_ = [], []
     for even, odd in plan:
@@ -104,10 +106,6 @@
     out[...] = x[out.shape[0]:, :]
 
 
-def slot(device):
-    return (device >> 1 ^ device >> 2) & 1, (device >> 2) * 2 + (device & 1)
-
-
 def unpack(pieces, held):
     step = held.shape[1]
     for ref, at, place in pieces:
@@ -126,23 +124,23 @@
     return (first, 0, first_from), (first, 1, first_from ^ 1), (second, 0, second_from), (second, 1, second_from ^ 1)
 
 
-def outer_stage(came, held, table):
-    unpack([(ref, at, slot(device)[1]) for ref, at, device in came], held)
-    diagonal = slot(came[0][2])[0]
-    half, chunks = 4 * held.shape[1] // 3, held.shape[1] // 3
-    whole = [held[:, i * chunks:(i + 1) * chunks, :].reshape(half, LANES) for i in range(3)]
+def outer_stage(came, step, table):
+    half, chunks = 4 * step // 3, step // 3
+    whole = []
+    for i in range(3):
+        whole.append(jnp.concatenate([ref[at * step + i * chunks:at * step + (i + 1) * chunks, :] for ref, at, _ in came]))
     high, low = split(jnp.concatenate(whole, axis=1))
     both = jnp.concatenate([high, low], axis=0)
-    m = table.shape[1] // PARTS
+    m = table.shape[0] // PARTS
     sums = []
     for q in range(PARTS):
-        rows = pl.ds(q * m, m)
-        sums.append((dot(table[diagonal, rows, 2 * half:], high), dot(table[diagonal, rows, :2 * half], both)))
+        rows = slice(q * m, (q + 1) * m)
+        sums.append((dot(table[rows, 2 * half:], high), dot(table[rows, :2 * half], both)))
     return sums
 
 
-def early(own, aside, far, far_other, table, out, held):
-    sums = outer_stage(came_first(PLANS[0], (own, aside, far, far_other)), held, table)
+def early(own, aside, far, far_other, table, out):
+    sums = outer_stage(came_first(PLANS[0], (own, aside, far, far_other)), own.shape[0], table.at[0])
     m = out.shape[0] // PARTS
     for q, (less, more) in enumerate(sums):
         out[q * m:(q + 1) * m, :] = less + more
@@ -150,7 +148,8 @@
 
 def fetch(*refs):
     count = (len(refs) - 2) // 2
-    copies = [pltpu.make_async_copy(refs[i], refs[count + 1 + i], refs[-1].at[i]) for i in range(count)]
+    sources = [refs[0].at[lax.axis_index("context")], *refs[1:count]]
+    copies = [pltpu.make_async_copy(sources[i], refs[count + 1 + i], refs[-1].at[i]) for i in range(count)]
     for copy in copies:
         copy.start()
     for copy in copies:
@@ -181,12 +180,12 @@
 
 
 def transform(*refs):
-    got, (begun, first, last, into, twiddle), outs, (held, y) = refs[:2], refs[2:7], refs[7:11], refs[11:]
+    got, (begun, first, last, into, twiddle), outs, (y,) = refs[:2], refs[2:7], refs[7:11], refs[11:]
     n, chunks = y.shape[0], y.shape[1] // 2
     rows = n * chunks
     m = rows // PARTS
     turns = [lanes_of(twiddle, q, m) for q in range(PARTS)]
-    sums = outer_stage(came_last(PLANS[0], got), held, first)
+    sums = outer_stage(came_last(PLANS[0], got), got[0].shape[0] // 2, first.at[1])
     outer = [(begun[2 * m * q:2 * m * (q + 1), :] + less) + more for q, (less, more) in enumerate(sums)]
     spectra = []
     for z, (c, s) in zip(outer, turns):
@@ -261,19 +260,18 @@
         (half,) = call(second_half, [far, *made[:1]], [((step, LANES), kind)])
         return [own, aside, far, swap(half, 1, 1), first, second, *made]
 
-    held = [jnp.asarray(t) for t in tables(n * block, PARTS, JOINED)]
+    held = [jnp.asarray(t) for t in tables(n * block, n, PARTS, JOINED)]
 
     def bring(after):
-        return call(fetch, [*held, after], [(t.shape, t.dtype) for t in held], [pltpu.SemaphoreType.DMA((len(held),))], len(held))
+        return call(fetch, [*held, after], [(t.shape[1:] if t is held[0] else t.shape, t.dtype) for t in held], [pltpu.SemaphoreType.DMA((len(held),))], len(held))
 
     near = [pltpu.VMEM((channels, block), kind)] * 3
     near += [pltpu.VMEM((channels, 3 * chunks, LANES), kind), pltpu.SemaphoreType.DMA((3 * LOADS,))]
     sent = call(spread, [inputs, grads, response], sizes(3), near, 3)
     got = exchange(PLANS[0], *sent, meanwhile=bring)
-    near = [pltpu.VMEM((n // 2, 3 * chunks, LANES), kind)]
-    (begun,) = call(early, [*got[:4], got[6]], [((2 * n * chunks, 3 * LANES), kind)], near)
+    (begun,) = call(early, [*got[:4], got[6]], [((2 * n * chunks, 3 * LANES), kind)])
     pieces = [pltpu.VMEM((n, 2 * chunks, LANES), kind)]
-    got = exchange(PLANS[1], *call(transform, [*got[4:6], begun, *got[6:]], sizes(2), near + pieces))
+    got = exchange(PLANS[1], *call(transform, [*got[4:6], begun, *got[6:]], sizes(2), pieces))
     return call(gather, got, [((channels, block), kind)] * 2, pieces, near_out=False)
 
 

time: 20.5 us -> 20.4 us (level)
  no operation moved by 1% of the time
where the time goes in v8:
time: 20.4 us; the launch traced here: 20.2 us
  starting transfers between devices  10.6 us (52%)
  Pallas kernels  5.03 us (25%)
  waiting for transfers between devices  3.94 us (19%)
  between operations  0.68 us (3%)
    ppermute x10, starting transfers between devices, swap(): lax.ppermute(x, 'context', [(i, i ^ (odd if i % 2 else even)) for i in ra...  10.6 us
    pallas_call x9, Pallas kernels, call(): pl.pallas_call(body, out_shape=[kind(shape, dtype) for shape, dtype in ou...  5.03 us
    ppermute x10, waiting for transfers between devices, swap(): lax.ppermute(x, 'context', [(i, i ^ (odd if i % 2 else even)) for i in ra...  3.94 us
  transfers between devices with their start and end apart: 10, of which 6 were waited for; matrix products, arithmetic and copies ran while one was open for 0% of the time, Pallas kernels for 9%

profile of v8, /device:TPU:0, one launch (start us, length us, event | category | flops | bytes accessed | tf_op | source)
XLA Modules:
  0.0 20.2 jit_solution(2905067484356480021)
XLA Ops:
  0.6 1.1 %spread.1 = (f32[96,128]{1,0:T(8,128)S(1)}, f32[192,128]{1,0:T(8,128)S(1)}, f32[288,128]{1,0:T(8,128)S(1)}, f32[192,128]{1,0:T(8,128)S(1)}) custom-call(f32[8,4096]{1,0:T(8,128)} %refs_0_.2, f32[8,4096]{1,0:T(8,128)} %refs_1_.2, f32[8,4096]{1,0:T(8,128)} %refs_2_.2), custom_call_target="tpu_custom_call" | custom-call | tf_op jit(solution)/shard_map/spread/pallas_call | solution.py:230
  1.7 0.5 %collective-permute-start = (f32[288,128]{1,0:T(8,128)S(1)}, f32[288,128]{1,0:T(8,128)S(1)}, u32[]{:S(2)}, u32[]{:S(2)}) collective-permute-start(f32[288,128]{1,0:T(8,128)S(1)} %get-tuple-element.19), channel_id=1, source_target_pairs={{0,4},{4,0},{8,12},{12,8},{16,20},{20,16},{24,28},{28,24},{1,5},{5... | collective-permute-start | bytes 442376 | tf_op jit(solution)/shard_map/ppermute | solution.py:248
  2.2 3.6 %collective-permute-start.3 = (f32[192,128]{1,0:T(8,128)S(1)}, f32[192,128]{1,0:T(8,128)S(1)}, u32[]{:S(2)}, u32[]{:S(2)}) collective-permute-start(f32[192,128]{1,0:T(8,128)S(1)} %get-tuple-element.23), channel_id=1, source_target_pairs={{0,28},{4,24},{8,20},{12,16},{16,12},{20,8},{24,4},{28,0},{1,29},{... | collective-permute-start | bytes 294920 | tf_op jit(solution)/shard_map/ppermute | solution.py:248
  5.8 0.0 collective-permute-done.aside
  5.8 0.3 %collective-permute-start.1 = (f32[192,128]{1,0:T(8,128)S(1)}, f32[192,128]{1,0:T(8,128)S(1)}, u32[]{:S(2)}, u32[]{:S(2)}) collective-permute-start(f32[192,128]{1,0:T(8,128)S(1)} %get-tuple-element.20), channel_id=1, source_target_pairs={{0,12},{4,8},{8,4},{12,0},{16,28},{20,24},{24,20},{28,16},{1,13},{... | collective-permute-start | bytes 294920 | tf_op jit(solution)/shard_map/ppermute | solution.py:248
  6.1 1.3 %collective-permute-start.2 = (f32[192,128]{1,0:T(8,128)S(1)}, f32[192,128]{1,0:T(8,128)S(1)}, u32[]{:S(2)}, u32[]{:S(2)}) collective-permute-start(f32[192,128]{1,0:T(8,128)S(1)} %get-tuple-element.21.refs_4_), channel_id=1, source_target_pairs={{0,20},{4,16},{8,28},{12,24},{16,4},{20,0},{24,12},{28,8},{1,21},{... | collective-permute-start | bytes 294920 | tf_op jit(solution)/shard_map/ppermute | solution.py:248
  7.4 1.5 %fetch.1 = (bf16[2,512,384]{2,1,0:T(8,128)(2,1)S(1)}, bf16[2,2,256,256]{3,2,1,0:T(8,128)(2,1)S(1)}, bf16[2,256,256]{2,1,0:T(8,128)(2,1)S(1)}, f32[256,256]{1,0:T(8,128)S(1)}) custom-call(bf16[8,2,512,384]{3,2,1,0:T(8,128)(2,1)} %constant.8.clone.refs_0_, bf16[2,2,256,256]{3,2,1,0:T(8,128)(2,1)} %constant.9.clone.refs_1_, ...), custom_call_target="tpu_custom_call" | custom-call | tf_op jit(solution)/shard_map/fetch/pallas_call | solution.py:230
  8.9 0.1 collective-permute-done.3.x.far
  8.9 0.3 %collective-permute-start.4 = (f32[96,128]{1,0:T(8,128)S(1)}, f32[96,128]{1,0:T(8,128)S(1)}, u32[]{:S(2)}, u32[]{:S(2)}) collective-permute-start(f32[96,128]{1,0:T(8,128)S(1)} %second_half.2), channel_id=1, source_target_pairs={{0,4},{4,0},{8,12},{12,8},{16,20},{20,16},{24,28},{28,24},{1,5},{5... | collective-permute-start | bytes 147464 | tf_op jit(solution)/shard_map/ppermute | solution.py:248
  9.2 1.0 %collective-permute-done.4.far_other = f32[96,128]{1,0:T(8,128)S(1)} collective-permute-done((f32[96,128]{1,0:T(8,128)S(1)}, f32[96,128]{1,0:T(8,128)S(1)}, u32[]{:S(2)}, u32[]{:S(2)}) %collective-permute-start.4) | collective-permute-done | bytes 49184 | tf_op jit(solution)/shard_map/ppermute | solution.py:248
  10.2 0.4 %early.1.refs_2_ = f32[512,384]{1,0:T(8,128)S(1)} custom-call(f32[96,128]{1,0:T(8,128)S(1)} %get-tuple-element.22.own, f32[288,128]{1,0:T(8,128)S(1)} %collective-permute-done.aside, f32[192,128]{1,0:T(8,128)S(1)} %collective-permute-done.3.x.far, f32[96,128]{1,0:T(8,128)S(1)} %collective-permute-done.4.far_other, ...), custom_call_target="tpu_custom_call" | custom-call | tf_op jit(solution)/shard_map/early/pallas_call | solution.py:230
  10.6 0.4 %collective-permute-done.1.refs_0_ = f32[192,128]{1,0:T(8,128)S(1)} collective-permute-done((f32[192,128]{1,0:T(8,128)S(1)}, f32[192,128]{1,0:T(8,128)S(1)}, u32[]{:S(2)}, u32[]{:S(2)}) %collective-permute-start.1) | collective-permute-done | bytes 98336 | tf_op jit(solution)/shard_map/ppermute | solution.py:248
  11.0 0.0 collective-permute-done.2.refs_1_
  11.0 1.3 %transform.1 = (f32[64,128]{1,0:T(8,128)S(1)}, f32[128,128]{1,0:T(8,128)S(1)}, f32[192,128]{1,0:T(8,128)S(1)}, f32[128,128]{1,0:T(8,128)S(1)}) custom-call(f32[192,128]{1,0:T(8,128)S(1)} %collective-permute-done.1.refs_0_, f32[192,128]{1,0:T(8,128)S(1)} %collective-permute-done.2.refs_1_, f32[512,384]{1,0:T(8,128)S(1)} %early.1.refs_2_, ...), custom_call_target="tpu_custom_call" | custom-call | tf_op jit(solution)/shard_map/transform/pallas_call | solution.py:230
  12.3 0.4 %collective-permute-start.5 = (f32[192,128]{1,0:T(8,128)S(1)}, f32[192,128]{1,0:T(8,128)S(1)}, u32[]{:S(2)}, u32[]{:S(2)}) collective-permute-start(f32[192,128]{1,0:T(8,128)S(1)} %get-tuple-element.29), channel_id=1, source_target_pairs={{0,4},{4,0},{8,12},{12,8},{16,20},{20,16},{24,28},{28,24},{1,5},{5... | collective-permute-start | bytes 294920 | tf_op jit(solution)/shard_map/ppermute | solution.py:248
  12.7 2.6 %collective-permute-start.6 = (f32[128,128]{1,0:T(8,128)S(1)}, f32[128,128]{1,0:T(8,128)S(1)}, u32[]{:S(2)}, u32[]{:S(2)}) collective-permute-start(f32[128,128]{1,0:T(8,128)S(1)} %get-tuple-element.30), channel_id=1, source_target_pairs={{0,28},{4,24},{8,20},{12,16},{16,12},{20,8},{24,4},{28,0},{1,29},{... | collective-permute-start | bytes 196616 | tf_op jit(solution)/shard_map/ppermute | solution.py:248
  15.3 0.0 collective-permute-done.5.aside.refs_1_
  15.3 0.2 %collective-permute-start.8 = (f32[128,128]{1,0:T(8,128)S(1)}, f32[128,128]{1,0:T(8,128)S(1)}, u32[]{:S(2)}, u32[]{:S(2)}) collective-permute-start(f32[128,128]{1,0:T(8,128)S(1)} %get-tuple-element.32), channel_id=1, source_target_pairs={{0,12},{4,8},{8,4},{12,0},{16,28},{20,24},{24,20},{28,16},{1,13},{... | collective-permute-start | bytes 196616 | tf_op jit(solution)/shard_map/ppermute | solution.py:248
  15.5 1.3 %collective-permute-start.9 = (f32[128,128]{1,0:T(8,128)S(1)}, f32[128,128]{1,0:T(8,128)S(1)}, u32[]{:S(2)}, u32[]{:S(2)}) collective-permute-start(f32[128,128]{1,0:T(8,128)S(1)} %get-tuple-element.33), channel_id=1, source_target_pairs={{0,20},{4,16},{8,28},{12,24},{16,4},{20,0},{24,12},{28,8},{1,21},{... | collective-permute-start | bytes 196616 | tf_op jit(solution)/shard_map/ppermute | solution.py:248
  16.8 0.9 %collective-permute-done.6.x.refs_2_ = f32[128,128]{1,0:T(8,128)S(1)} collective-permute-done((f32[128,128]{1,0:T(8,128)S(1)}, f32[128,128]{1,0:T(8,128)S(1)}, u32[]{:S(2)}, u32[]{:S(2)}) %collective-permute-start.6) | collective-permute-done | bytes 65568 | tf_op jit(solution)/shard_map/ppermute | solution.py:248
  17.7 0.1 collective-permute-start.7
  17.8 1.1 %collective-permute-done.7.refs_3_ = f32[64,128]{1,0:T(8,128)S(1)} collective-permute-done((f32[64,128]{1,0:T(8,128)S(1)}, f32[64,128]{1,0:T(8,128)S(1)}, u32[]{:S(2)}, u32[]{:S(2)}) %collective-permute-start.7) | collective-permute-done | bytes 32800 | tf_op jit(solution)/shard_map/ppermute | solution.py:248
  18.9 0.5 %collective-permute-done.8.refs_4_ = f32[128,128]{1,0:T(8,128)S(1)} collective-permute-done((f32[128,128]{1,0:T(8,128)S(1)}, f32[128,128]{1,0:T(8,128)S(1)}, u32[]{:S(2)}, u32[]{:S(2)}) %collective-permute-start.8) | collective-permute-done | bytes 65568 | tf_op jit(solution)/shard_map/ppermute | solution.py:248
  19.4 0.0 collective-permute-done.9.refs_5_
  19.5 0.8 %gather.1 = (f32[8,4096]{1,0:T(8,128)}, f32[8,4096]{1,0:T(8,128)}) custom-call(f32[64,128]{1,0:T(8,128)S(1)} %get-tuple-element.28.refs_0_, f32[192,128]{1,0:T(8,128)S(1)} %collective-permute-done.5.aside.refs_1_, f32[128,128]{1,0:T(8,128)S(1)} %collective-permute-done.6.x.refs_2_, f32[64,128]{1,0:T(8,128)S(1)} %collective-permute-done.7.refs_3_, ...), custom_call_target="tpu_custom_call" | custom-call | tf_op jit(solution)/shard_map/gather/pallas_call | solution.py:230
  (4 shorter events, 0.0 us)
Async XLA Ops:
  1.7 4.1 %collective-permute-start = (f32[288,128]{1,0:T(8,128)S(1)}, f32[288,128]{1,0:T(8,128)S(1)}, u32[]{:S(2)}, u32[]{:S(2)}) collective-permute-start(f32[288,128]{1,0:T(8,128)S(1)} %get-tuple-element.19), channel_id=1, source_target_pairs={{0,4},{4,0},{8,12},{12,8},{16,20},{20,16},{24,28},{28,24},{1,5},{5... | collective-permute-start | bytes 442376 | tf_op jit(solution)/shard_map/ppermute | solution.py:248
  2.2 6.7 %collective-permute-start.3 = (f32[192,128]{1,0:T(8,128)S(1)}, f32[192,128]{1,0:T(8,128)S(1)}, u32[]{:S(2)}, u32[]{:S(2)}) collective-permute-start(f32[192,128]{1,0:T(8,128)S(1)} %get-tuple-element.23), channel_id=1, source_target_pairs={{0,28},{4,24},{8,20},{12,16},{16,12},{20,8},{24,4},{28,0},{1,29},{... | collective-permute-start | bytes 294920 | tf_op jit(solution)/shard_map/ppermute | solution.py:248
  5.8 5.2 %collective-permute-start.1 = (f32[192,128]{1,0:T(8,128)S(1)}, f32[192,128]{1,0:T(8,128)S(1)}, u32[]{:S(2)}, u32[]{:S(2)}) collective-permute-start(f32[192,128]{1,0:T(8,128)S(1)} %get-tuple-element.20), channel_id=1, source_target_pairs={{0,12},{4,8},{8,4},{12,0},{16,28},{20,24},{24,20},{28,16},{1,13},{... | collective-permute-start | bytes 294920 | tf_op jit(solution)/shard_map/ppermute | solution.py:248
  6.1 4.9 %collective-permute-start.2 = (f32[192,128]{1,0:T(8,128)S(1)}, f32[192,128]{1,0:T(8,128)S(1)}, u32[]{:S(2)}, u32[]{:S(2)}) collective-permute-start(f32[192,128]{1,0:T(8,128)S(1)} %get-tuple-element.21.refs_4_), channel_id=1, source_target_pairs={{0,20},{4,16},{8,28},{12,24},{16,4},{20,0},{24,12},{28,8},{1,21},{... | collective-permute-start | bytes 294920 | tf_op jit(solution)/shard_map/ppermute | solution.py:248
  8.9 1.3 %collective-permute-start.4 = (f32[96,128]{1,0:T(8,128)S(1)}, f32[96,128]{1,0:T(8,128)S(1)}, u32[]{:S(2)}, u32[]{:S(2)}) collective-permute-start(f32[96,128]{1,0:T(8,128)S(1)} %second_half.2), channel_id=1, source_target_pairs={{0,4},{4,0},{8,12},{12,8},{16,20},{20,16},{24,28},{28,24},{1,5},{5... | collective-permute-start | bytes 147464 | tf_op jit(solution)/shard_map/ppermute | solution.py:248
  12.3 3.0 %collective-permute-start.5 = (f32[192,128]{1,0:T(8,128)S(1)}, f32[192,128]{1,0:T(8,128)S(1)}, u32[]{:S(2)}, u32[]{:S(2)}) collective-permute-start(f32[192,128]{1,0:T(8,128)S(1)} %get-tuple-element.29), channel_id=1, source_target_pairs={{0,4},{4,0},{8,12},{12,8},{16,20},{20,16},{24,28},{28,24},{1,5},{5... | collective-permute-start | bytes 294920 | tf_op jit(solution)/shard_map/ppermute | solution.py:248
  12.7 5.0 %collective-permute-start.6 = (f32[128,128]{1,0:T(8,128)S(1)}, f32[128,128]{1,0:T(8,128)S(1)}, u32[]{:S(2)}, u32[]{:S(2)}) collective-permute-start(f32[128,128]{1,0:T(8,128)S(1)} %get-tuple-element.30), channel_id=1, source_target_pairs={{0,28},{4,24},{8,20},{12,16},{16,12},{20,8},{24,4},{28,0},{1,29},{... | collective-permute-start | bytes 196616 | tf_op jit(solution)/shard_map/ppermute | solution.py:248
  15.3 4.1 %collective-permute-start.8 = (f32[128,128]{1,0:T(8,128)S(1)}, f32[128,128]{1,0:T(8,128)S(1)}, u32[]{:S(2)}, u32[]{:S(2)}) collective-permute-start(f32[128,128]{1,0:T(8,128)S(1)} %get-tuple-element.32), channel_id=1, source_target_pairs={{0,12},{4,8},{8,4},{12,0},{16,28},{20,24},{24,20},{28,16},{1,13},{... | collective-permute-start | bytes 196616 | tf_op jit(solution)/shard_map/ppermute | solution.py:248
  15.5 3.9 %collective-permute-start.9 = (f32[128,128]{1,0:T(8,128)S(1)}, f32[128,128]{1,0:T(8,128)S(1)}, u32[]{:S(2)}, u32[]{:S(2)}) collective-permute-start(f32[128,128]{1,0:T(8,128)S(1)} %get-tuple-element.33), channel_id=1, source_target_pairs={{0,20},{4,16},{8,28},{12,24},{16,4},{20,0},{24,12},{28,8},{1,21},{... | collective-permute-start | bytes 196616 | tf_op jit(solution)/shard_map/ppermute | solution.py:248
  17.7 1.2 %collective-permute-start.7 = (f32[64,128]{1,0:T(8,128)S(1)}, f32[64,128]{1,0:T(8,128)S(1)}, u32[]{:S(2)}, u32[]{:S(2)}) collective-permute-start(f32[64,128]{1,0:T(8,128)S(1)} %second_half.3), channel_id=1, source_target_pairs={{0,4},{4,0},{8,12},{12,8},{16,20},{20,16},{24,28},{28,24},{1,5},{5... | collective-permute-start | bytes 98312 | tf_op jit(solution)/shard_map/ppermute | solution.py:248

commit v9 on v8

--- a/solution.py
+++ b/solution.py
@@ -83,13 +83,12 @@
     return me, to, from_
 
 
-def pack(plan, pieces, own, far, aside, beside):
+def pack(plan, pieces, own, far, aside, beside, other):
     me, ((far_to, _), (first_to, first_aside), (second_to, second_aside)), _ = route(plan)
     step = own.shape[0]
     for out, at, device in (
-        (own, 0, me), (far, 0, far_to), (far, 1, far_to ^ 1),
-        (aside, 0, me ^ 1), (aside, 1, first_aside), (aside, 2, second_aside),
-        (beside, 0, first_to), (beside, 1, second_to),
+        (own, 0, me), (far, 0, far_to), (far, 1, far_to ^ 1), (aside, 0, first_aside), (aside, 1, second_aside),
+        (beside, 0, first_to), (beside, 1, second_to), (other, 0, me ^ 1),
     ):
         out[at * step:(at + 1) * step, :] = pieces[device]
 
@@ -98,7 +97,7 @@
     step = beside.shape[0] // 2
     for i, out in enumerate((first, second)):
         out[:step, :] = beside[i * step:(i + 1) * step, :]
-        out[step:, :] = aside[(i + 1) * step:(i + 2) * step, :]
+        out[step:, :] = aside[i * step:(i + 1) * step, :]
 
 
 def second_half(x, *rest):
@@ -114,8 +113,8 @@
 
 def came_first(plan, got):
     me, _, ((far_from, far_others), *_) = route(plan)
-    own, aside, far, far_other = got
-    return (own, 0, me), (aside, 0, me ^ 1), (far, 0, far_from), (far_other, 0, far_others)
+    own, other, far, handed = got
+    return (own, 0, me), (other, 0, me ^ 1), (far, 0, far_from), (handed, 0, far_others)
 
 
 def came_last(plan, got):
@@ -139,8 +138,8 @@
     return sums
 
 
-def early(own, aside, far, far_other, table, out):
-    sums = outer_stage(came_first(PLANS[0], (own, aside, far, far_other)), own.shape[0], table.at[0])
+def early(own, other, far, handed, table, out):
+    sums = outer_stage(came_first(PLANS[0], (own, other, far, handed)), own.shape[0], table.at[0])
     m = out.shape[0] // PARTS
     for q, (less, more) in enumerate(sums):
         out[q * m:(q + 1) * m, :] = less + more
@@ -157,7 +156,7 @@
 
 
 def spread(*refs):
-    signals, outs, near, (held, arrived) = refs[:3], refs[3:7], refs[7:10], refs[10:]
+    signals, outs, near, (held, arrived) = refs[:3], refs[3:8], refs[8:11], refs[11:]
     channels, block = signals[0].shape
     chunks = block // LANES
     width = block // LOADS
@@ -180,7 +179,7 @@
 
 
 def transform(*refs):
-    got, (begun, first, last, into, twiddle), outs, (y,) = refs[:2], refs[2:7], refs[7:11], refs[11:]
+    got, (begun, first, last, into, twiddle), outs, (y,) = refs[:2], refs[2:7], refs[7:12], refs[12:]
     n, chunks = y.shape[0], y.shape[1] // 2
     rows = n * chunks
     m = rows // PARTS
@@ -248,17 +247,17 @@
         return lax.ppermute(x, "context", [(i, i ^ (odd if i % 2 else even)) for i in range(n)])
 
     def sizes(arrays):
-        return [((u * arrays * chunks, LANES), kind) for u in (1, 2, 3, 2)]
-
-    def exchange(plan, own, far, aside, beside, meanwhile=lambda x: []):
+        return [((u * arrays * chunks, LANES), kind) for u in (1, 2, 2, 2, 1)]
+
+    def exchange(plan, own, far, aside, beside, other, meanwhile=lambda x: []):
         step = own.shape[0]
         aside = swap(aside, 1, 1)
         far = swap(far, *plan[0])
         first, second = call(merge, [beside, aside], [((2 * step, LANES), kind)] * 2)
         made = meanwhile(second)
         first, second = swap(first, *plan[1]), swap(second, *plan[2])
-        (half,) = call(second_half, [far, *made[:1]], [((step, LANES), kind)])
-        return [own, aside, far, swap(half, 1, 1), first, second, *made]
+        (handed,) = call(second_half, [far, *made[:1]], [((step, LANES), kind)])
+        return [own, swap(other, 1, 1), far, swap(handed, 1, 1), first, second, *made]
 
     held = [jnp.asarray(t) for t in tables(n * block, n, PARTS, JOINED)]
 

time: 20.4 us -> 20.4 us (level)
  waiting for transfers between devices: 3.94 us -> 3.59 us
  starting transfers between devices: 10.6 us -> 10.9 us
    ppermute x10 -> x12, waiting for transfers between devices: 3.94 us -> 3.59 us  [swap(): lax.ppermute(x, 'context', [(i, i ^ (odd if i % 2 else even)) for i in ra...]
    ppermute x10 -> x12, starting transfers between devices: 10.6 us -> 10.9 us  [swap(): lax.ppermute(x, 'context', [(i, i ^ (odd if i % 2 else even)) for i in ra...]
  transfers between devices with their start and end apart: 10 -> 12, of which waited for: 6 -> 6; matrix products, arithmetic and copies ran while one was open for 0% -> 0% of each run, Pallas kernels for 9% -> 9%
where the time goes in v9:
time: 20.4 us; the launch traced here: 20.2 us
  starting transfers between devices  10.9 us (53%)
  Pallas kernels  5.03 us (25%)
  waiting for transfers between devices  3.59 us (18%)
  between operations  0.69 us (3%)
    ppermute x12, starting transfers between devices, swap(): lax.ppermute(x, 'context', [(i, i ^ (odd if i % 2 else even)) for i in ra...  10.9 us
    pallas_call x9, Pallas kernels, call(): pl.pallas_call(body, out_shape=[kind(shape, dtype) for shape, dtype in ou...  5.03 us
    ppermute x12, waiting for transfers between devices, swap(): lax.ppermute(x, 'context', [(i, i ^ (odd if i % 2 else even)) for i in ra...  3.59 us
  transfers between devices with their start and end apart: 12, of which 6 were waited for; matrix products, arithmetic and copies ran while one was open for 0% of the time, Pallas kernels for 9%

profile of v9, /device:TPU:0, one launch (start us, length us, event | category | flops | bytes accessed | tf_op | source)
XLA Modules:
  0.0 20.2 jit_solution(17495949341852609645)
XLA Ops:
  0.6 1.1 %spread.1 = (f32[96,128]{1,0:T(8,128)S(1)}, f32[192,128]{1,0:T(8,128)S(1)}, f32[192,128]{1,0:T(8,128)S(1)}, f32[192,128]{1,0:T(8,128)S(1)}, f32[96,128]{1,0:T(8,128)S(1)}) custom-call(f32[8,4096]{1,0:T(8,128)} %refs_0_.2, f32[8,4096]{1,0:T(8,128)} %refs_1_.2, f32[8,4096]{1,0:T(8,128)} %refs_2_.2), custom_call_target="tpu_custom_call" | custom-call | tf_op jit(solution)/shard_map/spread/pallas_call | solution.py:229
  1.7 0.5 %collective-permute-start = (f32[192,128]{1,0:T(8,128)S(1)}, f32[192,128]{1,0:T(8,128)S(1)}, u32[]{:S(2)}, u32[]{:S(2)}) collective-permute-start(f32[192,128]{1,0:T(8,128)S(1)} %get-tuple-element.21), channel_id=1, source_target_pairs={{0,4},{4,0},{8,12},{12,8},{16,20},{20,16},{24,28},{28,24},{1,5},{5... | collective-permute-start | bytes 294920 | tf_op jit(solution)/shard_map/ppermute | solution.py:247
  2.2 3.6 %collective-permute-start.4 = (f32[192,128]{1,0:T(8,128)S(1)}, f32[192,128]{1,0:T(8,128)S(1)}, u32[]{:S(2)}, u32[]{:S(2)}) collective-permute-start(f32[192,128]{1,0:T(8,128)S(1)} %get-tuple-element.26), channel_id=1, source_target_pairs={{0,28},{4,24},{8,20},{12,16},{16,12},{20,8},{24,4},{28,0},{1,29},{... | collective-permute-start | bytes 294920 | tf_op jit(solution)/shard_map/ppermute | solution.py:247
  5.8 0.0 collective-permute-done.aside
  5.8 0.3 %collective-permute-start.1 = (f32[192,128]{1,0:T(8,128)S(1)}, f32[192,128]{1,0:T(8,128)S(1)}, u32[]{:S(2)}, u32[]{:S(2)}) collective-permute-start(f32[192,128]{1,0:T(8,128)S(1)} %get-tuple-element.22), channel_id=1, source_target_pairs={{0,12},{4,8},{8,4},{12,0},{16,28},{20,24},{24,20},{28,16},{1,13},{... | collective-permute-start | bytes 294920 | tf_op jit(solution)/shard_map/ppermute | solution.py:247
  6.1 1.2 %collective-permute-start.2 = (f32[192,128]{1,0:T(8,128)S(1)}, f32[192,128]{1,0:T(8,128)S(1)}, u32[]{:S(2)}, u32[]{:S(2)}) collective-permute-start(f32[192,128]{1,0:T(8,128)S(1)} %get-tuple-element.23.refs_4_), channel_id=1, source_target_pairs={{0,20},{4,16},{8,28},{12,24},{16,4},{20,0},{24,12},{28,8},{1,21},{... | collective-permute-start | bytes 294920 | tf_op jit(solution)/shard_map/ppermute | solution.py:247
  7.3 0.2 collective-permute-start.3
  7.5 1.5 %fetch.1 = (bf16[2,512,384]{2,1,0:T(8,128)(2,1)S(1)}, bf16[2,2,256,256]{3,2,1,0:T(8,128)(2,1)S(1)}, bf16[2,256,256]{2,1,0:T(8,128)(2,1)S(1)}, f32[256,256]{1,0:T(8,128)S(1)}) custom-call(bf16[8,2,512,384]{3,2,1,0:T(8,128)(2,1)} %constant.8.clone.refs_0_, bf16[2,2,256,256]{3,2,1,0:T(8,128)(2,1)} %constant.9.clone.refs_1_, ...), custom_call_target="tpu_custom_call" | custom-call | tf_op jit(solution)/shard_map/fetch/pallas_call | solution.py:229
  9.0 0.0 collective-permute-done.4.x.far
  9.0 0.4 %collective-permute-start.5 = (f32[96,128]{1,0:T(8,128)S(1)}, f32[96,128]{1,0:T(8,128)S(1)}, u32[]{:S(2)}, u32[]{:S(2)}) collective-permute-start(f32[96,128]{1,0:T(8,128)S(1)} %second_half.2), channel_id=1, source_target_pairs={{0,4},{4,0},{8,12},{12,8},{16,20},{20,16},{24,28},{28,24},{1,5},{5... | collective-permute-start | bytes 147464 | tf_op jit(solution)/shard_map/ppermute | solution.py:247
  9.4 0.0 collective-permute-done.3.other
  9.4 0.9 %collective-permute-done.5.handed = f32[96,128]{1,0:T(8,128)S(1)} collective-permute-done((f32[96,128]{1,0:T(8,128)S(1)}, f32[96,128]{1,0:T(8,128)S(1)}, u32[]{:S(2)}, u32[]{:S(2)}) %collective-permute-start.5) | collective-permute-done | bytes 49184 | tf_op jit(solution)/shard_map/ppermute | solution.py:247
  10.3 0.4 %early.1.refs_2_ = f32[512,384]{1,0:T(8,128)S(1)} custom-call(f32[96,128]{1,0:T(8,128)S(1)} %get-tuple-element.24.own, f32[96,128]{1,0:T(8,128)S(1)} %collective-permute-done.3.other, f32[192,128]{1,0:T(8,128)S(1)} %collective-permute-done.4.x.far, f32[96,128]{1,0:T(8,128)S(1)} %collective-permute-done.5.handed, ...), custom_call_target="tpu_custom_call" | custom-call | tf_op jit(solution)/shard_map/early/pallas_call | solution.py:229
  10.7 0.3 %collective-permute-done.1.refs_0_ = f32[192,128]{1,0:T(8,128)S(1)} collective-permute-done((f32[192,128]{1,0:T(8,128)S(1)}, f32[192,128]{1,0:T(8,128)S(1)}, u32[]{:S(2)}, u32[]{:S(2)}) %collective-permute-start.1) | collective-permute-done | bytes 98336 | tf_op jit(solution)/shard_map/ppermute | solution.py:247
  11.0 0.0 collective-permute-done.2.refs_1_
  11.0 1.3 %transform.1 = (f32[64,128]{1,0:T(8,128)S(1)}, f32[128,128]{1,0:T(8,128)S(1)}, f32[128,128]{1,0:T(8,128)S(1)}, f32[128,128]{1,0:T(8,128)S(1)}, f32[64,128]{1,0:T(8,128)S(1)}) custom-call(f32[192,128]{1,0:T(8,128)S(1)} %collective-permute-done.1.refs_0_, f32[192,128]{1,0:T(8,128)S(1)} %collective-permute-done.2.refs_1_, f32[512,384]{1,0:T(8,128)S(1)} %early.1.refs_2_, ...), custom_call_target="tpu_custom_call" | custom-call | tf_op jit(solution)/shard_map/transform/pallas_call | solution.py:229
  12.3 0.4 %collective-permute-start.9 = (f32[128,128]{1,0:T(8,128)S(1)}, f32[128,128]{1,0:T(8,128)S(1)}, u32[]{:S(2)}, u32[]{:S(2)}) collective-permute-start(f32[128,128]{1,0:T(8,128)S(1)} %get-tuple-element.35), channel_id=1, source_target_pairs={{0,4},{4,0},{8,12},{12,8},{16,20},{20,16},{24,28},{28,24},{1,5},{5... | collective-permute-start | bytes 196616 | tf_op jit(solution)/shard_map/ppermute | solution.py:247
  12.7 2.6 %collective-permute-start.7 = (f32[128,128]{1,0:T(8,128)S(1)}, f32[128,128]{1,0:T(8,128)S(1)}, u32[]{:S(2)}, u32[]{:S(2)}) collective-permute-start(f32[128,128]{1,0:T(8,128)S(1)} %get-tuple-element.33), channel_id=1, source_target_pairs={{0,28},{4,24},{8,20},{12,16},{16,12},{20,8},{24,4},{28,0},{1,29},{... | collective-permute-start | bytes 196616 | tf_op jit(solution)/shard_map/ppermute | solution.py:247
  15.3 0.0 collective-permute-done.9.aside
  15.3 0.2 collective-permute-start.10
  15.5 1.3 %collective-permute-start.11 = (f32[128,128]{1,0:T(8,128)S(1)}, f32[128,128]{1,0:T(8,128)S(1)}, u32[]{:S(2)}, u32[]{:S(2)}) collective-permute-start(f32[128,128]{1,0:T(8,128)S(1)} %get-tuple-element.37), channel_id=1, source_target_pairs={{0,20},{4,16},{8,28},{12,24},{16,4},{20,0},{24,12},{28,8},{1,21},{... | collective-permute-start | bytes 196616 | tf_op jit(solution)/shard_map/ppermute | solution.py:247
  16.8 0.2 collective-permute-start.6
  17.0 0.8 %collective-permute-done.7.x.refs_2_ = f32[128,128]{1,0:T(8,128)S(1)} collective-permute-done((f32[128,128]{1,0:T(8,128)S(1)}, f32[128,128]{1,0:T(8,128)S(1)}, u32[]{:S(2)}, u32[]{:S(2)}) %collective-permute-start.7) | collective-permute-done | bytes 65568 | tf_op jit(solution)/shard_map/ppermute | solution.py:247
  17.7 0.1 collective-permute-start.8
  17.8 0.2 %collective-permute-done.6.refs_1_ = f32[64,128]{1,0:T(8,128)S(1)} collective-permute-done((f32[64,128]{1,0:T(8,128)S(1)}, f32[64,128]{1,0:T(8,128)S(1)}, u32[]{:S(2)}, u32[]{:S(2)}) %collective-permute-start.6) | collective-permute-done | bytes 32800 | tf_op jit(solution)/shard_map/ppermute | solution.py:247
  18.0 0.9 %collective-permute-done.8.refs_3_ = f32[64,128]{1,0:T(8,128)S(1)} collective-permute-done((f32[64,128]{1,0:T(8,128)S(1)}, f32[64,128]{1,0:T(8,128)S(1)}, u32[]{:S(2)}, u32[]{:S(2)}) %collective-permute-start.8) | collective-permute-done | bytes 32800 | tf_op jit(solution)/shard_map/ppermute | solution.py:247
  18.9 0.5 %collective-permute-done.10.refs_4_ = f32[128,128]{1,0:T(8,128)S(1)} collective-permute-done((f32[128,128]{1,0:T(8,128)S(1)}, f32[128,128]{1,0:T(8,128)S(1)}, u32[]{:S(2)}, u32[]{:S(2)}) %collective-permute-start.10) | collective-permute-done | bytes 65568 | tf_op jit(solution)/shard_map/ppermute | solution.py:247
  19.4 0.0 collective-permute-done.11.refs_5_
  19.4 0.8 %gather.1 = (f32[8,4096]{1,0:T(8,128)}, f32[8,4096]{1,0:T(8,128)}) custom-call(f32[64,128]{1,0:T(8,128)S(1)} %get-tuple-element.31.refs_0_, f32[64,128]{1,0:T(8,128)S(1)} %collective-permute-done.6.refs_1_, f32[128,128]{1,0:T(8,128)S(1)} %collective-permute-done.7.x.refs_2_, f32[64,128]{1,0:T(8,128)S(1)} %collective-permute-done.8.refs_3_, ...), custom_call_target="tpu_custom_call" | custom-call | tf_op jit(solution)/shard_map/gather/pallas_call | solution.py:229
  (4 shorter events, 0.0 us)
Async XLA Ops:
  1.7 4.1 %collective-permute-start = (f32[192,128]{1,0:T(8,128)S(1)}, f32[192,128]{1,0:T(8,128)S(1)}, u32[]{:S(2)}, u32[]{:S(2)}) collective-permute-start(f32[192,128]{1,0:T(8,128)S(1)} %get-tuple-element.21), channel_id=1, source_target_pairs={{0,4},{4,0},{8,12},{12,8},{16,20},{20,16},{24,28},{28,24},{1,5},{5... | collective-permute-start | bytes 294920 | tf_op jit(solution)/shard_map/ppermute | solution.py:247
  2.2 6.7 %collective-permute-start.4 = (f32[192,128]{1,0:T(8,128)S(1)}, f32[192,128]{1,0:T(8,128)S(1)}, u32[]{:S(2)}, u32[]{:S(2)}) collective-permute-start(f32[192,128]{1,0:T(8,128)S(1)} %get-tuple-element.26), channel_id=1, source_target_pairs={{0,28},{4,24},{8,20},{12,16},{16,12},{20,8},{24,4},{28,0},{1,29},{... | collective-permute-start | bytes 294920 | tf_op jit(solution)/shard_map/ppermute | solution.py:247
  5.8 5.2 %collective-permute-start.1 = (f32[192,128]{1,0:T(8,128)S(1)}, f32[192,128]{1,0:T(8,128)S(1)}, u32[]{:S(2)}, u32[]{:S(2)}) collective-permute-start(f32[192,128]{1,0:T(8,128)S(1)} %get-tuple-element.22), channel_id=1, source_target_pairs={{0,12},{4,8},{8,4},{12,0},{16,28},{20,24},{24,20},{28,16},{1,13},{... | collective-permute-start | bytes 294920 | tf_op jit(solution)/shard_map/ppermute | solution.py:247
  6.1 4.9 %collective-permute-start.2 = (f32[192,128]{1,0:T(8,128)S(1)}, f32[192,128]{1,0:T(8,128)S(1)}, u32[]{:S(2)}, u32[]{:S(2)}) collective-permute-start(f32[192,128]{1,0:T(8,128)S(1)} %get-tuple-element.23.refs_4_), channel_id=1, source_target_pairs={{0,20},{4,16},{8,28},{12,24},{16,4},{20,0},{24,12},{28,8},{1,21},{... | collective-permute-start | bytes 294920 | tf_op jit(solution)/shard_map/ppermute | solution.py:247
  7.3 2.1 %collective-permute-start.3 = (f32[96,128]{1,0:T(8,128)S(1)}, f32[96,128]{1,0:T(8,128)S(1)}, u32[]{:S(2)}, u32[]{:S(2)}) collective-permute-start(f32[96,128]{1,0:T(8,128)S(1)} %get-tuple-element.25), channel_id=1, source_target_pairs={{0,4},{4,0},{8,12},{12,8},{16,20},{20,16},{24,28},{28,24},{1,5},{5... | collective-permute-start | bytes 147464 | tf_op jit(solution)/shard_map/ppermute | solution.py:247
  9.0 1.3 %collective-permute-start.5 = (f32[96,128]{1,0:T(8,128)S(1)}, f32[96,128]{1,0:T(8,128)S(1)}, u32[]{:S(2)}, u32[]{:S(2)}) collective-permute-start(f32[96,128]{1,0:T(8,128)S(1)} %second_half.2), channel_id=1, source_target_pairs={{0,4},{4,0},{8,12},{12,8},{16,20},{20,16},{24,28},{28,24},{1,5},{5... | collective-permute-start | bytes 147464 | tf_op jit(solution)/shard_map/ppermute | solution.py:247
  12.3 3.0 %collective-permute-start.9 = (f32[128,128]{1,0:T(8,128)S(1)}, f32[128,128]{1,0:T(8,128)S(1)}, u32[]{:S(2)}, u32[]{:S(2)}) collective-permute-start(f32[128,128]{1,0:T(8,128)S(1)} %get-tuple-element.35), channel_id=1, source_target_pairs={{0,4},{4,0},{8,12},{12,8},{16,20},{20,16},{24,28},{28,24},{1,5},{5... | collective-permute-start | bytes 196616 | tf_op jit(solution)/shard_map/ppermute | solution.py:247
  12.7 5.0 %collective-permute-start.7 = (f32[128,128]{1,0:T(8,128)S(1)}, f32[128,128]{1,0:T(8,128)S(1)}, u32[]{:S(2)}, u32[]{:S(2)}) collective-permute-start(f32[128,128]{1,0:T(8,128)S(1)} %get-tuple-element.33), channel_id=1, source_target_pairs={{0,28},{4,24},{8,20},{12,16},{16,12},{20,8},{24,4},{28,0},{1,29},{... | collective-permute-start | bytes 196616 | tf_op jit(solution)/shard_map/ppermute | solution.py:247
  15.3 4.1 %collective-permute-start.10 = (f32[128,128]{1,0:T(8,128)S(1)}, f32[128,128]{1,0:T(8,128)S(1)}, u32[]{:S(2)}, u32[]{:S(2)}) collective-permute-start(f32[128,128]{1,0:T(8,128)S(1)} %get-tuple-element.36), channel_id=1, source_target_pairs={{0,12},{4,8},{8,4},{12,0},{16,28},{20,24},{24,20},{28,16},{1,13},{... | collective-permute-start | bytes 196616 | tf_op jit(solution)/shard_map/ppermute | solution.py:247
  15.5 4.0 %collective-permute-start.11 = (f32[128,128]{1,0:T(8,128)S(1)}, f32[128,128]{1,0:T(8,128)S(1)}, u32[]{:S(2)}, u32[]{:S(2)}) collective-permute-start(f32[128,128]{1,0:T(8,128)S(1)} %get-tuple-element.37), channel_id=1, source_target_pairs={{0,20},{4,16},{8,28},{12,24},{16,4},{20,0},{24,12},{28,8},{1,21},{... | collective-permute-start | bytes 196616 | tf_op jit(solution)/shard_map/ppermute | solution.py:247
  16.8 1.2 %collective-permute-start.6 = (f32[64,128]{1,0:T(8,128)S(1)}, f32[64,128]{1,0:T(8,128)S(1)}, u32[]{:S(2)}, u32[]{:S(2)}) collective-permute-start(f32[64,128]{1,0:T(8,128)S(1)} %get-tuple-element.32), channel_id=1, source_target_pairs={{0,4},{4,0},{8,12},{12,8},{16,20},{20,16},{24,28},{28,24},{1,5},{5... | collective-permute-start | bytes 98312 | tf_op jit(solution)/shard_map/ppermute | solution.py:247
  17.7 1.2 %collective-permute-start.8 = (f32[64,128]{1,0:T(8,128)S(1)}, f32[64,128]{1,0:T(8,128)S(1)}, u32[]{:S(2)}, u32[]{:S(2)}) collective-permute-start(f32[64,128]{1,0:T(8,128)S(1)} %second_half.3), channel_id=1, source_target_pairs={{0,4},{4,0},{8,12},{12,8},{16,20},{20,16},{24,28},{28,24},{1,5},{5... | collective-permute-start | bytes 98312 | tf_op jit(solution)/shard_map/ppermute | solution.py:247

commit v10 on v6

--- a/solution.py
+++ b/solution.py
@@ -11,7 +11,7 @@
 
 LANES = 128
 BF = jnp.bfloat16
-PARTS, JOINED, LOADS = 4, 2, 4
+PARTS, JOINED, LOADS = 4, 2, 1
 PLANS = ((7, 7), (3, 3), (5, 5)), ((7, 7), (3, 3), (5, 5))
 
 

time: 20.5 us -> 20.4 us (level)
  no operation moved by 1% of the time
where the time goes in v10:
time: 20.4 us; the launch traced here: 20.3 us
  starting transfers between devices  10.6 us (52%)
  Pallas kernels  5.11 us (25%)
  waiting for transfers between devices  3.91 us (19%)
  between operations  0.68 us (3%)
    ppermute x10, starting transfers between devices, swap(): lax.ppermute(x, 'context', [(i, i ^ (odd if i % 2 else even)) for i in ra...  10.6 us
    pallas_call x9, Pallas kernels, call(): pl.pallas_call(body, out_shape=[kind(shape, dtype) for shape, dtype in ou...  5.11 us
    ppermute x10, waiting for transfers between devices, swap(): lax.ppermute(x, 'context', [(i, i ^ (odd if i % 2 else even)) for i in ra...  3.91 us
  transfers between devices with their start and end apart: 10, of which 6 were waited for; matrix products, arithmetic and copies ran while one was open for 0% of the time, Pallas kernels for 9%

profile of v10, /device:TPU:0, one launch (start us, length us, event | category | flops | bytes accessed | tf_op | source)
XLA Modules:
  0.0 20.3 jit_solution(3184556745347319879)
XLA Ops:
  0.6 1.1 %spread.1 = (f32[96,128]{1,0:T(8,128)S(1)}, f32[192,128]{1,0:T(8,128)S(1)}, f32[288,128]{1,0:T(8,128)S(1)}, f32[192,128]{1,0:T(8,128)S(1)}) custom-call(f32[8,4096]{1,0:T(8,128)} %refs_0_.2, f32[8,4096]{1,0:T(8,128)} %refs_1_.2, f32[8,4096]{1,0:T(8,128)} %refs_2_.2), custom_call_target="tpu_custom_call" | custom-call | tf_op jit(solution)/shard_map/spread/pallas_call | solution.py:231
  1.7 0.5 %collective-permute-start = (f32[288,128]{1,0:T(8,128)S(1)}, f32[288,128]{1,0:T(8,128)S(1)}, u32[]{:S(2)}, u32[]{:S(2)}) collective-permute-start(f32[288,128]{1,0:T(8,128)S(1)} %get-tuple-element.19), channel_id=1, source_target_pairs={{0,4},{4,0},{8,12},{12,8},{16,20},{20,16},{24,28},{28,24},{1,5},{5... | collective-permute-start | bytes 442376 | tf_op jit(solution)/shard_map/ppermute | solution.py:249
  2.3 3.6 %collective-permute-start.3 = (f32[192,128]{1,0:T(8,128)S(1)}, f32[192,128]{1,0:T(8,128)S(1)}, u32[]{:S(2)}, u32[]{:S(2)}) collective-permute-start(f32[192,128]{1,0:T(8,128)S(1)} %get-tuple-element.23), channel_id=1, source_target_pairs={{0,28},{4,24},{8,20},{12,16},{16,12},{20,8},{24,4},{28,0},{1,29},{... | collective-permute-start | bytes 294920 | tf_op jit(solution)/shard_map/ppermute | solution.py:249
  5.8 0.0 collective-permute-done.aside
  5.9 0.3 %collective-permute-start.1 = (f32[192,128]{1,0:T(8,128)S(1)}, f32[192,128]{1,0:T(8,128)S(1)}, u32[]{:S(2)}, u32[]{:S(2)}) collective-permute-start(f32[192,128]{1,0:T(8,128)S(1)} %get-tuple-element.20), channel_id=1, source_target_pairs={{0,12},{4,8},{8,4},{12,0},{16,28},{20,24},{24,20},{28,16},{1,13},{... | collective-permute-start | bytes 294920 | tf_op jit(solution)/shard_map/ppermute | solution.py:249
  6.1 1.3 %collective-permute-start.2 = (f32[192,128]{1,0:T(8,128)S(1)}, f32[192,128]{1,0:T(8,128)S(1)}, u32[]{:S(2)}, u32[]{:S(2)}) collective-permute-start(f32[192,128]{1,0:T(8,128)S(1)} %get-tuple-element.21.refs_4_), channel_id=1, source_target_pairs={{0,20},{4,16},{8,28},{12,24},{16,4},{20,0},{24,12},{28,8},{1,21},{... | collective-permute-start | bytes 294920 | tf_op jit(solution)/shard_map/ppermute | solution.py:249
  7.4 1.5 %fetch.1 = (bf16[2,512,384]{2,1,0:T(8,128)(2,1)S(1)}, bf16[2,2,256,256]{3,2,1,0:T(8,128)(2,1)S(1)}, bf16[2,256,256]{2,1,0:T(8,128)(2,1)S(1)}, f32[256,256]{1,0:T(8,128)S(1)}) custom-call(bf16[2,512,384]{2,1,0:T(8,128)(2,1)} %constant.8.clone.refs_0_, bf16[2,2,256,256]{3,2,1,0:T(8,128)(2,1)} %constant.9.clone.refs_1_, ...), custom_call_target="tpu_custom_call" | custom-call | tf_op jit(solution)/shard_map/fetch/pallas_call | solution.py:231
  8.9 0.1 collective-permute-done.3.x.far
  9.0 0.3 %collective-permute-start.4 = (f32[96,128]{1,0:T(8,128)S(1)}, f32[96,128]{1,0:T(8,128)S(1)}, u32[]{:S(2)}, u32[]{:S(2)}) collective-permute-start(f32[96,128]{1,0:T(8,128)S(1)} %second_half.2), channel_id=1, source_target_pairs={{0,4},{4,0},{8,12},{12,8},{16,20},{20,16},{24,28},{28,24},{1,5},{5... | collective-permute-start | bytes 147464 | tf_op jit(solution)/shard_map/ppermute | solution.py:249
  9.3 1.0 %collective-permute-done.4.far_other = f32[96,128]{1,0:T(8,128)S(1)} collective-permute-done((f32[96,128]{1,0:T(8,128)S(1)}, f32[96,128]{1,0:T(8,128)S(1)}, u32[]{:S(2)}, u32[]{:S(2)}) %collective-permute-start.4) | collective-permute-done | bytes 49184 | tf_op jit(solution)/shard_map/ppermute | solution.py:249
  10.2 0.4 %early.1.refs_2_ = f32[512,384]{1,0:T(8,128)S(1)} custom-call(f32[96,128]{1,0:T(8,128)S(1)} %get-tuple-element.22.own, f32[288,128]{1,0:T(8,128)S(1)} %collective-permute-done.aside, f32[192,128]{1,0:T(8,128)S(1)} %collective-permute-done.3.x.far, f32[96,128]{1,0:T(8,128)S(1)} %collective-permute-done.4.far_other, ...), custom_call_target="tpu_custom_call" | custom-call | tf_op jit(solution)/shard_map/early/pallas_call | solution.py:231
  10.7 0.4 %collective-permute-done.1.refs_0_ = f32[192,128]{1,0:T(8,128)S(1)} collective-permute-done((f32[192,128]{1,0:T(8,128)S(1)}, f32[192,128]{1,0:T(8,128)S(1)}, u32[]{:S(2)}, u32[]{:S(2)}) %collective-permute-start.1) | collective-permute-done | bytes 98336 | tf_op jit(solution)/shard_map/ppermute | solution.py:249
  11.0 0.0 collective-permute-done.2.refs_1_
  11.0 1.3 %transform.1 = (f32[64,128]{1,0:T(8,128)S(1)}, f32[128,128]{1,0:T(8,128)S(1)}, f32[192,128]{1,0:T(8,128)S(1)}, f32[128,128]{1,0:T(8,128)S(1)}) custom-call(f32[192,128]{1,0:T(8,128)S(1)} %collective-permute-done.1.refs_0_, f32[192,128]{1,0:T(8,128)S(1)} %collective-permute-done.2.refs_1_, f32[512,384]{1,0:T(8,128)S(1)} %early.1.refs_2_, ...), custom_call_target="tpu_custom_call" | custom-call | tf_op jit(solution)/shard_map/transform/pallas_call | solution.py:231
  12.4 0.4 %collective-permute-start.5 = (f32[192,128]{1,0:T(8,128)S(1)}, f32[192,128]{1,0:T(8,128)S(1)}, u32[]{:S(2)}, u32[]{:S(2)}) collective-permute-start(f32[192,128]{1,0:T(8,128)S(1)} %get-tuple-element.29), channel_id=1, source_target_pairs={{0,4},{4,0},{8,12},{12,8},{16,20},{20,16},{24,28},{28,24},{1,5},{5... | collective-permute-start | bytes 294920 | tf_op jit(solution)/shard_map/ppermute | solution.py:249
  12.7 2.6 %collective-permute-start.6 = (f32[128,128]{1,0:T(8,128)S(1)}, f32[128,128]{1,0:T(8,128)S(1)}, u32[]{:S(2)}, u32[]{:S(2)}) collective-permute-start(f32[128,128]{1,0:T(8,128)S(1)} %get-tuple-element.30), channel_id=1, source_target_pairs={{0,28},{4,24},{8,20},{12,16},{16,12},{20,8},{24,4},{28,0},{1,29},{... | collective-permute-start | bytes 196616 | tf_op jit(solution)/shard_map/ppermute | solution.py:249
  15.4 0.0 collective-permute-done.5.aside.refs_1_
  15.4 0.2 collective-permute-start.8
  15.5 1.4 %collective-permute-start.9 = (f32[128,128]{1,0:T(8,128)S(1)}, f32[128,128]{1,0:T(8,128)S(1)}, u32[]{:S(2)}, u32[]{:S(2)}) collective-permute-start(f32[128,128]{1,0:T(8,128)S(1)} %get-tuple-element.33), channel_id=1, source_target_pairs={{0,20},{4,16},{8,28},{12,24},{16,4},{20,0},{24,12},{28,8},{1,21},{... | collective-permute-start | bytes 196616 | tf_op jit(solution)/shard_map/ppermute | solution.py:249
  16.9 0.9 %collective-permute-done.6.x.refs_2_ = f32[128,128]{1,0:T(8,128)S(1)} collective-permute-done((f32[128,128]{1,0:T(8,128)S(1)}, f32[128,128]{1,0:T(8,128)S(1)}, u32[]{:S(2)}, u32[]{:S(2)}) %collective-permute-start.6) | collective-permute-done | bytes 65568 | tf_op jit(solution)/shard_map/ppermute | solution.py:249
  17.8 0.1 collective-permute-start.7
  17.9 1.1 %collective-permute-done.7.refs_3_ = f32[64,128]{1,0:T(8,128)S(1)} collective-permute-done((f32[64,128]{1,0:T(8,128)S(1)}, f32[64,128]{1,0:T(8,128)S(1)}, u32[]{:S(2)}, u32[]{:S(2)}) %collective-permute-start.7) | collective-permute-done | bytes 32800 | tf_op jit(solution)/shard_map/ppermute | solution.py:249
  19.0 0.5 %collective-permute-done.8.refs_4_ = f32[128,128]{1,0:T(8,128)S(1)} collective-permute-done((f32[128,128]{1,0:T(8,128)S(1)}, f32[128,128]{1,0:T(8,128)S(1)}, u32[]{:S(2)}, u32[]{:S(2)}) %collective-permute-start.8) | collective-permute-done | bytes 65568 | tf_op jit(solution)/shard_map/ppermute | solution.py:249
  19.5 0.0 collective-permute-done.9.refs_5_
  19.5 0.8 %gather.1 = (f32[8,4096]{1,0:T(8,128)}, f32[8,4096]{1,0:T(8,128)}) custom-call(f32[64,128]{1,0:T(8,128)S(1)} %get-tuple-element.28.refs_0_, f32[192,128]{1,0:T(8,128)S(1)} %collective-permute-done.5.aside.refs_1_, f32[128,128]{1,0:T(8,128)S(1)} %collective-permute-done.6.x.refs_2_, f32[64,128]{1,0:T(8,128)S(1)} %collective-permute-done.7.refs_3_, ...), custom_call_target="tpu_custom_call" | custom-call | tf_op jit(solution)/shard_map/gather/pallas_call | solution.py:231
  (4 shorter events, 0.0 us)
Async XLA Ops:
  1.7 4.1 %collective-permute-start = (f32[288,128]{1,0:T(8,128)S(1)}, f32[288,128]{1,0:T(8,128)S(1)}, u32[]{:S(2)}, u32[]{:S(2)}) collective-permute-start(f32[288,128]{1,0:T(8,128)S(1)} %get-tuple-element.19), channel_id=1, source_target_pairs={{0,4},{4,0},{8,12},{12,8},{16,20},{20,16},{24,28},{28,24},{1,5},{5... | collective-permute-start | bytes 442376 | tf_op jit(solution)/shard_map/ppermute | solution.py:249
  2.3 6.7 %collective-permute-start.3 = (f32[192,128]{1,0:T(8,128)S(1)}, f32[192,128]{1,0:T(8,128)S(1)}, u32[]{:S(2)}, u32[]{:S(2)}) collective-permute-start(f32[192,128]{1,0:T(8,128)S(1)} %get-tuple-element.23), channel_id=1, source_target_pairs={{0,28},{4,24},{8,20},{12,16},{16,12},{20,8},{24,4},{28,0},{1,29},{... | collective-permute-start | bytes 294920 | tf_op jit(solution)/shard_map/ppermute | solution.py:249
  5.9 5.2 %collective-permute-start.1 = (f32[192,128]{1,0:T(8,128)S(1)}, f32[192,128]{1,0:T(8,128)S(1)}, u32[]{:S(2)}, u32[]{:S(2)}) collective-permute-start(f32[192,128]{1,0:T(8,128)S(1)} %get-tuple-element.20), channel_id=1, source_target_pairs={{0,12},{4,8},{8,4},{12,0},{16,28},{20,24},{24,20},{28,16},{1,13},{... | collective-permute-start | bytes 294920 | tf_op jit(solution)/shard_map/ppermute | solution.py:249
  6.1 4.9 %collective-permute-start.2 = (f32[192,128]{1,0:T(8,128)S(1)}, f32[192,128]{1,0:T(8,128)S(1)}, u32[]{:S(2)}, u32[]{:S(2)}) collective-permute-start(f32[192,128]{1,0:T(8,128)S(1)} %get-tuple-element.21.refs_4_), channel_id=1, source_target_pairs={{0,20},{4,16},{8,28},{12,24},{16,4},{20,0},{24,12},{28,8},{1,21},{... | collective-permute-start | bytes 294920 | tf_op jit(solution)/shard_map/ppermute | solution.py:249
  9.0 1.3 %collective-permute-start.4 = (f32[96,128]{1,0:T(8,128)S(1)}, f32[96,128]{1,0:T(8,128)S(1)}, u32[]{:S(2)}, u32[]{:S(2)}) collective-permute-start(f32[96,128]{1,0:T(8,128)S(1)} %second_half.2), channel_id=1, source_target_pairs={{0,4},{4,0},{8,12},{12,8},{16,20},{20,16},{24,28},{28,24},{1,5},{5... | collective-permute-start | bytes 147464 | tf_op jit(solution)/shard_map/ppermute | solution.py:249
  12.4 3.0 %collective-permute-start.5 = (f32[192,128]{1,0:T(8,128)S(1)}, f32[192,128]{1,0:T(8,128)S(1)}, u32[]{:S(2)}, u32[]{:S(2)}) collective-permute-start(f32[192,128]{1,0:T(8,128)S(1)} %get-tuple-element.29), channel_id=1, source_target_pairs={{0,4},{4,0},{8,12},{12,8},{16,20},{20,16},{24,28},{28,24},{1,5},{5... | collective-permute-start | bytes 294920 | tf_op jit(solution)/shard_map/ppermute | solution.py:249
  12.7 5.0 %collective-permute-start.6 = (f32[128,128]{1,0:T(8,128)S(1)}, f32[128,128]{1,0:T(8,128)S(1)}, u32[]{:S(2)}, u32[]{:S(2)}) collective-permute-start(f32[128,128]{1,0:T(8,128)S(1)} %get-tuple-element.30), channel_id=1, source_target_pairs={{0,28},{4,24},{8,20},{12,16},{16,12},{20,8},{24,4},{28,0},{1,29},{... | collective-permute-start | bytes 196616 | tf_op jit(solution)/shard_map/ppermute | solution.py:249
  15.4 4.1 %collective-permute-start.8 = (f32[128,128]{1,0:T(8,128)S(1)}, f32[128,128]{1,0:T(8,128)S(1)}, u32[]{:S(2)}, u32[]{:S(2)}) collective-permute-start(f32[128,128]{1,0:T(8,128)S(1)} %get-tuple-element.32), channel_id=1, source_target_pairs={{0,12},{4,8},{8,4},{12,0},{16,28},{20,24},{24,20},{28,16},{1,13},{... | collective-permute-start | bytes 196616 | tf_op jit(solution)/shard_map/ppermute | solution.py:249
  15.5 4.0 %collective-permute-start.9 = (f32[128,128]{1,0:T(8,128)S(1)}, f32[128,128]{1,0:T(8,128)S(1)}, u32[]{:S(2)}, u32[]{:S(2)}) collective-permute-start(f32[128,128]{1,0:T(8,128)S(1)} %get-tuple-element.33), channel_id=1, source_target_pairs={{0,20},{4,16},{8,28},{12,24},{16,4},{20,0},{24,12},{28,8},{1,21},{... | collective-permute-start | bytes 196616 | tf_op jit(solution)/shard_map/ppermute | solution.py:249
  17.8 1.2 %collective-permute-start.7 = (f32[64,128]{1,0:T(8,128)S(1)}, f32[64,128]{1,0:T(8,128)S(1)}, u32[]{:S(2)}, u32[]{:S(2)}) collective-permute-start(f32[64,128]{1,0:T(8,128)S(1)} %second_half.3), channel_id=1, source_target_pairs={{0,4},{4,0},{8,12},{12,8},{16,20},{20,16},{24,28},{28,24},{1,5},{5... | collective-permute-start | bytes 98312 | tf_op jit(solution)/shard_map/ppermute | solution.py:249

commit v11 on v7

--- a/solution.py
+++ b/solution.py
@@ -11,7 +11,7 @@
 
 LANES = 128
 BF = jnp.bfloat16
-PARTS, JOINED, LOADS = 4, 2, 4
+PARTS, JOINED, LOADS = 4, 2, 1
 PLANS = ((7, 7), (3, 3), (5, 5)), ((7, 7), (3, 3), (5, 5))
 
 

time: 20.5 us -> 20.4 us (level)
  no operation moved by 1% of the time
where the time goes in v11:
time: 20.4 us; the launch traced here: 20.3 us
  starting transfers between devices  10.9 us (53%)
  Pallas kernels  5.12 us (25%)
  waiting for transfers between devices  3.56 us (17%)
  between operations  0.69 us (3%)
    ppermute x12, starting transfers between devices, swap(): lax.ppermute(x, 'context', [(i, i ^ (odd if i % 2 else even)) for i in ra...  10.9 us
    pallas_call x9, Pallas kernels, call(): pl.pallas_call(body, out_shape=[kind(shape, dtype) for shape, dtype in ou...  5.12 us
    ppermute x12, waiting for transfers between devices, swap(): lax.ppermute(x, 'context', [(i, i ^ (odd if i % 2 else even)) for i in ra...  3.56 us
  transfers between devices with their start and end apart: 12, of which 6 were waited for; matrix products, arithmetic and copies ran while one was open for 0% of the time, Pallas kernels for 9%

profile of v11, /device:TPU:0, one launch (start us, length us, event | category | flops | bytes accessed | tf_op | source)
XLA Modules:
  0.0 20.3 jit_solution(11267380088586098865)
XLA Ops:
  0.6 1.1 %spread.1 = (f32[96,128]{1,0:T(8,128)S(1)}, f32[192,128]{1,0:T(8,128)S(1)}, f32[192,128]{1,0:T(8,128)S(1)}, f32[192,128]{1,0:T(8,128)S(1)}, f32[96,128]{1,0:T(8,128)S(1)}) custom-call(f32[8,4096]{1,0:T(8,128)} %refs_0_.2, f32[8,4096]{1,0:T(8,128)} %refs_1_.2, f32[8,4096]{1,0:T(8,128)} %refs_2_.2), custom_call_target="tpu_custom_call" | custom-call | tf_op jit(solution)/shard_map/spread/pallas_call | solution.py:230
  1.7 0.5 %collective-permute-start = (f32[192,128]{1,0:T(8,128)S(1)}, f32[192,128]{1,0:T(8,128)S(1)}, u32[]{:S(2)}, u32[]{:S(2)}) collective-permute-start(f32[192,128]{1,0:T(8,128)S(1)} %get-tuple-element.21), channel_id=1, source_target_pairs={{0,4},{4,0},{8,12},{12,8},{16,20},{20,16},{24,28},{28,24},{1,5},{5... | collective-permute-start | bytes 294920 | tf_op jit(solution)/shard_map/ppermute | solution.py:248
  2.3 3.6 %collective-permute-start.4 = (f32[192,128]{1,0:T(8,128)S(1)}, f32[192,128]{1,0:T(8,128)S(1)}, u32[]{:S(2)}, u32[]{:S(2)}) collective-permute-start(f32[192,128]{1,0:T(8,128)S(1)} %get-tuple-element.26), channel_id=1, source_target_pairs={{0,28},{4,24},{8,20},{12,16},{16,12},{20,8},{24,4},{28,0},{1,29},{... | collective-permute-start | bytes 294920 | tf_op jit(solution)/shard_map/ppermute | solution.py:248
  5.8 0.0 collective-permute-done.aside
  5.9 0.3 %collective-permute-start.1 = (f32[192,128]{1,0:T(8,128)S(1)}, f32[192,128]{1,0:T(8,128)S(1)}, u32[]{:S(2)}, u32[]{:S(2)}) collective-permute-start(f32[192,128]{1,0:T(8,128)S(1)} %get-tuple-element.22), channel_id=1, source_target_pairs={{0,12},{4,8},{8,4},{12,0},{16,28},{20,24},{24,20},{28,16},{1,13},{... | collective-permute-start | bytes 294920 | tf_op jit(solution)/shard_map/ppermute | solution.py:248
  6.1 1.2 %collective-permute-start.2 = (f32[192,128]{1,0:T(8,128)S(1)}, f32[192,128]{1,0:T(8,128)S(1)}, u32[]{:S(2)}, u32[]{:S(2)}) collective-permute-start(f32[192,128]{1,0:T(8,128)S(1)} %get-tuple-element.23.refs_4_), channel_id=1, source_target_pairs={{0,20},{4,16},{8,28},{12,24},{16,4},{20,0},{24,12},{28,8},{1,21},{... | collective-permute-start | bytes 294920 | tf_op jit(solution)/shard_map/ppermute | solution.py:248
  7.4 0.2 collective-permute-start.3
  7.5 1.5 %fetch.1 = (bf16[2,512,384]{2,1,0:T(8,128)(2,1)S(1)}, bf16[2,2,256,256]{3,2,1,0:T(8,128)(2,1)S(1)}, bf16[2,256,256]{2,1,0:T(8,128)(2,1)S(1)}, f32[256,256]{1,0:T(8,128)S(1)}) custom-call(bf16[2,512,384]{2,1,0:T(8,128)(2,1)} %constant.8.clone.refs_0_, bf16[2,2,256,256]{3,2,1,0:T(8,128)(2,1)} %constant.9.clone.refs_1_, ...), custom_call_target="tpu_custom_call" | custom-call | tf_op jit(solution)/shard_map/fetch/pallas_call | solution.py:230
  9.0 0.0 collective-permute-done.4.x.far
  9.0 0.4 %collective-permute-start.5 = (f32[96,128]{1,0:T(8,128)S(1)}, f32[96,128]{1,0:T(8,128)S(1)}, u32[]{:S(2)}, u32[]{:S(2)}) collective-permute-start(f32[96,128]{1,0:T(8,128)S(1)} %second_half.2), channel_id=1, source_target_pairs={{0,4},{4,0},{8,12},{12,8},{16,20},{20,16},{24,28},{28,24},{1,5},{5... | collective-permute-start | bytes 147464 | tf_op jit(solution)/shard_map/ppermute | solution.py:248
  9.4 0.0 collective-permute-done.3.other
  9.4 0.9 %collective-permute-done.5.handed = f32[96,128]{1,0:T(8,128)S(1)} collective-permute-done((f32[96,128]{1,0:T(8,128)S(1)}, f32[96,128]{1,0:T(8,128)S(1)}, u32[]{:S(2)}, u32[]{:S(2)}) %collective-permute-start.5) | collective-permute-done | bytes 49184 | tf_op jit(solution)/shard_map/ppermute | solution.py:248
  10.3 0.4 %early.1.refs_2_ = f32[512,384]{1,0:T(8,128)S(1)} custom-call(f32[96,128]{1,0:T(8,128)S(1)} %get-tuple-element.24.own, f32[96,128]{1,0:T(8,128)S(1)} %collective-permute-done.3.other, f32[192,128]{1,0:T(8,128)S(1)} %collective-permute-done.4.x.far, f32[96,128]{1,0:T(8,128)S(1)} %collective-permute-done.5.handed, ...), custom_call_target="tpu_custom_call" | custom-call | tf_op jit(solution)/shard_map/early/pallas_call | solution.py:230
  10.8 0.3 %collective-permute-done.1.refs_0_ = f32[192,128]{1,0:T(8,128)S(1)} collective-permute-done((f32[192,128]{1,0:T(8,128)S(1)}, f32[192,128]{1,0:T(8,128)S(1)}, u32[]{:S(2)}, u32[]{:S(2)}) %collective-permute-start.1) | collective-permute-done | bytes 98336 | tf_op jit(solution)/shard_map/ppermute | solution.py:248
  11.0 0.0 collective-permute-done.2.refs_1_
  11.0 1.3 %transform.1 = (f32[64,128]{1,0:T(8,128)S(1)}, f32[128,128]{1,0:T(8,128)S(1)}, f32[128,128]{1,0:T(8,128)S(1)}, f32[128,128]{1,0:T(8,128)S(1)}, f32[64,128]{1,0:T(8,128)S(1)}) custom-call(f32[192,128]{1,0:T(8,128)S(1)} %collective-permute-done.1.refs_0_, f32[192,128]{1,0:T(8,128)S(1)} %collective-permute-done.2.refs_1_, f32[512,384]{1,0:T(8,128)S(1)} %early.1.refs_2_, ...), custom_call_target="tpu_custom_call" | custom-call | tf_op jit(solution)/shard_map/transform/pallas_call | solution.py:230
  12.4 0.4 %collective-permute-start.9 = (f32[128,128]{1,0:T(8,128)S(1)}, f32[128,128]{1,0:T(8,128)S(1)}, u32[]{:S(2)}, u32[]{:S(2)}) collective-permute-start(f32[128,128]{1,0:T(8,128)S(1)} %get-tuple-element.35), channel_id=1, source_target_pairs={{0,4},{4,0},{8,12},{12,8},{16,20},{20,16},{24,28},{28,24},{1,5},{5... | collective-permute-start | bytes 196616 | tf_op jit(solution)/shard_map/ppermute | solution.py:248
  12.7 2.6 %collective-permute-start.7 = (f32[128,128]{1,0:T(8,128)S(1)}, f32[128,128]{1,0:T(8,128)S(1)}, u32[]{:S(2)}, u32[]{:S(2)}) collective-permute-start(f32[128,128]{1,0:T(8,128)S(1)} %get-tuple-element.33), channel_id=1, source_target_pairs={{0,28},{4,24},{8,20},{12,16},{16,12},{20,8},{24,4},{28,0},{1,29},{... | collective-permute-start | bytes 196616 | tf_op jit(solution)/shard_map/ppermute | solution.py:248
  15.4 0.0 collective-permute-done.9.aside
  15.4 0.2 collective-permute-start.10
  15.5 1.3 %collective-permute-start.11 = (f32[128,128]{1,0:T(8,128)S(1)}, f32[128,128]{1,0:T(8,128)S(1)}, u32[]{:S(2)}, u32[]{:S(2)}) collective-permute-start(f32[128,128]{1,0:T(8,128)S(1)} %get-tuple-element.37), channel_id=1, source_target_pairs={{0,20},{4,16},{8,28},{12,24},{16,4},{20,0},{24,12},{28,8},{1,21},{... | collective-permute-start | bytes 196616 | tf_op jit(solution)/shard_map/ppermute | solution.py:248
  16.9 0.2 collective-permute-start.6
  17.0 0.8 %collective-permute-done.7.x.refs_2_ = f32[128,128]{1,0:T(8,128)S(1)} collective-permute-done((f32[128,128]{1,0:T(8,128)S(1)}, f32[128,128]{1,0:T(8,128)S(1)}, u32[]{:S(2)}, u32[]{:S(2)}) %collective-permute-start.7) | collective-permute-done | bytes 65568 | tf_op jit(solution)/shard_map/ppermute | solution.py:248
  17.8 0.1 collective-permute-start.8
  17.9 0.2 %collective-permute-done.6.refs_1_ = f32[64,128]{1,0:T(8,128)S(1)} collective-permute-done((f32[64,128]{1,0:T(8,128)S(1)}, f32[64,128]{1,0:T(8,128)S(1)}, u32[]{:S(2)}, u32[]{:S(2)}) %collective-permute-start.6) | collective-permute-done | bytes 32800 | tf_op jit(solution)/shard_map/ppermute | solution.py:248
  18.1 0.9 %collective-permute-done.8.refs_3_ = f32[64,128]{1,0:T(8,128)S(1)} collective-permute-done((f32[64,128]{1,0:T(8,128)S(1)}, f32[64,128]{1,0:T(8,128)S(1)}, u32[]{:S(2)}, u32[]{:S(2)}) %collective-permute-start.8) | collective-permute-done | bytes 32800 | tf_op jit(solution)/shard_map/ppermute | solution.py:248
  19.0 0.5 %collective-permute-done.10.refs_4_ = f32[128,128]{1,0:T(8,128)S(1)} collective-permute-done((f32[128,128]{1,0:T(8,128)S(1)}, f32[128,128]{1,0:T(8,128)S(1)}, u32[]{:S(2)}, u32[]{:S(2)}) %collective-permute-start.10) | collective-permute-done | bytes 65568 | tf_op jit(solution)/shard_map/ppermute | solution.py:248
  19.5 0.0 collective-permute-done.11.refs_5_
  19.5 0.8 %gather.1 = (f32[8,4096]{1,0:T(8,128)}, f32[8,4096]{1,0:T(8,128)}) custom-call(f32[64,128]{1,0:T(8,128)S(1)} %get-tuple-element.31.refs_0_, f32[64,128]{1,0:T(8,128)S(1)} %collective-permute-done.6.refs_1_, f32[128,128]{1,0:T(8,128)S(1)} %collective-permute-done.7.x.refs_2_, f32[64,128]{1,0:T(8,128)S(1)} %collective-permute-done.8.refs_3_, ...), custom_call_target="tpu_custom_call" | custom-call | tf_op jit(solution)/shard_map/gather/pallas_call | solution.py:230
  (4 shorter events, 0.0 us)
Async XLA Ops:
  1.7 4.1 %collective-permute-start = (f32[192,128]{1,0:T(8,128)S(1)}, f32[192,128]{1,0:T(8,128)S(1)}, u32[]{:S(2)}, u32[]{:S(2)}) collective-permute-start(f32[192,128]{1,0:T(8,128)S(1)} %get-tuple-element.21), channel_id=1, source_target_pairs={{0,4},{4,0},{8,12},{12,8},{16,20},{20,16},{24,28},{28,24},{1,5},{5... | collective-permute-start | bytes 294920 | tf_op jit(solution)/shard_map/ppermute | solution.py:248
  2.3 6.7 %collective-permute-start.4 = (f32[192,128]{1,0:T(8,128)S(1)}, f32[192,128]{1,0:T(8,128)S(1)}, u32[]{:S(2)}, u32[]{:S(2)}) collective-permute-start(f32[192,128]{1,0:T(8,128)S(1)} %get-tuple-element.26), channel_id=1, source_target_pairs={{0,28},{4,24},{8,20},{12,16},{16,12},{20,8},{24,4},{28,0},{1,29},{... | collective-permute-start | bytes 294920 | tf_op jit(solution)/shard_map/ppermute | solution.py:248
  5.9 5.2 %collective-permute-start.1 = (f32[192,128]{1,0:T(8,128)S(1)}, f32[192,128]{1,0:T(8,128)S(1)}, u32[]{:S(2)}, u32[]{:S(2)}) collective-permute-start(f32[192,128]{1,0:T(8,128)S(1)} %get-tuple-element.22), channel_id=1, source_target_pairs={{0,12},{4,8},{8,4},{12,0},{16,28},{20,24},{24,20},{28,16},{1,13},{... | collective-permute-start | bytes 294920 | tf_op jit(solution)/shard_map/ppermute | solution.py:248
  6.1 4.9 %collective-permute-start.2 = (f32[192,128]{1,0:T(8,128)S(1)}, f32[192,128]{1,0:T(8,128)S(1)}, u32[]{:S(2)}, u32[]{:S(2)}) collective-permute-start(f32[192,128]{1,0:T(8,128)S(1)} %get-tuple-element.23.refs_4_), channel_id=1, source_target_pairs={{0,20},{4,16},{8,28},{12,24},{16,4},{20,0},{24,12},{28,8},{1,21},{... | collective-permute-start | bytes 294920 | tf_op jit(solution)/shard_map/ppermute | solution.py:248
  7.4 2.1 %collective-permute-start.3 = (f32[96,128]{1,0:T(8,128)S(1)}, f32[96,128]{1,0:T(8,128)S(1)}, u32[]{:S(2)}, u32[]{:S(2)}) collective-permute-start(f32[96,128]{1,0:T(8,128)S(1)} %get-tuple-element.25), channel_id=1, source_target_pairs={{0,4},{4,0},{8,12},{12,8},{16,20},{20,16},{24,28},{28,24},{1,5},{5... | collective-permute-start | bytes 147464 | tf_op jit(solution)/shard_map/ppermute | solution.py:248
  9.0 1.3 %collective-permute-start.5 = (f32[96,128]{1,0:T(8,128)S(1)}, f32[96,128]{1,0:T(8,128)S(1)}, u32[]{:S(2)}, u32[]{:S(2)}) collective-permute-start(f32[96,128]{1,0:T(8,128)S(1)} %second_half.2), channel_id=1, source_target_pairs={{0,4},{4,0},{8,12},{12,8},{16,20},{20,16},{24,28},{28,24},{1,5},{5... | collective-permute-start | bytes 147464 | tf_op jit(solution)/shard_map/ppermute | solution.py:248
  12.4 3.0 %collective-permute-start.9 = (f32[128,128]{1,0:T(8,128)S(1)}, f32[128,128]{1,0:T(8,128)S(1)}, u32[]{:S(2)}, u32[]{:S(2)}) collective-permute-start(f32[128,128]{1,0:T(8,128)S(1)} %get-tuple-element.35), channel_id=1, source_target_pairs={{0,4},{4,0},{8,12},{12,8},{16,20},{20,16},{24,28},{28,24},{1,5},{5... | collective-permute-start | bytes 196616 | tf_op jit(solution)/shard_map/ppermute | solution.py:248
  12.7 5.0 %collective-permute-start.7 = (f32[128,128]{1,0:T(8,128)S(1)}, f32[128,128]{1,0:T(8,128)S(1)}, u32[]{:S(2)}, u32[]{:S(2)}) collective-permute-start(f32[128,128]{1,0:T(8,128)S(1)} %get-tuple-element.33), channel_id=1, source_target_pairs={{0,28},{4,24},{8,20},{12,16},{16,12},{20,8},{24,4},{28,0},{1,29},{... | collective-permute-start | bytes 196616 | tf_op jit(solution)/shard_map/ppermute | solution.py:248
  15.4 4.1 %collective-permute-start.10 = (f32[128,128]{1,0:T(8,128)S(1)}, f32[128,128]{1,0:T(8,128)S(1)}, u32[]{:S(2)}, u32[]{:S(2)}) collective-permute-start(f32[128,128]{1,0:T(8,128)S(1)} %get-tuple-element.36), channel_id=1, source_target_pairs={{0,12},{4,8},{8,4},{12,0},{16,28},{20,24},{24,20},{28,16},{1,13},{... | collective-permute-start | bytes 196616 | tf_op jit(solution)/shard_map/ppermute | solution.py:248
  15.5 4.0 %collective-permute-start.11 = (f32[128,128]{1,0:T(8,128)S(1)}, f32[128,128]{1,0:T(8,128)S(1)}, u32[]{:S(2)}, u32[]{:S(2)}) collective-permute-start(f32[128,128]{1,0:T(8,128)S(1)} %get-tuple-element.37), channel_id=1, source_target_pairs={{0,20},{4,16},{8,28},{12,24},{16,4},{20,0},{24,12},{28,8},{1,21},{... | collective-permute-start | bytes 196616 | tf_op jit(solution)/shard_map/ppermute | solution.py:248
  16.9 1.2 %collective-permute-start.6 = (f32[64,128]{1,0:T(8,128)S(1)}, f32[64,128]{1,0:T(8,128)S(1)}, u32[]{:S(2)}, u32[]{:S(2)}) collective-permute-start(f32[64,128]{1,0:T(8,128)S(1)} %get-tuple-element.32), channel_id=1, source_target_pairs={{0,4},{4,0},{8,12},{12,8},{16,20},{20,16},{24,28},{28,24},{1,5},{5... | collective-permute-start | bytes 98312 | tf_op jit(solution)/shard_map/ppermute | solution.py:248
  17.8 1.2 %collective-permute-start.8 = (f32[64,128]{1,0:T(8,128)S(1)}, f32[64,128]{1,0:T(8,128)S(1)}, u32[]{:S(2)}, u32[]{:S(2)}) collective-permute-start(f32[64,128]{1,0:T(8,128)S(1)} %second_half.3), channel_id=1, source_target_pairs={{0,4},{4,0},{8,12},{12,8},{16,20},{20,16},{24,28},{28,24},{1,5},{5... | collective-permute-start | bytes 98312 | tf_op jit(solution)/shard_map/ppermute | solution.py:248

commit v12 on v9

--- a/solution.py
+++ b/solution.py
@@ -11,7 +11,7 @@
 
 LANES = 128
 BF = jnp.bfloat16
-PARTS, JOINED, LOADS = 4, 2, 4
+PARTS, JOINED, LOADS = 4, 2, 1
 PLANS = ((7, 7), (3, 3), (5, 5)), ((7, 7), (3, 3), (5, 5))
 
 

time: 20.4 us -> 20.4 us (level)
  no operation moved by 1% of the time
where the time goes in v12:
time: 20.4 us; the launch traced here: 20.2 us
  starting transfers between devices  10.9 us (53%)
  Pallas kernels  5.07 us (25%)
  waiting for transfers between devices  3.58 us (18%)
  between operations  0.69 us (3%)
    ppermute x12, starting transfers between devices, swap(): lax.ppermute(x, 'context', [(i, i ^ (odd if i % 2 else even)) for i in ra...  10.9 us
    pallas_call x9, Pallas kernels, call(): pl.pallas_call(body, out_shape=[kind(shape, dtype) for shape, dtype in ou...  5.07 us
    ppermute x12, waiting for transfers between devices, swap(): lax.ppermute(x, 'context', [(i, i ^ (odd if i % 2 else even)) for i in ra...  3.58 us
  transfers between devices with their start and end apart: 12, of which 6 were waited for; matrix products, arithmetic and copies ran while one was open for 0% of the time, Pallas kernels for 9%

profile of v12, /device:TPU:0, one launch (start us, length us, event | category | flops | bytes accessed | tf_op | source)
XLA Modules:
  0.0 20.2 jit_solution(13006818440201379185)
XLA Ops:
  0.6 1.1 %spread.1 = (f32[96,128]{1,0:T(8,128)S(1)}, f32[192,128]{1,0:T(8,128)S(1)}, f32[192,128]{1,0:T(8,128)S(1)}, f32[192,128]{1,0:T(8,128)S(1)}, f32[96,128]{1,0:T(8,128)S(1)}) custom-call(f32[8,4096]{1,0:T(8,128)} %refs_0_.2, f32[8,4096]{1,0:T(8,128)} %refs_1_.2, f32[8,4096]{1,0:T(8,128)} %refs_2_.2), custom_call_target="tpu_custom_call" | custom-call | tf_op jit(solution)/shard_map/spread/pallas_call | solution.py:229
  1.7 0.5 %collective-permute-start = (f32[192,128]{1,0:T(8,128)S(1)}, f32[192,128]{1,0:T(8,128)S(1)}, u32[]{:S(2)}, u32[]{:S(2)}) collective-permute-start(f32[192,128]{1,0:T(8,128)S(1)} %get-tuple-element.21), channel_id=1, source_target_pairs={{0,4},{4,0},{8,12},{12,8},{16,20},{20,16},{24,28},{28,24},{1,5},{5... | collective-permute-start | bytes 294920 | tf_op jit(solution)/shard_map/ppermute | solution.py:247
  2.3 3.6 %collective-permute-start.4 = (f32[192,128]{1,0:T(8,128)S(1)}, f32[192,128]{1,0:T(8,128)S(1)}, u32[]{:S(2)}, u32[]{:S(2)}) collective-permute-start(f32[192,128]{1,0:T(8,128)S(1)} %get-tuple-element.26), channel_id=1, source_target_pairs={{0,28},{4,24},{8,20},{12,16},{16,12},{20,8},{24,4},{28,0},{1,29},{... | collective-permute-start | bytes 294920 | tf_op jit(solution)/shard_map/ppermute | solution.py:247
  5.8 0.0 collective-permute-done.aside
  5.9 0.3 %collective-permute-start.1 = (f32[192,128]{1,0:T(8,128)S(1)}, f32[192,128]{1,0:T(8,128)S(1)}, u32[]{:S(2)}, u32[]{:S(2)}) collective-permute-start(f32[192,128]{1,0:T(8,128)S(1)} %get-tuple-element.22), channel_id=1, source_target_pairs={{0,12},{4,8},{8,4},{12,0},{16,28},{20,24},{24,20},{28,16},{1,13},{... | collective-permute-start | bytes 294920 | tf_op jit(solution)/shard_map/ppermute | solution.py:247
  6.1 1.2 %collective-permute-start.2 = (f32[192,128]{1,0:T(8,128)S(1)}, f32[192,128]{1,0:T(8,128)S(1)}, u32[]{:S(2)}, u32[]{:S(2)}) collective-permute-start(f32[192,128]{1,0:T(8,128)S(1)} %get-tuple-element.23.refs_4_), channel_id=1, source_target_pairs={{0,20},{4,16},{8,28},{12,24},{16,4},{20,0},{24,12},{28,8},{1,21},{... | collective-permute-start | bytes 294920 | tf_op jit(solution)/shard_map/ppermute | solution.py:247
  7.4 0.2 collective-permute-start.3
  7.5 1.5 %fetch.1 = (bf16[2,512,384]{2,1,0:T(8,128)(2,1)S(1)}, bf16[2,2,256,256]{3,2,1,0:T(8,128)(2,1)S(1)}, bf16[2,256,256]{2,1,0:T(8,128)(2,1)S(1)}, f32[256,256]{1,0:T(8,128)S(1)}) custom-call(bf16[8,2,512,384]{3,2,1,0:T(8,128)(2,1)} %constant.8.clone.refs_0_, bf16[2,2,256,256]{3,2,1,0:T(8,128)(2,1)} %constant.9.clone.refs_1_, ...), custom_call_target="tpu_custom_call" | custom-call | tf_op jit(solution)/shard_map/fetch/pallas_call | solution.py:229
  9.0 0.0 collective-permute-done.4.x.far
  9.0 0.4 %collective-permute-start.5 = (f32[96,128]{1,0:T(8,128)S(1)}, f32[96,128]{1,0:T(8,128)S(1)}, u32[]{:S(2)}, u32[]{:S(2)}) collective-permute-start(f32[96,128]{1,0:T(8,128)S(1)} %second_half.2), channel_id=1, source_target_pairs={{0,4},{4,0},{8,12},{12,8},{16,20},{20,16},{24,28},{28,24},{1,5},{5... | collective-permute-start | bytes 147464 | tf_op jit(solution)/shard_map/ppermute | solution.py:247
  9.4 0.0 collective-permute-done.3.other
  9.4 0.9 %collective-permute-done.5.handed = f32[96,128]{1,0:T(8,128)S(1)} collective-permute-done((f32[96,128]{1,0:T(8,128)S(1)}, f32[96,128]{1,0:T(8,128)S(1)}, u32[]{:S(2)}, u32[]{:S(2)}) %collective-permute-start.5) | collective-permute-done | bytes 49184 | tf_op jit(solution)/shard_map/ppermute | solution.py:247
  10.3 0.4 %early.1.refs_2_ = f32[512,384]{1,0:T(8,128)S(1)} custom-call(f32[96,128]{1,0:T(8,128)S(1)} %get-tuple-element.24.own, f32[96,128]{1,0:T(8,128)S(1)} %collective-permute-done.3.other, f32[192,128]{1,0:T(8,128)S(1)} %collective-permute-done.4.x.far, f32[96,128]{1,0:T(8,128)S(1)} %collective-permute-done.5.handed, ...), custom_call_target="tpu_custom_call" | custom-call | tf_op jit(solution)/shard_map/early/pallas_call | solution.py:229
  10.7 0.3 %collective-permute-done.1.refs_0_ = f32[192,128]{1,0:T(8,128)S(1)} collective-permute-done((f32[192,128]{1,0:T(8,128)S(1)}, f32[192,128]{1,0:T(8,128)S(1)}, u32[]{:S(2)}, u32[]{:S(2)}) %collective-permute-start.1) | collective-permute-done | bytes 98336 | tf_op jit(solution)/shard_map/ppermute | solution.py:247
  11.0 0.0 collective-permute-done.2.refs_1_
  11.0 1.3 %transform.1 = (f32[64,128]{1,0:T(8,128)S(1)}, f32[128,128]{1,0:T(8,128)S(1)}, f32[128,128]{1,0:T(8,128)S(1)}, f32[128,128]{1,0:T(8,128)S(1)}, f32[64,128]{1,0:T(8,128)S(1)}) custom-call(f32[192,128]{1,0:T(8,128)S(1)} %collective-permute-done.1.refs_0_, f32[192,128]{1,0:T(8,128)S(1)} %collective-permute-done.2.refs_1_, f32[512,384]{1,0:T(8,128)S(1)} %early.1.refs_2_, ...), custom_call_target="tpu_custom_call" | custom-call | tf_op jit(solution)/shard_map/transform/pallas_call | solution.py:229
  12.3 0.4 %collective-permute-start.9 = (f32[128,128]{1,0:T(8,128)S(1)}, f32[128,128]{1,0:T(8,128)S(1)}, u32[]{:S(2)}, u32[]{:S(2)}) collective-permute-start(f32[128,128]{1,0:T(8,128)S(1)} %get-tuple-element.35), channel_id=1, source_target_pairs={{0,4},{4,0},{8,12},{12,8},{16,20},{20,16},{24,28},{28,24},{1,5},{5... | collective-permute-start | bytes 196616 | tf_op jit(solution)/shard_map/ppermute | solution.py:247
  12.7 2.6 %collective-permute-start.7 = (f32[128,128]{1,0:T(8,128)S(1)}, f32[128,128]{1,0:T(8,128)S(1)}, u32[]{:S(2)}, u32[]{:S(2)}) collective-permute-start(f32[128,128]{1,0:T(8,128)S(1)} %get-tuple-element.33), channel_id=1, source_target_pairs={{0,28},{4,24},{8,20},{12,16},{16,12},{20,8},{24,4},{28,0},{1,29},{... | collective-permute-start | bytes 196616 | tf_op jit(solution)/shard_map/ppermute | solution.py:247
  15.3 0.0 collective-permute-done.9.aside
  15.3 0.1 collective-permute-start.10
  15.5 1.3 %collective-permute-start.11 = (f32[128,128]{1,0:T(8,128)S(1)}, f32[128,128]{1,0:T(8,128)S(1)}, u32[]{:S(2)}, u32[]{:S(2)}) collective-permute-start(f32[128,128]{1,0:T(8,128)S(1)} %get-tuple-element.37), channel_id=1, source_target_pairs={{0,20},{4,16},{8,28},{12,24},{16,4},{20,0},{24,12},{28,8},{1,21},{... | collective-permute-start | bytes 196616 | tf_op jit(solution)/shard_map/ppermute | solution.py:247
  16.8 0.2 collective-permute-start.6
  17.0 0.8 %collective-permute-done.7.x.refs_2_ = f32[128,128]{1,0:T(8,128)S(1)} collective-permute-done((f32[128,128]{1,0:T(8,128)S(1)}, f32[128,128]{1,0:T(8,128)S(1)}, u32[]{:S(2)}, u32[]{:S(2)}) %collective-permute-start.7) | collective-permute-done | bytes 65568 | tf_op jit(solution)/shard_map/ppermute | solution.py:247
  17.7 0.1 collective-permute-start.8
  17.8 0.2 %collective-permute-done.6.refs_1_ = f32[64,128]{1,0:T(8,128)S(1)} collective-permute-done((f32[64,128]{1,0:T(8,128)S(1)}, f32[64,128]{1,0:T(8,128)S(1)}, u32[]{:S(2)}, u32[]{:S(2)}) %collective-permute-start.6) | collective-permute-done | bytes 32800 | tf_op jit(solution)/shard_map/ppermute | solution.py:247
  18.0 0.9 %collective-permute-done.8.refs_3_ = f32[64,128]{1,0:T(8,128)S(1)} collective-permute-done((f32[64,128]{1,0:T(8,128)S(1)}, f32[64,128]{1,0:T(8,128)S(1)}, u32[]{:S(2)}, u32[]{:S(2)}) %collective-permute-start.8) | collective-permute-done | bytes 32800 | tf_op jit(solution)/shard_map/ppermute | solution.py:247
  19.0 0.5 %collective-permute-done.10.refs_4_ = f32[128,128]{1,0:T(8,128)S(1)} collective-permute-done((f32[128,128]{1,0:T(8,128)S(1)}, f32[128,128]{1,0:T(8,128)S(1)}, u32[]{:S(2)}, u32[]{:S(2)}) %collective-permute-start.10) | collective-permute-done | bytes 65568 | tf_op jit(solution)/shard_map/ppermute | solution.py:247
  19.5 0.0 collective-permute-done.11.refs_5_
  19.5 0.8 %gather.1 = (f32[8,4096]{1,0:T(8,128)}, f32[8,4096]{1,0:T(8,128)}) custom-call(f32[64,128]{1,0:T(8,128)S(1)} %get-tuple-element.31.refs_0_, f32[64,128]{1,0:T(8,128)S(1)} %collective-permute-done.6.refs_1_, f32[128,128]{1,0:T(8,128)S(1)} %collective-permute-done.7.x.refs_2_, f32[64,128]{1,0:T(8,128)S(1)} %collective-permute-done.8.refs_3_, ...), custom_call_target="tpu_custom_call" | custom-call | tf_op jit(solution)/shard_map/gather/pallas_call | solution.py:229
  (4 shorter events, 0.0 us)
Async XLA Ops:
  1.7 4.1 %collective-permute-start = (f32[192,128]{1,0:T(8,128)S(1)}, f32[192,128]{1,0:T(8,128)S(1)}, u32[]{:S(2)}, u32[]{:S(2)}) collective-permute-start(f32[192,128]{1,0:T(8,128)S(1)} %get-tuple-element.21), channel_id=1, source_target_pairs={{0,4},{4,0},{8,12},{12,8},{16,20},{20,16},{24,28},{28,24},{1,5},{5... | collective-permute-start | bytes 294920 | tf_op jit(solution)/shard_map/ppermute | solution.py:247
  2.3 6.7 %collective-permute-start.4 = (f32[192,128]{1,0:T(8,128)S(1)}, f32[192,128]{1,0:T(8,128)S(1)}, u32[]{:S(2)}, u32[]{:S(2)}) collective-permute-start(f32[192,128]{1,0:T(8,128)S(1)} %get-tuple-element.26), channel_id=1, source_target_pairs={{0,28},{4,24},{8,20},{12,16},{16,12},{20,8},{24,4},{28,0},{1,29},{... | collective-permute-start | bytes 294920 | tf_op jit(solution)/shard_map/ppermute | solution.py:247
  5.9 5.2 %collective-permute-start.1 = (f32[192,128]{1,0:T(8,128)S(1)}, f32[192,128]{1,0:T(8,128)S(1)}, u32[]{:S(2)}, u32[]{:S(2)}) collective-permute-start(f32[192,128]{1,0:T(8,128)S(1)} %get-tuple-element.22), channel_id=1, source_target_pairs={{0,12},{4,8},{8,4},{12,0},{16,28},{20,24},{24,20},{28,16},{1,13},{... | collective-permute-start | bytes 294920 | tf_op jit(solution)/shard_map/ppermute | solution.py:247
  6.1 4.9 %collective-permute-start.2 = (f32[192,128]{1,0:T(8,128)S(1)}, f32[192,128]{1,0:T(8,128)S(1)}, u32[]{:S(2)}, u32[]{:S(2)}) collective-permute-start(f32[192,128]{1,0:T(8,128)S(1)} %get-tuple-element.23.refs_4_), channel_id=1, source_target_pairs={{0,20},{4,16},{8,28},{12,24},{16,4},{20,0},{24,12},{28,8},{1,21},{... | collective-permute-start | bytes 294920 | tf_op jit(solution)/shard_map/ppermute | solution.py:247
  7.4 2.1 %collective-permute-start.3 = (f32[96,128]{1,0:T(8,128)S(1)}, f32[96,128]{1,0:T(8,128)S(1)}, u32[]{:S(2)}, u32[]{:S(2)}) collective-permute-start(f32[96,128]{1,0:T(8,128)S(1)} %get-tuple-element.25), channel_id=1, source_target_pairs={{0,4},{4,0},{8,12},{12,8},{16,20},{20,16},{24,28},{28,24},{1,5},{5... | collective-permute-start | bytes 147464 | tf_op jit(solution)/shard_map/ppermute | solution.py:247
  9.0 1.3 %collective-permute-start.5 = (f32[96,128]{1,0:T(8,128)S(1)}, f32[96,128]{1,0:T(8,128)S(1)}, u32[]{:S(2)}, u32[]{:S(2)}) collective-permute-start(f32[96,128]{1,0:T(8,128)S(1)} %second_half.2), channel_id=1, source_target_pairs={{0,4},{4,0},{8,12},{12,8},{16,20},{20,16},{24,28},{28,24},{1,5},{5... | collective-permute-start | bytes 147464 | tf_op jit(solution)/shard_map/ppermute | solution.py:247
  12.3 3.0 %collective-permute-start.9 = (f32[128,128]{1,0:T(8,128)S(1)}, f32[128,128]{1,0:T(8,128)S(1)}, u32[]{:S(2)}, u32[]{:S(2)}) collective-permute-start(f32[128,128]{1,0:T(8,128)S(1)} %get-tuple-element.35), channel_id=1, source_target_pairs={{0,4},{4,0},{8,12},{12,8},{16,20},{20,16},{24,28},{28,24},{1,5},{5... | collective-permute-start | bytes 196616 | tf_op jit(solution)/shard_map/ppermute | solution.py:247
  12.7 5.0 %collective-permute-start.7 = (f32[128,128]{1,0:T(8,128)S(1)}, f32[128,128]{1,0:T(8,128)S(1)}, u32[]{:S(2)}, u32[]{:S(2)}) collective-permute-start(f32[128,128]{1,0:T(8,128)S(1)} %get-tuple-element.33), channel_id=1, source_target_pairs={{0,28},{4,24},{8,20},{12,16},{16,12},{20,8},{24,4},{28,0},{1,29},{... | collective-permute-start | bytes 196616 | tf_op jit(solution)/shard_map/ppermute | solution.py:247
  15.3 4.1 %collective-permute-start.10 = (f32[128,128]{1,0:T(8,128)S(1)}, f32[128,128]{1,0:T(8,128)S(1)}, u32[]{:S(2)}, u32[]{:S(2)}) collective-permute-start(f32[128,128]{1,0:T(8,128)S(1)} %get-tuple-element.36), channel_id=1, source_target_pairs={{0,12},{4,8},{8,4},{12,0},{16,28},{20,24},{24,20},{28,16},{1,13},{... | collective-permute-start | bytes 196616 | tf_op jit(solution)/shard_map/ppermute | solution.py:247
  15.5 4.0 %collective-permute-start.11 = (f32[128,128]{1,0:T(8,128)S(1)}, f32[128,128]{1,0:T(8,128)S(1)}, u32[]{:S(2)}, u32[]{:S(2)}) collective-permute-start(f32[128,128]{1,0:T(8,128)S(1)} %get-tuple-element.37), channel_id=1, source_target_pairs={{0,20},{4,16},{8,28},{12,24},{16,4},{20,0},{24,12},{28,8},{1,21},{... | collective-permute-start | bytes 196616 | tf_op jit(solution)/shard_map/ppermute | solution.py:247
  16.8 1.2 %collective-permute-start.6 = (f32[64,128]{1,0:T(8,128)S(1)}, f32[64,128]{1,0:T(8,128)S(1)}, u32[]{:S(2)}, u32[]{:S(2)}) collective-permute-start(f32[64,128]{1,0:T(8,128)S(1)} %get-tuple-element.32), channel_id=1, source_target_pairs={{0,4},{4,0},{8,12},{12,8},{16,20},{20,16},{24,28},{28,24},{1,5},{5... | collective-permute-start | bytes 98312 | tf_op jit(solution)/shard_map/ppermute | solution.py:247
  17.7 1.2 %collective-permute-start.8 = (f32[64,128]{1,0:T(8,128)S(1)}, f32[64,128]{1,0:T(8,128)S(1)}, u32[]{:S(2)}, u32[]{:S(2)}) collective-permute-start(f32[64,128]{1,0:T(8,128)S(1)} %second_half.3), channel_id=1, source_target_pairs={{0,4},{4,0},{8,12},{12,8},{16,20},{20,16},{24,28},{28,24},{1,5},{5... | collective-permute-start | bytes 98312 | tf_op jit(solution)/shard_map/ppermute | solution.py:247

commit v13 on v12

--- a/solution.py
+++ b/solution.py
@@ -219,8 +219,8 @@
     channels, block = a.shape
     chunks = block // LANES
     for i, ref in enumerate((a, b)):
-        for j in range(0, chunks, 8):
-            ref[:, pl.ds(j * LANES, 8 * LANES)] = held[:, pl.ds(i * chunks + j, 8), :].reshape(channels, 8 * LANES)
+        for j in range(0, chunks, 16):
+            ref[:, pl.ds(j * LANES, 16 * LANES)] = held[:, pl.ds(i * chunks + j, 16), :].reshape(channels, 16 * LANES)
 
 
 def call(body, ins, outs, scratch=(), far_in=0, near_out=True):

time: 20.4 us -> 20.4 us (level)
  no operation moved by 1% of the time
where the time goes in v13:
time: 20.4 us; the launch traced here: 20.2 us
  starting transfers between devices  10.9 us (53%)
  Pallas kernels  5.07 us (25%)
  waiting for transfers between devices  3.58 us (18%)
  between operations  0.69 us (3%)
    ppermute x12, starting transfers between devices, swap(): lax.ppermute(x, 'context', [(i, i ^ (odd if i % 2 else even)) for i in ra...  10.9 us
    pallas_call x9, Pallas kernels, call(): pl.pallas_call(body, out_shape=[kind(shape, dtype) for shape, dtype in ou...  5.07 us
    ppermute x12, waiting for transfers between devices, swap(): lax.ppermute(x, 'context', [(i, i ^ (odd if i % 2 else even)) for i in ra...  3.58 us
  transfers between devices with their start and end apart: 12, of which 6 were waited for; matrix products, arithmetic and copies ran while one was open for 0% of the time, Pallas kernels for 9%

profile of v13, /device:TPU:0, one launch (start us, length us, event | category | flops | bytes accessed | tf_op | source)
XLA Modules:
  0.0 20.2 jit_solution(4306007184212911529)
XLA Ops:
  0.6 1.1 %spread.1 = (f32[96,128]{1,0:T(8,128)S(1)}, f32[192,128]{1,0:T(8,128)S(1)}, f32[192,128]{1,0:T(8,128)S(1)}, f32[192,128]{1,0:T(8,128)S(1)}, f32[96,128]{1,0:T(8,128)S(1)}) custom-call(f32[8,4096]{1,0:T(8,128)} %refs_0_.2, f32[8,4096]{1,0:T(8,128)} %refs_1_.2, f32[8,4096]{1,0:T(8,128)} %refs_2_.2), custom_call_target="tpu_custom_call" | custom-call | tf_op jit(solution)/shard_map/spread/pallas_call | solution.py:229
  1.7 0.5 %collective-permute-start = (f32[192,128]{1,0:T(8,128)S(1)}, f32[192,128]{1,0:T(8,128)S(1)}, u32[]{:S(2)}, u32[]{:S(2)}) collective-permute-start(f32[192,128]{1,0:T(8,128)S(1)} %get-tuple-element.21), channel_id=1, source_target_pairs={{0,4},{4,0},{8,12},{12,8},{16,20},{20,16},{24,28},{28,24},{1,5},{5... | collective-permute-start | bytes 294920 | tf_op jit(solution)/shard_map/ppermute | solution.py:247
  2.3 3.6 %collective-permute-start.4 = (f32[192,128]{1,0:T(8,128)S(1)}, f32[192,128]{1,0:T(8,128)S(1)}, u32[]{:S(2)}, u32[]{:S(2)}) collective-permute-start(f32[192,128]{1,0:T(8,128)S(1)} %get-tuple-element.26), channel_id=1, source_target_pairs={{0,28},{4,24},{8,20},{12,16},{16,12},{20,8},{24,4},{28,0},{1,29},{... | collective-permute-start | bytes 294920 | tf_op jit(solution)/shard_map/ppermute | solution.py:247
  5.8 0.0 collective-permute-done.aside
  5.9 0.3 %collective-permute-start.1 = (f32[192,128]{1,0:T(8,128)S(1)}, f32[192,128]{1,0:T(8,128)S(1)}, u32[]{:S(2)}, u32[]{:S(2)}) collective-permute-start(f32[192,128]{1,0:T(8,128)S(1)} %get-tuple-element.22), channel_id=1, source_target_pairs={{0,12},{4,8},{8,4},{12,0},{16,28},{20,24},{24,20},{28,16},{1,13},{... | collective-permute-start | bytes 294920 | tf_op jit(solution)/shard_map/ppermute | solution.py:247
  6.1 1.2 %collective-permute-start.2 = (f32[192,128]{1,0:T(8,128)S(1)}, f32[192,128]{1,0:T(8,128)S(1)}, u32[]{:S(2)}, u32[]{:S(2)}) collective-permute-start(f32[192,128]{1,0:T(8,128)S(1)} %get-tuple-element.23.refs_4_), channel_id=1, source_target_pairs={{0,20},{4,16},{8,28},{12,24},{16,4},{20,0},{24,12},{28,8},{1,21},{... | collective-permute-start | bytes 294920 | tf_op jit(solution)/shard_map/ppermute | solution.py:247
  7.4 0.2 collective-permute-start.3
  7.5 1.5 %fetch.1 = (bf16[2,512,384]{2,1,0:T(8,128)(2,1)S(1)}, bf16[2,2,256,256]{3,2,1,0:T(8,128)(2,1)S(1)}, bf16[2,256,256]{2,1,0:T(8,128)(2,1)S(1)}, f32[256,256]{1,0:T(8,128)S(1)}) custom-call(bf16[8,2,512,384]{3,2,1,0:T(8,128)(2,1)} %constant.8.clone.refs_0_, bf16[2,2,256,256]{3,2,1,0:T(8,128)(2,1)} %constant.9.clone.refs_1_, ...), custom_call_target="tpu_custom_call" | custom-call | tf_op jit(solution)/shard_map/fetch/pallas_call | solution.py:229
  9.0 0.0 collective-permute-done.4.x.far
  9.0 0.4 %collective-permute-start.5 = (f32[96,128]{1,0:T(8,128)S(1)}, f32[96,128]{1,0:T(8,128)S(1)}, u32[]{:S(2)}, u32[]{:S(2)}) collective-permute-start(f32[96,128]{1,0:T(8,128)S(1)} %second_half.2), channel_id=1, source_target_pairs={{0,4},{4,0},{8,12},{12,8},{16,20},{20,16},{24,28},{28,24},{1,5},{5... | collective-permute-start | bytes 147464 | tf_op jit(solution)/shard_map/ppermute | solution.py:247
  9.4 0.0 collective-permute-done.3.other
  9.4 0.9 %collective-permute-done.5.handed = f32[96,128]{1,0:T(8,128)S(1)} collective-permute-done((f32[96,128]{1,0:T(8,128)S(1)}, f32[96,128]{1,0:T(8,128)S(1)}, u32[]{:S(2)}, u32[]{:S(2)}) %collective-permute-start.5) | collective-permute-done | bytes 49184 | tf_op jit(solution)/shard_map/ppermute | solution.py:247
  10.3 0.4 %early.1.refs_2_ = f32[512,384]{1,0:T(8,128)S(1)} custom-call(f32[96,128]{1,0:T(8,128)S(1)} %get-tuple-element.24.own, f32[96,128]{1,0:T(8,128)S(1)} %collective-permute-done.3.other, f32[192,128]{1,0:T(8,128)S(1)} %collective-permute-done.4.x.far, f32[96,128]{1,0:T(8,128)S(1)} %collective-permute-done.5.handed, ...), custom_call_target="tpu_custom_call" | custom-call | tf_op jit(solution)/shard_map/early/pallas_call | solution.py:229
  10.7 0.3 %collective-permute-done.1.refs_0_ = f32[192,128]{1,0:T(8,128)S(1)} collective-permute-done((f32[192,128]{1,0:T(8,128)S(1)}, f32[192,128]{1,0:T(8,128)S(1)}, u32[]{:S(2)}, u32[]{:S(2)}) %collective-permute-start.1) | collective-permute-done | bytes 98336 | tf_op jit(solution)/shard_map/ppermute | solution.py:247
  11.0 0.0 collective-permute-done.2.refs_1_
  11.0 1.3 %transform.1 = (f32[64,128]{1,0:T(8,128)S(1)}, f32[128,128]{1,0:T(8,128)S(1)}, f32[128,128]{1,0:T(8,128)S(1)}, f32[128,128]{1,0:T(8,128)S(1)}, f32[64,128]{1,0:T(8,128)S(1)}) custom-call(f32[192,128]{1,0:T(8,128)S(1)} %collective-permute-done.1.refs_0_, f32[192,128]{1,0:T(8,128)S(1)} %collective-permute-done.2.refs_1_, f32[512,384]{1,0:T(8,128)S(1)} %early.1.refs_2_, ...), custom_call_target="tpu_custom_call" | custom-call | tf_op jit(solution)/shard_map/transform/pallas_call | solution.py:229
  12.3 0.4 %collective-permute-start.9 = (f32[128,128]{1,0:T(8,128)S(1)}, f32[128,128]{1,0:T(8,128)S(1)}, u32[]{:S(2)}, u32[]{:S(2)}) collective-permute-start(f32[128,128]{1,0:T(8,128)S(1)} %get-tuple-element.35), channel_id=1, source_target_pairs={{0,4},{4,0},{8,12},{12,8},{16,20},{20,16},{24,28},{28,24},{1,5},{5... | collective-permute-start | bytes 196616 | tf_op jit(solution)/shard_map/ppermute | solution.py:247
  12.7 2.6 %collective-permute-start.7 = (f32[128,128]{1,0:T(8,128)S(1)}, f32[128,128]{1,0:T(8,128)S(1)}, u32[]{:S(2)}, u32[]{:S(2)}) collective-permute-start(f32[128,128]{1,0:T(8,128)S(1)} %get-tuple-element.33), channel_id=1, source_target_pairs={{0,28},{4,24},{8,20},{12,16},{16,12},{20,8},{24,4},{28,0},{1,29},{... | collective-permute-start | bytes 196616 | tf_op jit(solution)/shard_map/ppermute | solution.py:247
  15.3 0.0 collective-permute-done.9.aside
  15.3 0.1 collective-permute-start.10
  15.5 1.3 %collective-permute-start.11 = (f32[128,128]{1,0:T(8,128)S(1)}, f32[128,128]{1,0:T(8,128)S(1)}, u32[]{:S(2)}, u32[]{:S(2)}) collective-permute-start(f32[128,128]{1,0:T(8,128)S(1)} %get-tuple-element.37), channel_id=1, source_target_pairs={{0,20},{4,16},{8,28},{12,24},{16,4},{20,0},{24,12},{28,8},{1,21},{... | collective-permute-start | bytes 196616 | tf_op jit(solution)/shard_map/ppermute | solution.py:247
  16.8 0.2 collective-permute-start.6
  17.0 0.8 %collective-permute-done.7.x.refs_2_ = f32[128,128]{1,0:T(8,128)S(1)} collective-permute-done((f32[128,128]{1,0:T(8,128)S(1)}, f32[128,128]{1,0:T(8,128)S(1)}, u32[]{:S(2)}, u32[]{:S(2)}) %collective-permute-start.7) | collective-permute-done | bytes 65568 | tf_op jit(solution)/shard_map/ppermute | solution.py:247
  17.7 0.1 collective-permute-start.8
  17.8 0.2 %collective-permute-done.6.refs_1_ = f32[64,128]{1,0:T(8,128)S(1)} collective-permute-done((f32[64,128]{1,0:T(8,128)S(1)}, f32[64,128]{1,0:T(8,128)S(1)}, u32[]{:S(2)}, u32[]{:S(2)}) %collective-permute-start.6) | collective-permute-done | bytes 32800 | tf_op jit(solution)/shard_map/ppermute | solution.py:247
  18.0 0.9 %collective-permute-done.8.refs_3_ = f32[64,128]{1,0:T(8,128)S(1)} collective-permute-done((f32[64,128]{1,0:T(8,128)S(1)}, f32[64,128]{1,0:T(8,128)S(1)}, u32[]{:S(2)}, u32[]{:S(2)}) %collective-permute-start.8) | collective-permute-done | bytes 32800 | tf_op jit(solution)/shard_map/ppermute | solution.py:247
  19.0 0.5 %collective-permute-done.10.refs_4_ = f32[128,128]{1,0:T(8,128)S(1)} collective-permute-done((f32[128,128]{1,0:T(8,128)S(1)}, f32[128,128]{1,0:T(8,128)S(1)}, u32[]{:S(2)}, u32[]{:S(2)}) %collective-permute-start.10) | collective-permute-done | bytes 65568 | tf_op jit(solution)/shard_map/ppermute | solution.py:247
  19.5 0.0 collective-permute-done.11.refs_5_
  19.5 0.8 %gather.1 = (f32[8,4096]{1,0:T(8,128)}, f32[8,4096]{1,0:T(8,128)}) custom-call(f32[64,128]{1,0:T(8,128)S(1)} %get-tuple-element.31.refs_0_, f32[64,128]{1,0:T(8,128)S(1)} %collective-permute-done.6.refs_1_, f32[128,128]{1,0:T(8,128)S(1)} %collective-permute-done.7.x.refs_2_, f32[64,128]{1,0:T(8,128)S(1)} %collective-permute-done.8.refs_3_, ...), custom_call_target="tpu_custom_call" | custom-call | tf_op jit(solution)/shard_map/gather/pallas_call | solution.py:229
  (4 shorter events, 0.0 us)
Async XLA Ops:
  1.7 4.1 %collective-permute-start = (f32[192,128]{1,0:T(8,128)S(1)}, f32[192,128]{1,0:T(8,128)S(1)}, u32[]{:S(2)}, u32[]{:S(2)}) collective-permute-start(f32[192,128]{1,0:T(8,128)S(1)} %get-tuple-element.21), channel_id=1, source_target_pairs={{0,4},{4,0},{8,12},{12,8},{16,20},{20,16},{24,28},{28,24},{1,5},{5... | collective-permute-start | bytes 294920 | tf_op jit(solution)/shard_map/ppermute | solution.py:247
  2.3 6.7 %collective-permute-start.4 = (f32[192,128]{1,0:T(8,128)S(1)}, f32[192,128]{1,0:T(8,128)S(1)}, u32[]{:S(2)}, u32[]{:S(2)}) collective-permute-start(f32[192,128]{1,0:T(8,128)S(1)} %get-tuple-element.26), channel_id=1, source_target_pairs={{0,28},{4,24},{8,20},{12,16},{16,12},{20,8},{24,4},{28,0},{1,29},{... | collective-permute-start | bytes 294920 | tf_op jit(solution)/shard_map/ppermute | solution.py:247
  5.9 5.2 %collective-permute-start.1 = (f32[192,128]{1,0:T(8,128)S(1)}, f32[192,128]{1,0:T(8,128)S(1)}, u32[]{:S(2)}, u32[]{:S(2)}) collective-permute-start(f32[192,128]{1,0:T(8,128)S(1)} %get-tuple-element.22), channel_id=1, source_target_pairs={{0,12},{4,8},{8,4},{12,0},{16,28},{20,24},{24,20},{28,16},{1,13},{... | collective-permute-start | bytes 294920 | tf_op jit(solution)/shard_map/ppermute | solution.py:247
  6.1 4.9 %collective-permute-start.2 = (f32[192,128]{1,0:T(8,128)S(1)}, f32[192,128]{1,0:T(8,128)S(1)}, u32[]{:S(2)}, u32[]{:S(2)}) collective-permute-start(f32[192,128]{1,0:T(8,128)S(1)} %get-tuple-element.23.refs_4_), channel_id=1, source_target_pairs={{0,20},{4,16},{8,28},{12,24},{16,4},{20,0},{24,12},{28,8},{1,21},{... | collective-permute-start | bytes 294920 | tf_op jit(solution)/shard_map/ppermute | solution.py:247
  7.4 2.1 %collective-permute-start.3 = (f32[96,128]{1,0:T(8,128)S(1)}, f32[96,128]{1,0:T(8,128)S(1)}, u32[]{:S(2)}, u32[]{:S(2)}) collective-permute-start(f32[96,128]{1,0:T(8,128)S(1)} %get-tuple-element.25), channel_id=1, source_target_pairs={{0,4},{4,0},{8,12},{12,8},{16,20},{20,16},{24,28},{28,24},{1,5},{5... | collective-permute-start | bytes 147464 | tf_op jit(solution)/shard_map/ppermute | solution.py:247
  9.0 1.3 %collective-permute-start.5 = (f32[96,128]{1,0:T(8,128)S(1)}, f32[96,128]{1,0:T(8,128)S(1)}, u32[]{:S(2)}, u32[]{:S(2)}) collective-permute-start(f32[96,128]{1,0:T(8,128)S(1)} %second_half.2), channel_id=1, source_target_pairs={{0,4},{4,0},{8,12},{12,8},{16,20},{20,16},{24,28},{28,24},{1,5},{5... | collective-permute-start | bytes 147464 | tf_op jit(solution)/shard_map/ppermute | solution.py:247
  12.3 3.0 %collective-permute-start.9 = (f32[128,128]{1,0:T(8,128)S(1)}, f32[128,128]{1,0:T(8,128)S(1)}, u32[]{:S(2)}, u32[]{:S(2)}) collective-permute-start(f32[128,128]{1,0:T(8,128)S(1)} %get-tuple-element.35), channel_id=1, source_target_pairs={{0,4},{4,0},{8,12},{12,8},{16,20},{20,16},{24,28},{28,24},{1,5},{5... | collective-permute-start | bytes 196616 | tf_op jit(solution)/shard_map/ppermute | solution.py:247
  12.7 5.0 %collective-permute-start.7 = (f32[128,128]{1,0:T(8,128)S(1)}, f32[128,128]{1,0:T(8,128)S(1)}, u32[]{:S(2)}, u32[]{:S(2)}) collective-permute-start(f32[128,128]{1,0:T(8,128)S(1)} %get-tuple-element.33), channel_id=1, source_target_pairs={{0,28},{4,24},{8,20},{12,16},{16,12},{20,8},{24,4},{28,0},{1,29},{... | collective-permute-start | bytes 196616 | tf_op jit(solution)/shard_map/ppermute | solution.py:247
  15.3 4.1 %collective-permute-start.10 = (f32[128,128]{1,0:T(8,128)S(1)}, f32[128,128]{1,0:T(8,128)S(1)}, u32[]{:S(2)}, u32[]{:S(2)}) collective-permute-start(f32[128,128]{1,0:T(8,128)S(1)} %get-tuple-element.36), channel_id=1, source_target_pairs={{0,12},{4,8},{8,4},{12,0},{16,28},{20,24},{24,20},{28,16},{1,13},{... | collective-permute-start | bytes 196616 | tf_op jit(solution)/shard_map/ppermute | solution.py:247
  15.5 4.0 %collective-permute-start.11 = (f32[128,128]{1,0:T(8,128)S(1)}, f32[128,128]{1,0:T(8,128)S(1)}, u32[]{:S(2)}, u32[]{:S(2)}) collective-permute-start(f32[128,128]{1,0:T(8,128)S(1)} %get-tuple-element.37), channel_id=1, source_target_pairs={{0,20},{4,16},{8,28},{12,24},{16,4},{20,0},{24,12},{28,8},{1,21},{... | collective-permute-start | bytes 196616 | tf_op jit(solution)/shard_map/ppermute | solution.py:247
  16.8 1.2 %collective-permute-start.6 = (f32[64,128]{1,0:T(8,128)S(1)}, f32[64,128]{1,0:T(8,128)S(1)}, u32[]{:S(2)}, u32[]{:S(2)}) collective-permute-start(f32[64,128]{1,0:T(8,128)S(1)} %get-tuple-element.32), channel_id=1, source_target_pairs={{0,4},{4,0},{8,12},{12,8},{16,20},{20,16},{24,28},{28,24},{1,5},{5... | collective-permute-start | bytes 98312 | tf_op jit(solution)/shard_map/ppermute | solution.py:247
  17.7 1.2 %collective-permute-start.8 = (f32[64,128]{1,0:T(8,128)S(1)}, f32[64,128]{1,0:T(8,128)S(1)}, u32[]{:S(2)}, u32[]{:S(2)}) collective-permute-start(f32[64,128]{1,0:T(8,128)S(1)} %second_half.3), channel_id=1, source_target_pairs={{0,4},{4,0},{8,12},{12,8},{16,20},{20,16},{24,28},{28,24},{1,5},{5... | collective-permute-start | bytes 98312 | tf_op jit(solution)/shard_map/ppermute | solution.py:247
